TPU v7x, 32 devices: a whole 2x2x4 slice. The times are simulated.
32 devices in a mesh: view: 8 (over z, y), feat: 4 (over x, core).
Axes of the slice: x: 2, y: 2, z: 4, core: 2. Of those that a mesh axis runs over, the one named last changes fastest.
Arguments:
- points: bfloat16 [512, 768, 128], P('view', 'feat'), may hold values from -6 to 6
- head_weight: bfloat16 [768, 768], P('feat'), may hold values from -0.21875 to 0.21875
- teacher: bfloat16 [768, 16, 1369], P('feat', 'view'), may hold values from -6 to 6
- splat_weight: bfloat16 [16, 64, 74, 128], P('view'), may hold values from 0 to 0.19921875
- block_owner: int32 [16, 16, 4], P('view'), may hold values from 0 to 7, all different within a row; in each aligned block of 32 rows (0 to 31, 32 to 63, ..., all dimensions but the last counted through in order) at most 24 rows name the same one
- block_local: int32 [16, 64], P('view'), may hold values from 0 to 63
- block_row: int32 [16, 64], P('view'), may hold values from 0 to 35, as said below
Outputs:
- grad_points: bfloat16 [512, 768, 128], P('view', 'feat')
- head_grad: float32 [768, 768], P('feat')
Inputs may be any that keep to these rules, and one draw needn't show every extreme that they name: `block_owner`: over the 128 list entries of the views of one index of view, no owner appears more than 24 times, and some owner appears exactly 24 times. `block_row`: each view's list holds every value from 0 to 35 at least once.
All inputs are finite; a program needn't handle non-finite values.
Results may differ from a plain program's by a relative error of at most 0.0064.
Values may be sent and summed in bfloat16 or wider, within the bound.
No kernel may reach another device: no remote copies, remote signals or barrier semaphores. Data moves between devices by JAX's collectives and lax.ppermute only.
A program may use at most 128 MiB of HBM per device.

v0:
```python
import jax
import jax.numpy as jnp
from jax import lax
from jax.experimental import pallas as pl
from jax.experimental.pallas import tpu as pltpu
from jax.sharding import PartitionSpec as P

GRID = 37
BAND = 2
BLOCK = 128
GROUP = 4
VMEM_BYTES = 48 * 1024 * 1024


def slot_plan(owners, peer_count, capacity):
    total_requests = owners.shape[0]
    positions = jnp.arange(total_requests, dtype=jnp.int32)
    earlier = (owners[:, None] == owners[None, :]) & (positions[None, :] < positions[:, None])
    slot_rank = jnp.sum(earlier.astype(jnp.int32), axis=1)
    target = owners * capacity + slot_rank
    slot_ids = jnp.arange(peer_count * capacity, dtype=jnp.int32)
    matches = target[None, :] == slot_ids[:, None]
    source = jnp.sum(jnp.where(matches, positions[None, :], 0), axis=1)
    filled = jnp.any(matches, axis=1)
    return (target, source, filled)


def per_device_listed(points, head_weight, teacher, splat_weight, block_owner, block_local, block_row):
    peer_count = lax.axis_size("view")
    local_width = points.shape[1]
    view_count = splat_weight.shape[0]
    visible = splat_weight.shape[1]
    requests = view_count * visible
    capacity = max(3, (3 * requests + 2 * peer_count - 1) // (2 * peer_count))
    owners = block_owner.reshape(requests)
    local_ids = block_local.reshape(requests)
    target, source, filled = slot_plan(owners, peer_count, capacity)
    wanted = jnp.where(filled, jnp.take(local_ids, source), 0)
    columns = jnp.arange(GRID, dtype=jnp.int32)
    row_masks = [
        (block_row[:, :, None] + offset == columns[None, None, :]).astype(jnp.bfloat16)
        for offset in range(BAND)
    ]
    empty_bf = jnp.zeros((), jnp.bfloat16)
    asked_ids = lax.all_to_all(wanted, "view", split_axis=0, concat_axis=0, tiled=True)
    sent_rows = jnp.take(points, asked_ids, axis=0)
    arrived = lax.all_to_all(sent_rows, "view", split_axis=0, concat_axis=0, tiled=True)
    fetched = jnp.take(arrived, target, axis=0).reshape(view_count, visible, local_width, BLOCK)
    contrib = jnp.einsum(
        "vjcp,vjdp->vjcd", splat_weight, fetched, preferred_element_type=jnp.float32
    ).astype(jnp.bfloat16)
    rendered = jnp.zeros((view_count, GRID, GRID, local_width), jnp.float32)
    for offset in range(BAND):
        band_part = contrib[:, :, offset * GRID : (offset + 1) * GRID, :]
        rendered = rendered + jnp.einsum(
            "vjr,vjcd->vrcd", row_masks[offset], band_part, preferred_element_type=jnp.float32
        )
    rendered_rows = rendered.astype(jnp.bfloat16).reshape(view_count * GRID * GRID, local_width)
    pixel_rows = rendered_rows.shape[0]
    teacher_width = head_weight.shape[1]
    local_teacher = teacher.shape[0]
    contract_first = (((0,), (1,)), ((), ()))
    head_full = lax.all_gather(head_weight, "feat", axis=0, tiled=True)
    head_cols = lax.dynamic_slice_in_dim(
        head_full, lax.axis_index("feat") * local_teacher, local_teacher, 1
    )
    head_part = head_cols
    projected = lax.dot_general(
        head_part,
        lax.all_gather(rendered_rows, "feat", axis=1, tiled=True),
        contract_first,
        preferred_element_type=jnp.float32,
    )
    square_sum = lax.psum(jnp.sum(projected * projected, axis=0), "feat")
    scale_rows = jnp.sqrt(square_sum / teacher_width + 1e-06)
    normed = projected / scale_rows[None, :]
    target_feat = teacher.reshape(local_teacher, pixel_rows).astype(jnp.float32)
    residual = normed - target_feat
    row_dot = lax.psum(jnp.sum(residual * normed, axis=0), "feat")
    grad_proj = (
        (residual - normed * (row_dot / teacher_width)[None, :]) / scale_rows[None, :]
    ).astype(jnp.bfloat16)
    shard_part = lax.all_gather(grad_proj, "feat", axis=0, tiled=True)
    head_part = head_weight
    grad_image = lax.dot_general(
        shard_part, head_part, contract_first, preferred_element_type=jnp.float32
    )
    column_part = lax.dot_general(
        rendered_rows, shard_part, contract_first, preferred_element_type=jnp.float32
    )
    grad_head = column_part
    grad_image, grad_head = (grad_image, grad_head)
    head_grad = lax.psum(grad_head, "view") / (view_count * peer_count * GRID)
    grad_image = grad_image.astype(jnp.bfloat16).reshape(view_count, GRID, GRID, local_width)
    pieces = [
        jnp.einsum("vjr,vrcd->vjcd", row_mask, grad_image, preferred_element_type=jnp.float32)
        for row_mask in row_masks
    ]
    grad_contrib = jnp.concatenate(pieces, axis=2).astype(jnp.bfloat16)
    grad_block = jnp.einsum(
        "vjcp,vjcd->vjdp", splat_weight, grad_contrib, preferred_element_type=jnp.float32
    ).astype(jnp.bfloat16)
    grad_block = grad_block.reshape(requests, local_width, BLOCK)
    packed = jnp.where(filled[:, None, None], jnp.take(grad_block, source, axis=0), empty_bf)
    landed = lax.all_to_all(packed, "view", split_axis=0, concat_axis=0, tiled=True)
    summed = jax.ops.segment_sum(
        landed.astype(jnp.float32), asked_ids, num_segments=points.shape[0]
    )
    grad_points = summed.astype(jnp.bfloat16)
    return (grad_points, head_grad)


def price(us):
    return pl.CostEstimate(flops=int(us * 1e9), bytes_accessed=int(us * 2e6), transcendentals=0)


def call(body, out_shape, args, n_scalars, us, name, scratch=(), aliases=None):
    smem = pl.BlockSpec(memory_space=pltpu.SMEM)
    vmem = pl.BlockSpec(memory_space=pltpu.VMEM)
    many = isinstance(out_shape, list)
    return pl.pallas_call(
        body,
        out_shape=out_shape,
        in_specs=[smem] * n_scalars + [vmem] * (len(args) - n_scalars),
        out_specs=[vmem] * len(out_shape) if many else vmem,
        scratch_shapes=list(scratch),
        compiler_params=pltpu.CompilerParams(vmem_limit_bytes=VMEM_BYTES),
        cost_estimate=price(us),
        name=name,
    )(*args)


def pack_weights(source, listed, peers, aligned):
    quarter = source.shape[0] // peers
    band_rows = listed.shape[1]
    tail = aligned - 16

    def body(source_ref, listed_ref, *outs):
        for k in range(peers):
            for i in range(quarter):
                outs[k][i, tail:aligned, :] = jnp.zeros((16, BLOCK), jnp.bfloat16)
                outs[k][i, 0:band_rows, :] = listed_ref[source_ref[k * quarter + i]]

    out = jax.ShapeDtypeStruct((quarter, aligned, BLOCK), jnp.bfloat16)
    return call(body, [out] * peers, (source, listed), 1, 3, "pack_weights")


def shifted(rows, start):
    rows = rows.astype(jnp.float32)
    rows = jnp.concatenate([rows, jnp.zeros((8, rows.shape[1]), jnp.float32)], axis=0)
    return pltpu.roll(rows, lax.rem(start, 8), 0)


def rows_at(start, band_rows):
    return pl.ds(pl.multiple_of((start // 8) * 8, 8), band_rows + 8)


def beside(first, second):
    lane = lax.broadcasted_iota(jnp.int32, (first.shape[0], 128), 1)
    second = pltpu.roll(second, 64, 1)
    middle = jnp.where(lane < 64, first[:, 128:256], second[:, 0:128])
    return jnp.concatenate([first[:, 0:128], middle, second[:, 128:256]], axis=1)


def apart(packed):
    return packed[:, 0:256], pltpu.roll(packed[:, 128:384], 192, 1)


def rounds(count, group):
    return (count + group - 1) // group


def spread(count, block, where, weight, points):
    slots, band_rows = weight.shape[:2]
    width = points.shape[1]

    def body(count_ref, block_ref, where_ref, weight_ref, points_ref, out_ref):
        blank = jnp.zeros((width, BLOCK), jnp.bfloat16)

        def group(step, carry):
            for t in range(2):
                pair = 2 * step + t
                one, two = 2 * pair, 2 * pair + 1
                weights = jnp.concatenate(
                    [weight_ref[where_ref[one]], weight_ref[where_ref[two]]], axis=1
                )
                blocks = jnp.concatenate(
                    [
                        jnp.concatenate([points_ref[block_ref[one]], blank], axis=1),
                        jnp.concatenate([blank, points_ref[block_ref[two]]], axis=1),
                    ],
                    axis=0,
                )
                out_ref[pair] = lax.dot_general(
                    weights, blocks, (((1,), (1,)), ((), ())), preferred_element_type=jnp.float32
                ).astype(jnp.bfloat16)
            return carry

        lax.fori_loop(0, rounds(count_ref[0], 4), group, 0)

    out = jax.ShapeDtypeStruct((slots // 2, band_rows, 2 * width), jnp.bfloat16)
    return call(body, out, (count, block, where, weight, points), 3, 3, "spread_blocks")


def render(count, block, place, where, other_count, other_place, weight, points, other, views, half_rows):
    width = points.shape[1]
    band_rows = weight.shape[1]

    def body(
        count_ref, block_ref, place_ref, where_ref, other_count_ref, other_place_ref,
        weight_ref, points_ref, other_ref, *rest
    ):
        outs, acc = rest[:-1], rest[-1]
        acc[...] = jnp.zeros_like(acc)

        def group(step, carry):
            parts = []
            for t in range(GROUP):
                slot = step * GROUP + t
                parts.append(
                    lax.dot_general(
                        shifted(weight_ref[where_ref[slot]], place_ref[slot]).astype(jnp.bfloat16),
                        points_ref[block_ref[slot]],
                        (((1,), (1,)), ((), ())),
                        preferred_element_type=jnp.float32,
                    )
                )
            for t in range(GROUP):
                acc[rows_at(place_ref[step * GROUP + t], band_rows), 0:width] += parts[t]
            return carry

        def other_group(step, carry):
            for t in range(2):
                pair = 2 * step + t
                for value, slot in zip(apart(other_ref[pair].astype(jnp.float32)), (2 * pair, 2 * pair + 1)):
                    start = other_place_ref[slot]
                    acc[rows_at(start, band_rows), :] += shifted(value, start)
            return carry

        lax.fori_loop(0, rounds(count_ref[0], GROUP), group, 0)
        lax.fori_loop(0, rounds(other_count_ref[0], 4), other_group, 0)
        for u, out in enumerate(outs):
            first = acc[2 * u * half_rows : (2 * u + 1) * half_rows, :]
            second = acc[(2 * u + 1) * half_rows : (2 * u + 2) * half_rows, :]
            out[...] = beside(first, second).astype(out.dtype)

    image = jax.ShapeDtypeStruct((half_rows, 2 * width), jnp.bfloat16)
    args = (count, block, place, where, other_count, other_place, weight, points, other)
    scratch = [pltpu.VMEM((2 * views * half_rows + band_rows + 8, 256), jnp.float32)]
    return call(body, [image] * views, args, 6, 5, "render_blocks", scratch)


def unpack_images(image_refs, image, half_rows):
    for u, ref in enumerate(image_refs):
        first, second = apart(ref[...].astype(jnp.float32))
        image[2 * u * half_rows : (2 * u + 1) * half_rows, :] = first
        image[(2 * u + 1) * half_rows : (2 * u + 2) * half_rows, :] = second


def pick(count, place, images, slots, band_rows):
    half_rows, packed = images[0].shape
    views = len(images)

    def body(count_ref, place_ref, *rest):
        image_refs, (out_ref, image) = rest[:views], rest[views:]
        unpack_images(image_refs, image, half_rows)
        image[2 * views * half_rows :, :] = jnp.zeros((band_rows + 8, 256), jnp.float32)

        def group(step, carry):
            for t in range(2):
                pair = 2 * step + t
                bands = []
                for slot in (2 * pair, 2 * pair + 1):
                    start = place_ref[slot]
                    rows = image[rows_at(start, band_rows), :]
                    back = lax.rem(band_rows + 8 - lax.rem(start, 8), band_rows + 8)
                    bands.append(pltpu.roll(rows, back, 0)[0:band_rows])
                out_ref[pair] = beside(*bands).astype(out_ref.dtype)
            return carry

        lax.fori_loop(0, rounds(count_ref[0], 4), group, 0)

    out = jax.ShapeDtypeStruct((slots // 2, band_rows, packed), jnp.bfloat16)
    scratch = [pltpu.VMEM((2 * views * half_rows + band_rows + 8, 256), jnp.float32)]
    return call(body, out, (count, place) + tuple(images), 2, 4, "pick_bands", scratch)


def pull(parts, where, old, blocks, last):
    views = len(parts[0]["images"])
    half_rows, packed = parts[0]["images"][0].shape
    width = packed // 2
    band_rows = parts[0]["weights"].shape[2]
    first = old is None
    scalars = ("count", "block", "place", "other_count", "other_block")
    tables, arrays = [where], []
    for part in parts:
        tables += [part[name] for name in scalars]
        arrays += [part["weights"], part["bands"]] + list(part["images"])
    arrays += [] if first else [old]

    def body(*refs):
        where_ref, table_refs = refs[0], refs[1 : len(tables)]
        array_refs = refs[len(tables) : len(tables) + len(arrays)]
        out_ref, image, acc = refs[len(tables) + len(arrays) :]
        if first:
            acc[...] = jnp.zeros_like(acc)
        else:
            acc[0:blocks] = array_refs[-1][...]

        for i in range(len(parts)):
            count_ref, block_ref, place_ref, other_count_ref, other_block_ref = table_refs[5 * i : 5 * i + 5]
            weight_ref, other_ref, *image_refs = array_refs[(2 + views) * i : (2 + views) * (i + 1)]
            unpack_images(image_refs, image, half_rows)

            def group(step, carry):
                terms = []
                for t in range(GROUP):
                    slot = step * GROUP + t
                    start = place_ref[slot]
                    terms.append(
                        lax.dot_general(
                            image[rows_at(start, band_rows), 0:width].astype(jnp.bfloat16),
                            shifted(weight_ref[0, where_ref[slot]], start).astype(jnp.bfloat16),
                            (((0,), (0,)), ((), ())),
                            preferred_element_type=jnp.float32,
                        )
                    )
                for t in range(GROUP):
                    acc[block_ref[step * GROUP + t]] += terms[t]
                return carry

            def other_group(step, carry):
                terms = []
                for t in range(2):
                    pair = 2 * step + t
                    both = [weight_ref[1, where_ref[2 * pair + s]] for s in range(2)]
                    terms.append(
                        lax.dot_general(
                            other_ref[pair],
                            jnp.concatenate(both, axis=1),
                            (((0,), (0,)), ((), ())),
                            preferred_element_type=jnp.float32,
                        )
                    )
                for t in range(2):
                    pair = 2 * step + t
                    acc[other_block_ref[2 * pair]] += terms[t][0:width, 0:BLOCK]
                    acc[other_block_ref[2 * pair + 1]] += terms[t][width:, BLOCK:]
                return carry

            lax.fori_loop(0, rounds(count_ref[0], GROUP), group, 0)
            lax.fori_loop(0, rounds(other_count_ref[0], 4), other_group, 0)
        out_ref[...] = acc[0:blocks].astype(out_ref.dtype)

    out = jax.ShapeDtypeStruct((blocks, width, BLOCK), jnp.bfloat16 if last else jnp.float32)
    scratch = [
        pltpu.VMEM((2 * views * half_rows + band_rows + 8, 256), jnp.float32),
        pltpu.VMEM((blocks + 1, width, BLOCK), jnp.float32),
    ]
    us = 3 + 5 * len(parts)
    return call(body, out, tuple(tables + arrays), len(tables), us, "pull_blocks", scratch)


def loss_kernel(u, teacher_width, side_ref, parts_ref, head_ref, teacher_ref, image_ref, grad_ref):
    rows, packed = parts_ref.shape[1], parts_ref.shape[2]
    width = packed // 2
    lane = lax.broadcasted_iota(jnp.int32, (rows, packed), 1)
    head = head_ref[...]

    def halves_of(parts):
        halves = [[], []]
        for pair in range(2):
            one, two = (part.astype(jnp.float32) for part in parts[2 * pair : 2 * pair + 2])
            halves[0].append(jnp.where(lane < width, one, pltpu.roll(two, width, 1)))
            halves[1].append(jnp.where(lane < width, pltpu.roll(one, width, 1), two))
        return [jnp.concatenate(half, axis=1) for half in halves]

    halves = halves_of([parts_ref[d] for d in range(4)])
    targets = halves_of([teacher_ref[side_ref[0] ^ g, u] for g in range(4)])
    rendered_all, grad_all, images = [], [], []
    for half in range(2):
        rendered = halves[half].astype(jnp.bfloat16)
        projected = jnp.dot(rendered, head, preferred_element_type=jnp.float32)
        square = jnp.sum(projected * projected, axis=1, keepdims=True)
        scale = jnp.sqrt(square / teacher_width + 1e-06)
        normed = projected / scale
        residual = normed - targets[half]
        inner = jnp.sum(residual * normed, axis=1, keepdims=True) / teacher_width
        grad_proj = ((residual - normed * inner) / scale).astype(jnp.bfloat16)
        images.append(
            lax.dot_general(
                grad_proj, head, (((1,), (1,)), ((), ())), preferred_element_type=jnp.float32
            )
        )
        rendered_all.append(rendered)
        grad_all.append(grad_proj)
    for pair in range(2):
        cols = slice(2 * pair * width, 2 * (pair + 1) * width)
        first, second = images[0][:, cols], images[1][:, cols]
        image_ref[2 * pair] = jnp.where(lane < width, first, pltpu.roll(second, width, 1)).astype(
            image_ref.dtype
        )
        image_ref[2 * pair + 1] = jnp.where(
            lane < width, pltpu.roll(first, width, 1), second
        ).astype(image_ref.dtype)
    grad_ref[...] = lax.dot_general(
        jnp.concatenate(rendered_all, axis=0),
        jnp.concatenate(grad_all, axis=0),
        (((0,), (0,)), ((), ())),
        preferred_element_type=jnp.float32,
    )


def loss(u, side, parts, head, teacher):
    teacher_width = head.shape[1]
    outs = [
        jax.ShapeDtypeStruct(parts.shape, jnp.bfloat16),
        jax.ShapeDtypeStruct(head.shape, jnp.float32),
    ]
    body = lambda *refs: loss_kernel(u, teacher_width, *refs)
    return call(body, outs, (side, parts, head, teacher), 1, 3, "loss_rows")


def turn_teacher(side, teacher, sides, padded):
    views, width, pixels = teacher.shape
    half_rows = padded // 2
    rows = half_rows // sides
    whole = pixels // 128 * 128

    def body(side_ref, teacher_ref, *rest):
        outs, (across, turned) = rest[:sides], rest[sides:]
        for u in range(views):
            across[width:, :] = jnp.zeros((256 - width, padded), jnp.float32)
            across[0:width, whole:] = jnp.zeros((width, padded - whole), jnp.float32)
            across[0:width, 0:pixels] = teacher_ref[u].astype(jnp.float32)
            turned[...] = across[...].T
            for d in range(sides):
                start = pl.multiple_of((side_ref[0] ^ d) * rows, 16)
                first = turned[pl.ds(start, rows), :]
                second = turned[pl.ds(half_rows + start, rows), :]
                outs[d][u] = beside(first, second).astype(jnp.bfloat16)

    out = jax.ShapeDtypeStruct((views, rows, 2 * width), jnp.bfloat16)
    scratch = [pltpu.VMEM((256, padded), jnp.float32), pltpu.VMEM((padded, 256), jnp.float32)]
    return call(body, [out] * sides, (side, teacher), 1, 6, "turn_teacher", scratch)


def after(value, *earlier):
    return lax.optimization_barrier((value,) + earlier)[0]


def total(*terms):
    acc = terms[0].astype(jnp.float32)
    for term in terms[1:]:
        acc = acc + term.astype(jnp.float32)
    return acc.astype(jnp.bfloat16)


def in_order(own_first, other):
    index, mine = own_first
    return jnp.where(
        index == 0, jnp.concatenate([mine, other], 0), jnp.concatenate([other, mine], 0)
    )


def per_device(points, head_weight, teacher, splat_weight, block_owner, block_local, block_row):
    peers, sides = lax.axis_size("view"), lax.axis_size("feat")
    blocks, width = points.shape[0], points.shape[1]
    view_count, visible, band_rows = splat_weight.shape[:3]
    requests = view_count * visible
    capacity = max(3, (3 * requests + 2 * peers - 1) // (2 * peers))
    quarter = -(-capacity // sides)
    slots = quarter * sides
    pixels = teacher.shape[2]
    unit = 2 * sides * 16
    padded = -(-pixels // unit) * unit
    half_rows = padded // 2
    me, side = lax.axis_index("view"), lax.axis_index("feat")
    line, across, core = me // 2, side // 2, side % 2

    def hop(value, axis, pairs):
        return lax.ppermute(value, axis, pairs)

    def swap(value, axis, k):
        size = peers if axis == "view" else sides
        return hop(value, axis, [(i, i ^ k) for i in range(size)])

    def along(value, moves):
        return hop(value, "view", [(2 * a + y, 2 * b + y) for a, b in moves for y in range(2)])

    ints = jnp.int32
    owners = block_owner.reshape(requests)
    positions = jnp.arange(requests, dtype=ints)
    earlier = (owners[:, None] == owners[None, :]) & (positions[None, :] < positions[:, None])
    rank = jnp.sum(earlier.astype(ints), axis=1)
    peer_ids = me ^ jnp.arange(peers, dtype=ints)
    send_ranks = side * quarter + jnp.arange(quarter, dtype=ints)
    match = (owners[None, None, :] == peer_ids[:, None, None]) & (
        rank[None, None, :] == send_ranks[None, :, None]
    )
    source = jnp.sum(jnp.where(match, positions[None, None, :], 0), axis=2)
    aligned = -(-band_rows // 16) * 16
    listed = splat_weight.reshape(requests, band_rows, BLOCK)
    packed = pack_weights(source.reshape(peers * quarter), listed, peers, aligned)

    view_of = positions // visible
    start = view_of * padded + block_row.reshape(requests) * GRID
    told = jnp.stack([owners, rank, block_local.reshape(requests), start])
    heard = told[None]
    for k in (4, 2, 1):
        heard = jnp.concatenate([heard, swap(heard, "view", k)], axis=0)
    heard = heard.reshape((2, 2, 2) + told.shape).transpose(2, 1, 0, 3, 4).reshape((peers,) + told.shape)
    slot_ids = jnp.arange(slots, dtype=ints)

    def asked_of(owner, told):
        asked = (told[:, None, 0, :] == owner) & (told[:, None, 1, :] == slot_ids[None, :, None])
        filled = jnp.any(asked, axis=2)
        block = jnp.sum(jnp.where(asked, told[:, None, 2, :], 0), axis=2)
        place = jnp.sum(jnp.where(asked, told[:, None, 3, :], 0), axis=2)
        place = jnp.where(filled, place, view_count * padded)
        return jnp.sum(filled.astype(ints), axis=1), block, jnp.where(filled, block, blocks), place

    counts, block_of, pull_of, place_of = asked_of(me, heard)
    pair_counts, _, _, pair_places = asked_of(me ^ 1, heard[::2])
    turn = (slot_ids // quarter) ^ side
    turn = (turn % 2) * 2 + turn // 2
    where_of = turn * quarter + slot_ids % quarter

    weights, hops = {}, None
    for j in (3, 2, 1, 0):
        got = []
        for k in (2 * j + 1, 2 * j):
            value = packed[k] if hops is None else after(packed[k], hops)
            got.append(swap(value, "view", k) if k else value)
        got = hops = jnp.stack(got[::-1])
        got = jnp.concatenate([got, swap(got, "feat", 2)], axis=1)
        weights[j] = jnp.concatenate([got, swap(got, "feat", 1)], axis=1)

    kept, arrived = {}, None
    for j in (3, 2, 1, 0):
        k = 2 * j + 1
        given = spread(counts[k : k + 1], block_of[k], where_of, weights[j][1], points)
        arrived = swap(given if arrived is None else after(given, arrived), "view", 1)
        k = 2 * j
        kept[j] = render(
            counts[k : k + 1], block_of[k], place_of[k], where_of,
            pair_counts[j : j + 1], pair_places[j], weights[j][0], points, arrived, view_count, half_rows,
        )

    side_id = side.reshape(1).astype(ints)
    teacher = after(teacher.transpose(1, 0, 2), weights[0])
    target = turn_teacher(side_id, teacher, sides, padded)
    target = jnp.stack([swap(target[d], "feat", d) if d else target[d] for d in range(sides)])
    head_weight = after(head_weight, weights[0])
    head = jnp.concatenate([head_weight, swap(head_weight, "feat", 2)], axis=0)
    head = jnp.concatenate([head, swap(head, "feat", 1)], axis=0)

    rendered = []
    for u in range(view_count):
        far = along(kept[3][u], [(0, 1), (3, 2)])
        mid = total(kept[2][u], far)
        inward = along(mid, [(0, 1), (3, 2)])
        between = along(mid, [(1, 2), (2, 1)])
        near = along(total(kept[1][u], between), [(0, 1), (1, 0), (2, 3), (3, 2)])
        centre = along(total(kept[3][u], inward), [(1, 2), (2, 1)])
        rendered.append(total(kept[0][u], near, centre))

    grads, images = [], []
    side_rows, seventh = half_rows // 2, half_rows // sides
    for u in range(view_count):
        whole = rendered[u]
        mine = lax.dynamic_slice_in_dim(whole, across * side_rows, side_rows, 0)
        other = lax.dynamic_slice_in_dim(whole, (1 - across) * side_rows, side_rows, 0)
        both = jnp.stack([mine, swap(other, "feat", 2)])
        mine = lax.dynamic_slice_in_dim(both, core * seventh, seventh, 1)
        other = lax.dynamic_slice_in_dim(both, (1 - core) * seventh, seventh, 1)
        parts = jnp.concatenate([mine, swap(other, "feat", 1)], axis=0)
        image, grad = loss(u, side_id, parts, head, target)
        grads.append(grad)
        back = swap(image[2:4], "feat", 1)
        rows = [in_order((core, image[i]), back[i]) for i in range(2)]
        images.append(in_order((across, rows[0]), swap(rows[1], "feat", 2)))

    middle = (line == 1) | (line == 2)
    chunks = {j: [] for j in range(4)}
    marks = []
    for u in range(view_count):
        own = images[u]
        near = along(own, [(0, 1), (1, 0), (2, 3), (3, 2)])
        centre = along(own, [(1, 2), (2, 1)])
        out_near = along(centre, [(1, 0), (2, 3)])
        cross = along(near, [(1, 2), (2, 1)])
        out_far = along(cross, [(1, 0), (2, 3)])
        marks.append((near, cross, out_far))
        for j, value in enumerate(
            (own, near, jnp.where(middle, cross, out_near), jnp.where(middle, centre, out_far))
        ):
            chunks[j].append(value)
    parts, bands = [], None
    for j in range(4):
        bands = pick(pair_counts[j : j + 1], pair_places[j], chunks[j], slots, aligned)
        bands = swap(bands if not parts else after(bands, parts[-1]["bands"]), "view", 1)
        own, other = 2 * j, 2 * j + 1
        parts.append(
            dict(
                count=counts[own : own + 1], block=pull_of[own], place=place_of[own],
                other_count=counts[other : other + 1], other_block=pull_of[other],
                weights=weights[j], images=chunks[j], bands=bands,
            )
        )
    early = pull(parts[:3], where_of, None, blocks, False)
    grad_points = pull(parts[3:], where_of, early, blocks, True)

    grad = grads[0]
    for more in grads[1:]:
        grad = grad + more
    grad = grad.reshape(2, 2, width, grad.shape[1])
    grad = grad[0] + swap(grad[1], "feat", 1)
    grad = grad[0] + swap(grad[1], "feat", 2)
    marks = [marks[u][i] for i in range(3) for u in range(view_count)]
    bits = [(1, me % 2), (4, me // 4), (2, line % 2)]
    for (k, bit), mark in zip(bits, marks):
        rows = grad.shape[0] // 2
        grad = after(grad, mark)
        mine = lax.dynamic_slice_in_dim(grad, bit * rows, rows, 0)
        other = lax.dynamic_slice_in_dim(grad, (1 - bit) * rows, rows, 0)
        grad = mine + swap(other, "view", k)
    grad = grad / (view_count * peers * GRID)
    for (k, bit), mark in zip(bits[::-1], marks[3:]):
        grad = after(grad, mark)
        grad = in_order((bit, grad), swap(grad, "view", k))
    return (grad_points, grad)


def solution(mesh):
    size = mesh.shape
    paired = size["view"] == 8 and size["feat"] == 4
    placed = (
        P("view", "feat", None),
        P("feat", None),
        P("feat", "view", None),
        P("view", None, None, None),
        P("view", None, None),
        P("view", None),
        P("view", None),
    )
    return jax.shard_map(
        per_device if paired else per_device_listed,
        mesh=mesh,
        in_specs=placed,
        out_specs=(P("view", "feat", None), P("feat", None)),
        check_vma=False,
    )
```

profile of v0, /device:TPU:0, one launch (start us, length us, event | category | flops | bytes accessed | tf_op | source)
XLA Modules:
  0.0 333.2 jit_solution(7977113082021643697)
XLA Ops:
  3.4 4.1 %collective-permute-start = (s32[1,4,128]{2,1,0:T(4,128)S(1)}, s32[1,4,128]{2,1,0:T(4,128)S(1)}, u32[]{:S(2)}, u32[]{:S(2)}) collective-permute-start(s32[1,4,128]{2,1,0:T(4,128)S(1)} %add_bitcast_fusion), channel_id=1, source_target_pairs={{0,16},{4,20},{8,24},{12,28},{16,0},{20,4},{24,8},{28,12},{1,17},{... | collective-permute-start | bytes 6152 | tf_op jit(solution)/shard_map/ppermute | solution.py:482
  8.0 3.3 copy.22
  14.1 4.3 %collective-permute-start.4 = (bf16[6,80,128]{2,1,0:T(8,128)(2,1)S(1)}, bf16[6,80,128]{2,1,0:T(8,128)(2,1)S(1)}, u32[]{:S(2)}, u32[]{:S(2)}) collective-permute-start(bf16[6,80,128]{2,1,0:T(8,128)(2,1)S(1)} %get-tuple-element.47), channel_id=1, source_target_pairs={{0,28},{4,24},{8,20},{12,16},{16,12},{20,8},{24,4},{28,0},{1,29},{... | collective-permute-start | bytes 368648 | tf_op jit(solution)/shard_map/ppermute | solution.py:482
  19.2 2.8 collective-permute-done.2
  23.6 3.8 %collective-permute-start.7 = (bf16[6,80,128]{2,1,0:T(8,128)(2,1)S(1)}, bf16[6,80,128]{2,1,0:T(8,128)(2,1)S(1)}, u32[]{:S(2)}, u32[]{:S(2)}) collective-permute-start(bf16[6,80,128]{2,1,0:T(8,128)(2,1)S(1)} %get-tuple-element.51), channel_id=1, source_target_pairs={{0,16},{4,20},{8,24},{12,28},{16,0},{20,4},{24,8},{28,12},{1,17},{... | collective-permute-start | bytes 368648 | tf_op jit(solution)/shard_map/ppermute | solution.py:482
  28.9 7.6 %collective-permute-done.7 = bf16[6,80,128]{2,1,0:T(8,128)(2,1)S(1)} collective-permute-done((bf16[6,80,128]{2,1,0:T(8,128)(2,1)S(1)}, bf16[6,80,128]{2,1,0:T(8,128)(2,1)S(1)}, u32[]{:S(2)}, u32[]{:S(2)}) %collective-permute-start.7) | collective-permute-done | bytes 122912 | tf_op jit(solution)/shard_map/ppermute | solution.py:482
  37.9 3.0 collective-permute-start.10
  47.8 4.2 %collective-permute-done.11 = bf16[6,80,128]{2,1,0:T(8,128)(2,1)S(1)} collective-permute-done((bf16[6,80,128]{2,1,0:T(8,128)(2,1)S(1)}, bf16[6,80,128]{2,1,0:T(8,128)(2,1)S(1)}, u32[]{:S(2)}, u32[]{:S(2)}) %collective-permute-start.11) | collective-permute-done | bytes 122912 | tf_op jit(solution)/shard_map/ppermute | solution.py:482
  52.5 3.2 collective-permute-done.14
  55.9 2.9 collective-permute-done.12
  65.8 2.7 spread_blocks.6
  68.7 2.7 spread_blocks.5
  71.6 10.8 %collective-permute-done.18.other_ref = bf16[12,80,384]{2,1,0:T(8,128)(2,1)S(1)} collective-permute-done((bf16[12,80,384]{2,1,0:T(8,128)(2,1)S(1)}, bf16[12,80,384]{2,1,0:T(8,128)(2,1)S(1)}, u32[]{:S(2)}, u32[]{:S(2)}) %collective-permute-start.18) | collective-permute-done | bytes 737312 | tf_op jit(solution)/shard_map/ppermute | solution.py:482
  85.4 3.8 %render_blocks.7 = (bf16[704,384]{1,0:T(8,128)(2,1)S(1)}, bf16[704,384]{1,0:T(8,128)(2,1)S(1)}) custom-call(s32[1]{0:T(128)} %get-tuple-element.157.count_ref.refs_1_, s32[24]{0:T(128)S(1)} %get-tuple-element.132.block_ref, s32[24]{0:T(128)S(1)} %get-tuple-element.142.place_ref.refs_3_, s32[24]{0:T(128)S(1)} %fusion.12.where_ref.refs_0_, ...), custom_call_target="tpu_custom_call" | custom-call | flops 5000000000 | bytes 10000000 | tf_op jit(solution)/shard_map/render_blocks/pallas_call | solution.py:121
  89.2 3.5 %collective-permute-start.22 = (bf16[704,384]{1,0:T(8,128)(2,1)S(1)}, bf16[704,384]{1,0:T(8,128)(2,1)S(1)}, u32[]{:S(2)}, u32[]{:S(2)}) collective-permute-start(bf16[704,384]{1,0:T(8,128)(2,1)S(1)} %get-tuple-element.66), channel_id=1, source_target_pairs={{0,8},{4,12},{24,16},{28,20},{1,9},{5,13},{25,17},{29,21},{2,10},{... | collective-permute-start | bytes 1622024 | tf_op jit(solution)/shard_map/ppermute | solution.py:482
  95.4 5.0 %collective-permute-done.19.other_ref = bf16[12,80,384]{2,1,0:T(8,128)(2,1)S(1)} collective-permute-done((bf16[12,80,384]{2,1,0:T(8,128)(2,1)S(1)}, bf16[12,80,384]{2,1,0:T(8,128)(2,1)S(1)}, u32[]{:S(2)}, u32[]{:S(2)}) %collective-permute-start.19) | collective-permute-done | bytes 737312 | tf_op jit(solution)/shard_map/ppermute | solution.py:482
  100.9 4.2 %render_blocks.6 = (bf16[704,384]{1,0:T(8,128)(2,1)S(1)}, bf16[704,384]{1,0:T(8,128)(2,1)S(1)}) custom-call(s32[1]{0:T(128)} %get-tuple-element.151.count_ref.refs_11_, s32[24]{0:T(128)S(1)} %get-tuple-element.133.block_ref, s32[24]{0:T(128)S(1)} %get-tuple-element.140.place_ref.refs_13_, s32[24]{0:T(128)S(1)} %fusion.12.where_ref.refs_0_, ...), custom_call_target="tpu_custom_call" | custom-call | flops 5000000000 | bytes 10000000 | tf_op jit(solution)/shard_map/render_blocks/pallas_call | solution.py:121
  105.5 4.4 %collective-permute-start.25 = (bf16[704,384]{1,0:T(8,128)(2,1)S(1)}, bf16[704,384]{1,0:T(8,128)(2,1)S(1)}, u32[]{:S(2)}, u32[]{:S(2)}) collective-permute-start(bf16[704,384]{1,0:T(8,128)(2,1)S(1)} %add_convert_fusion.7), channel_id=1, source_target_pairs={{0,8},{4,12},{24,16},{28,20},{1,9},{5,13},{25,17},{29,21},{2,10},{... | collective-permute-start | bytes 1622024 | tf_op jit(solution)/shard_map/ppermute | solution.py:482
  109.9 7.0 %collective-permute-done.40 = bf16[704,384]{1,0:T(8,128)(2,1)S(1)} collective-permute-done((bf16[704,384]{1,0:T(8,128)(2,1)S(1)}, bf16[704,384]{1,0:T(8,128)(2,1)S(1)}, u32[]{:S(2)}, u32[]{:S(2)}) %collective-permute-start.40) | collective-permute-done | bytes 540704 | tf_op jit(solution)/shard_map/ppermute | solution.py:482
  117.1 4.4 %collective-permute-start.43 = (bf16[704,384]{1,0:T(8,128)(2,1)S(1)}, bf16[704,384]{1,0:T(8,128)(2,1)S(1)}, u32[]{:S(2)}, u32[]{:S(2)}) collective-permute-start(bf16[704,384]{1,0:T(8,128)(2,1)S(1)} %add_convert_fusion.3), channel_id=1, source_target_pairs={{0,8},{4,12},{24,16},{28,20},{1,9},{5,13},{25,17},{29,21},{2,10},{... | collective-permute-start | bytes 1622024 | tf_op jit(solution)/shard_map/ppermute | solution.py:482
  121.5 2.7 spread_blocks.4
  124.9 3.6 %collective-permute-done.25 = bf16[704,384]{1,0:T(8,128)(2,1)S(1)} collective-permute-done((bf16[704,384]{1,0:T(8,128)(2,1)S(1)}, bf16[704,384]{1,0:T(8,128)(2,1)S(1)}, u32[]{:S(2)}, u32[]{:S(2)}) %collective-permute-start.25) | collective-permute-done | bytes 540704 | tf_op jit(solution)/shard_map/ppermute | solution.py:482
  129.3 9.1 %collective-permute-done.43 = bf16[704,384]{1,0:T(8,128)(2,1)S(1)} collective-permute-done((bf16[704,384]{1,0:T(8,128)(2,1)S(1)}, bf16[704,384]{1,0:T(8,128)(2,1)S(1)}, u32[]{:S(2)}, u32[]{:S(2)}) %collective-permute-start.43) | collective-permute-done | bytes 540704 | tf_op jit(solution)/shard_map/ppermute | solution.py:482
  140.3 4.4 %render_blocks.5 = (bf16[704,384]{1,0:T(8,128)(2,1)S(1)}, bf16[704,384]{1,0:T(8,128)(2,1)S(1)}) custom-call(s32[1]{0:T(128)} %get-tuple-element.152.count_ref.refs_6_, s32[24]{0:T(128)S(1)} %get-tuple-element.134.block_ref, s32[24]{0:T(128)S(1)} %get-tuple-element.141.place_ref.refs_8_, s32[24]{0:T(128)S(1)} %fusion.12.where_ref.refs_0_, ...), custom_call_target="tpu_custom_call" | custom-call | flops 5000000000 | bytes 10000000 | tf_op jit(solution)/shard_map/render_blocks/pallas_call | solution.py:121
  145.8 6.6 %collective-permute-start.24 = (bf16[704,384]{1,0:T(8,128)(2,1)S(1)}, bf16[704,384]{1,0:T(8,128)(2,1)S(1)}, u32[]{:S(2)}, u32[]{:S(2)}) collective-permute-start(bf16[704,384]{1,0:T(8,128)(2,1)S(1)} %add_convert_fusion.6), channel_id=1, source_target_pairs={{0,8},{4,12},{8,0},{12,4},{16,24},{20,28},{24,16},{28,20},{1,9},{5... | collective-permute-start | bytes 1622024 | tf_op jit(solution)/shard_map/ppermute | solution.py:482
  152.6 3.7 %collective-permute-done.21.other_ref = bf16[12,80,384]{2,1,0:T(8,128)(2,1)S(1)} collective-permute-done((bf16[12,80,384]{2,1,0:T(8,128)(2,1)S(1)}, bf16[12,80,384]{2,1,0:T(8,128)(2,1)S(1)}, u32[]{:S(2)}, u32[]{:S(2)}) %collective-permute-start.21) | collective-permute-done | bytes 737312 | tf_op jit(solution)/shard_map/ppermute | solution.py:482
  156.3 4.4 %render_blocks.4 = (bf16[704,384]{1,0:T(8,128)(2,1)S(1)}, bf16[704,384]{1,0:T(8,128)(2,1)S(1)}) custom-call(s32[1]{0:T(128)} %get-tuple-element.155.count_ref.refs_1_, s32[24]{0:T(128)S(1)} %get-tuple-element.138.block_ref, s32[24]{0:T(128)S(1)} %get-tuple-element.139.place_ref.refs_3_, s32[24]{0:T(128)S(1)} %fusion.12.where_ref.refs_0_, ...), custom_call_target="tpu_custom_call" | custom-call | flops 5000000000 | bytes 10000000 | tf_op jit(solution)/shard_map/render_blocks/pallas_call | solution.py:121
  162.7 2.9 collective-permute-done.24
  165.6 8.5 %collective-permute-done.42 = bf16[704,384]{1,0:T(8,128)(2,1)S(1)} collective-permute-done((bf16[704,384]{1,0:T(8,128)(2,1)S(1)}, bf16[704,384]{1,0:T(8,128)(2,1)S(1)}, u32[]{:S(2)}, u32[]{:S(2)}) %collective-permute-start.42) | collective-permute-done | bytes 540704 | tf_op jit(solution)/shard_map/ppermute | solution.py:482
  177.1 6.9 %collective-permute-done.45 = bf16[352,384]{1,0:T(8,128)(2,1)S(1)} collective-permute-done((bf16[352,384]{1,0:T(8,128)(2,1)S(1)}, bf16[352,384]{1,0:T(8,128)(2,1)S(1)}, u32[]{:S(2)}, u32[]{:S(2)}) %collective-permute-start.45) | collective-permute-done | bytes 270368 | tf_op jit(solution)/shard_map/ppermute | solution.py:482
  184.2 2.9 collective-permute-done.27
  187.3 2.8 loss_rows.3
  190.2 2.8 loss_rows.2
  199.1 5.6 %collective-permute-done.48 = bf16[352,384]{1,0:T(8,128)(2,1)S(1)} collective-permute-done((bf16[352,384]{1,0:T(8,128)(2,1)S(1)}, bf16[352,384]{1,0:T(8,128)(2,1)S(1)}, u32[]{:S(2)}, u32[]{:S(2)}) %collective-permute-start.48) | collective-permute-done | bytes 270368 | tf_op jit(solution)/shard_map/ppermute | solution.py:482
  204.9 4.3 %collective-permute-start.50 = (bf16[704,384]{1,0:T(8,128)(2,1)S(1)}, bf16[704,384]{1,0:T(8,128)(2,1)S(1)}, u32[]{:S(2)}, u32[]{:S(2)}) collective-permute-start(bf16[704,384]{1,0:T(8,128)(2,1)S(1)} %maximum_select_fusion.2.rest_1_.refs_19_), channel_id=1, source_target_pairs={{0,8},{4,12},{8,0},{12,4},{16,24},{20,28},{24,16},{28,20},{1,9},{5... | collective-permute-start | bytes 1622024 | tf_op jit(solution)/shard_map/ppermute | solution.py:482
  210.2 4.3 %collective-permute-start.37 = (bf16[704,384]{1,0:T(8,128)(2,1)S(1)}, bf16[704,384]{1,0:T(8,128)(2,1)S(1)}, u32[]{:S(2)}, u32[]{:S(2)}) collective-permute-start(bf16[704,384]{1,0:T(8,128)(2,1)S(1)} %maximum_select_fusion.1.rest_0_.refs_18_), channel_id=1, source_target_pairs={{0,8},{4,12},{8,0},{12,4},{16,24},{20,28},{24,16},{28,20},{1,9},{5... | collective-permute-start | bytes 1622024 | tf_op jit(solution)/shard_map/ppermute | solution.py:482
  217.0 5.3 %collective-permute-done.50.rest_1_.refs_23_ = bf16[704,384]{1,0:T(8,128)(2,1)S(1)} collective-permute-done((bf16[704,384]{1,0:T(8,128)(2,1)S(1)}, bf16[704,384]{1,0:T(8,128)(2,1)S(1)}, u32[]{:S(2)}, u32[]{:S(2)}) %collective-permute-start.50) | collective-permute-done | bytes 540704 | tf_op jit(solution)/shard_map/ppermute | solution.py:482
  224.5 7.7 %collective-permute-done.37.rest_0_.refs_22_ = bf16[704,384]{1,0:T(8,128)(2,1)S(1)} collective-permute-done((bf16[704,384]{1,0:T(8,128)(2,1)S(1)}, bf16[704,384]{1,0:T(8,128)(2,1)S(1)}, u32[]{:S(2)}, u32[]{:S(2)}) %collective-permute-start.37) | collective-permute-done | bytes 540704 | tf_op jit(solution)/shard_map/ppermute | solution.py:482
  240.4 5.4 %collective-permute-done.60 = f32[192,768]{1,0:T(8,128)S(1)} collective-permute-done((f32[192,768]{1,0:T(8,128)S(1)}, f32[192,768]{1,0:T(8,128)S(1)}, u32[]{:S(2)}, u32[]{:S(2)}) %collective-permute-start.60) | collective-permute-done | bytes 589856 | tf_op jit(solution)/shard_map/ppermute | solution.py:482
  247.4 3.3 collective-permute-done.54
  252.0 10.3 %collective-permute-done.53 = bf16[704,384]{1,0:T(8,128)(2,1)S(1)} collective-permute-done((bf16[704,384]{1,0:T(8,128)(2,1)S(1)}, bf16[704,384]{1,0:T(8,128)(2,1)S(1)}, u32[]{:S(2)}, u32[]{:S(2)}) %collective-permute-start.53) | collective-permute-done | bytes 540704 | tf_op jit(solution)/shard_map/ppermute | solution.py:482
  262.5 8.2 %collective-permute-start.62 = (f32[48,768]{1,0:T(8,128)S(1)}, f32[48,768]{1,0:T(8,128)S(1)}, u32[]{:S(2)}, u32[]{:S(2)}) collective-permute-start(f32[48,768]{1,0:T(8,128)S(1)} %constant_dynamic-slice_fusion.1), channel_id=1, source_target_pairs={{0,16},{4,20},{8,24},{12,28},{16,0},{20,4},{24,8},{28,12},{1,17},{... | collective-permute-start | bytes 442376 | tf_op jit(solution)/shard_map/ppermute | solution.py:482
  275.1 2.7 collective-permute-start.63
  277.9 10.2 %collective-permute-done.63 = f32[24,768]{1,0:T(8,128)S(1)} collective-permute-done((f32[24,768]{1,0:T(8,128)S(1)}, f32[24,768]{1,0:T(8,128)S(1)}, u32[]{:S(2)}, u32[]{:S(2)}) %collective-permute-start.63) | collective-permute-done | bytes 73760 | tf_op jit(solution)/shard_map/ppermute | solution.py:482
  288.2 5.2 %collective-permute-done.64 = f32[24,768]{1,0:T(8,128)S(1)} collective-permute-done((f32[24,768]{1,0:T(8,128)S(1)}, f32[24,768]{1,0:T(8,128)S(1)}, u32[]{:S(2)}, u32[]{:S(2)}) %collective-permute-start.64) | collective-permute-done | bytes 73760 | tf_op jit(solution)/shard_map/ppermute | solution.py:482
  295.4 5.0 %collective-permute-done.65 = f32[48,768]{1,0:T(8,128)S(1)} collective-permute-done((f32[48,768]{1,0:T(8,128)S(1)}, f32[48,768]{1,0:T(8,128)S(1)}, u32[]{:S(2)}, u32[]{:S(2)}) %collective-permute-start.65) | collective-permute-done | bytes 147488 | tf_op jit(solution)/shard_map/ppermute | solution.py:482
  302.5 20.3 %pull_blocks.2.refs_10_ = f32[64,192,128]{2,1,0:T(8,128)} custom-call(s32[24]{0:T(128)S(1)} %fusion.12.where_ref.refs_0_, s32[1]{0:T(128)} %get-tuple-element.155.count_ref.refs_1_, s32[24]{0:T(128)S(1)} %get-tuple-element.128.refs_2_, s32[24]{0:T(128)S(1)} %get-tuple-element.139.place_ref.refs_3_, s32[1]{0:T(128)} %get-tuple-element.150.count_ref.refs_4_, ...), custom_call_target="tpu_custom_call" | custom-call | flops 17999998976 | bytes 36000000 | tf_op jit(solution)/shard_map/pull_blocks/pallas_call | solution.py:121
  323.7 9.5 %pull_blocks.3 = bf16[64,192,128]{2,1,0:T(8,128)(2,1)} custom-call(s32[24]{0:T(128)S(1)} %fusion.12.where_ref.refs_0_, s32[1]{0:T(128)} %get-tuple-element.157.count_ref.refs_1_, s32[24]{0:T(128)S(1)} %get-tuple-element.130.refs_2_, s32[24]{0:T(128)S(1)} %get-tuple-element.142.place_ref.refs_3_, s32[1]{0:T(128)} %get-tuple-element.156.count_ref.refs_4_, ...), custom_call_target="tpu_custom_call" | custom-call | flops 8000000000 | bytes 16000000 | tf_op jit(solution)/shard_map/pull_blocks/pallas_call | solution.py:121
  (224 shorter events, 75.2 us)
Async XLA Ops:
  23.6 12.9 %collective-permute-start.7 = (bf16[6,80,128]{2,1,0:T(8,128)(2,1)S(1)}, bf16[6,80,128]{2,1,0:T(8,128)(2,1)S(1)}, u32[]{:S(2)}, u32[]{:S(2)}) collective-permute-start(bf16[6,80,128]{2,1,0:T(8,128)(2,1)S(1)} %get-tuple-element.51), channel_id=1, source_target_pairs={{0,16},{4,20},{8,24},{12,28},{16,0},{20,4},{24,8},{28,12},{1,17},{... | collective-permute-start | bytes 368648 | tf_op jit(solution)/shard_map/ppermute | solution.py:482
  27.4 20.2 %collective-permute-start.5 = (bf16[2,6,80,128]{3,2,1,0:T(8,128)(2,1)S(1)}, bf16[2,6,80,128]{3,2,1,0:T(8,128)(2,1)S(1)}, u32[]{:S(2)}, u32[]{:S(2)}) collective-permute-start(bf16[2,6,80,128]{3,2,1,0:T(8,128)(2,1)S(1)} %pad_maximum_fusion.12), channel_id=1, source_target_pairs={{0,2},{1,3},{2,0},{3,1},{4,6},{5,7},{6,4},{7,5},{8,10},{9,11},{10,... | collective-permute-start | bytes 737288 | tf_op jit(solution)/shard_map/ppermute | solution.py:482
  45.3 10.5 %collective-permute-start.14 = (bf16[2,6,80,128]{3,2,1,0:T(8,128)(2,1)S(1)}, bf16[2,6,80,128]{3,2,1,0:T(8,128)(2,1)S(1)}, u32[]{:S(2)}, u32[]{:S(2)}) collective-permute-start(bf16[2,6,80,128]{3,2,1,0:T(8,128)(2,1)S(1)} %pad_maximum_fusion.14), channel_id=1, source_target_pairs={{0,2},{1,3},{2,0},{3,1},{4,6},{5,7},{6,4},{7,5},{8,10},{9,11},{10,... | collective-permute-start | bytes 737288 | tf_op jit(solution)/shard_map/ppermute | solution.py:482
  47.7 11.2 %collective-permute-start.6 = (bf16[2,12,80,128]{3,2,1,0:T(8,128)(2,1)S(1)}, bf16[2,12,80,128]{3,2,1,0:T(8,128)(2,1)S(1)}, u32[]{:S(2)}, u32[]{:S(2)}) collective-permute-start(bf16[2,12,80,128]{3,2,1,0:T(8,128)(2,1)S(1)} %pad_maximum_fusion.8), channel_id=1, source_target_pairs={{0,1},{1,0},{2,3},{3,2},{4,5},{5,4},{6,7},{7,6},{8,9},{9,8},{10,11... | collective-permute-start | bytes 1474568 | tf_op jit(solution)/shard_map/ppermute | solution.py:482
  52.4 11.1 %collective-permute-start.17 = (bf16[2,12,80,128]{3,2,1,0:T(8,128)(2,1)S(1)}, bf16[2,12,80,128]{3,2,1,0:T(8,128)(2,1)S(1)}, u32[]{:S(2)}, u32[]{:S(2)}) collective-permute-start(bf16[2,12,80,128]{3,2,1,0:T(8,128)(2,1)S(1)} %pad_maximum_fusion.11), channel_id=1, source_target_pairs={{0,1},{1,0},{2,3},{3,2},{4,5},{5,4},{6,7},{7,6},{8,9},{9,8},{10,11... | collective-permute-start | bytes 1474568 | tf_op jit(solution)/shard_map/ppermute | solution.py:482
  55.8 12.7 %collective-permute-start.15 = (bf16[2,12,80,128]{3,2,1,0:T(8,128)(2,1)S(1)}, bf16[2,12,80,128]{3,2,1,0:T(8,128)(2,1)S(1)}, u32[]{:S(2)}, u32[]{:S(2)}) collective-permute-start(bf16[2,12,80,128]{3,2,1,0:T(8,128)(2,1)S(1)} %pad_maximum_fusion.10), channel_id=1, source_target_pairs={{0,1},{1,0},{2,3},{3,2},{4,5},{5,4},{6,7},{7,6},{8,9},{9,8},{10,11... | collective-permute-start | bytes 1474568 | tf_op jit(solution)/shard_map/ppermute | solution.py:482
  58.8 12.6 %collective-permute-start.13 = (bf16[2,12,80,128]{3,2,1,0:T(8,128)(2,1)S(1)}, bf16[2,12,80,128]{3,2,1,0:T(8,128)(2,1)S(1)}, u32[]{:S(2)}, u32[]{:S(2)}) collective-permute-start(bf16[2,12,80,128]{3,2,1,0:T(8,128)(2,1)S(1)} %pad_maximum_fusion.9), channel_id=1, source_target_pairs={{0,1},{1,0},{2,3},{3,2},{4,5},{5,4},{6,7},{7,6},{8,9},{9,8},{10,11... | collective-permute-start | bytes 1474568 | tf_op jit(solution)/shard_map/ppermute | solution.py:482
  63.4 18.9 %collective-permute-start.18 = (bf16[12,80,384]{2,1,0:T(8,128)(2,1)S(1)}, bf16[12,80,384]{2,1,0:T(8,128)(2,1)S(1)}, u32[]{:S(2)}, u32[]{:S(2)}) collective-permute-start(bf16[12,80,384]{2,1,0:T(8,128)(2,1)S(1)} %spread_blocks.7), channel_id=1, source_target_pairs={{0,4},{4,0},{8,12},{12,8},{16,20},{20,16},{24,28},{28,24},{1,5},{5... | collective-permute-start | bytes 2211848 | tf_op jit(solution)/shard_map/ppermute | solution.py:482
  82.4 18.1 %collective-permute-start.19 = (bf16[12,80,384]{2,1,0:T(8,128)(2,1)S(1)}, bf16[12,80,384]{2,1,0:T(8,128)(2,1)S(1)}, u32[]{:S(2)}, u32[]{:S(2)}) collective-permute-start(bf16[12,80,384]{2,1,0:T(8,128)(2,1)S(1)} %spread_blocks.6), channel_id=1, source_target_pairs={{0,4},{4,0},{8,12},{12,8},{16,20},{20,16},{24,28},{28,24},{1,5},{5... | collective-permute-start | bytes 2211848 | tf_op jit(solution)/shard_map/ppermute | solution.py:482
  89.2 16.2 %collective-permute-start.22 = (bf16[704,384]{1,0:T(8,128)(2,1)S(1)}, bf16[704,384]{1,0:T(8,128)(2,1)S(1)}, u32[]{:S(2)}, u32[]{:S(2)}) collective-permute-start(bf16[704,384]{1,0:T(8,128)(2,1)S(1)} %get-tuple-element.66), channel_id=1, source_target_pairs={{0,8},{4,12},{24,16},{28,20},{1,9},{5,13},{25,17},{29,21},{2,10},{... | collective-permute-start | bytes 1622024 | tf_op jit(solution)/shard_map/ppermute | solution.py:482
  92.7 59.8 %collective-permute-start.29 = (bf16[192,768]{1,0:T(8,128)(2,1)S(1)}, bf16[192,768]{1,0:T(8,128)(2,1)S(1)}, u32[]{:S(2)}, u32[]{:S(2)}) collective-permute-start(bf16[192,768]{1,0:T(8,128)(2,1)S(1)} %copy-done.6), channel_id=1, source_target_pairs={{0,2},{1,3},{2,0},{3,1},{4,6},{5,7},{6,4},{7,5},{8,10},{9,11},{10,... | collective-permute-start | bytes 884744 | tf_op jit(solution)/shard_map/ppermute | solution.py:482
  94.1 22.8 %collective-permute-start.40 = (bf16[704,384]{1,0:T(8,128)(2,1)S(1)}, bf16[704,384]{1,0:T(8,128)(2,1)S(1)}, u32[]{:S(2)}, u32[]{:S(2)}) collective-permute-start(bf16[704,384]{1,0:T(8,128)(2,1)S(1)} %get-tuple-element.77), channel_id=1, source_target_pairs={{0,8},{4,12},{24,16},{28,20},{1,9},{5,13},{25,17},{29,21},{2,10},{... | collective-permute-start | bytes 1622024 | tf_op jit(solution)/shard_map/ppermute | solution.py:482
  100.5 38.9 %collective-permute-start.20 = (bf16[12,80,384]{2,1,0:T(8,128)(2,1)S(1)}, bf16[12,80,384]{2,1,0:T(8,128)(2,1)S(1)}, u32[]{:S(2)}, u32[]{:S(2)}) collective-permute-start(bf16[12,80,384]{2,1,0:T(8,128)(2,1)S(1)} %spread_blocks.5), channel_id=1, source_target_pairs={{0,4},{4,0},{8,12},{12,8},{16,20},{20,16},{24,28},{28,24},{1,5},{5... | collective-permute-start | bytes 2211848 | tf_op jit(solution)/shard_map/ppermute | solution.py:482
  105.5 23.0 %collective-permute-start.25 = (bf16[704,384]{1,0:T(8,128)(2,1)S(1)}, bf16[704,384]{1,0:T(8,128)(2,1)S(1)}, u32[]{:S(2)}, u32[]{:S(2)}) collective-permute-start(bf16[704,384]{1,0:T(8,128)(2,1)S(1)} %add_convert_fusion.7), channel_id=1, source_target_pairs={{0,8},{4,12},{24,16},{28,20},{1,9},{5,13},{25,17},{29,21},{2,10},{... | collective-permute-start | bytes 1622024 | tf_op jit(solution)/shard_map/ppermute | solution.py:482
  117.1 21.4 %collective-permute-start.43 = (bf16[704,384]{1,0:T(8,128)(2,1)S(1)}, bf16[704,384]{1,0:T(8,128)(2,1)S(1)}, u32[]{:S(2)}, u32[]{:S(2)}) collective-permute-start(bf16[704,384]{1,0:T(8,128)(2,1)S(1)} %add_convert_fusion.3), channel_id=1, source_target_pairs={{0,8},{4,12},{24,16},{28,20},{1,9},{5,13},{25,17},{29,21},{2,10},{... | collective-permute-start | bytes 1622024 | tf_op jit(solution)/shard_map/ppermute | solution.py:482
  124.2 20.5 %collective-permute-start.23 = (bf16[704,384]{1,0:T(8,128)(2,1)S(1)}, bf16[704,384]{1,0:T(8,128)(2,1)S(1)}, u32[]{:S(2)}, u32[]{:S(2)}) collective-permute-start(bf16[704,384]{1,0:T(8,128)(2,1)S(1)} %add_convert_fusion.7), channel_id=1, source_target_pairs={{8,16},{12,20},{16,8},{20,12},{9,17},{13,21},{17,9},{21,13},{10,18... | collective-permute-start | bytes 1622024 | tf_op jit(solution)/shard_map/ppermute | solution.py:482
  128.5 17.3 %collective-permute-start.41 = (bf16[704,384]{1,0:T(8,128)(2,1)S(1)}, bf16[704,384]{1,0:T(8,128)(2,1)S(1)}, u32[]{:S(2)}, u32[]{:S(2)}) collective-permute-start(bf16[704,384]{1,0:T(8,128)(2,1)S(1)} %add_convert_fusion.3), channel_id=1, source_target_pairs={{8,16},{12,20},{16,8},{20,12},{9,17},{13,21},{17,9},{21,13},{10,18... | collective-permute-start | bytes 1622024 | tf_op jit(solution)/shard_map/ppermute | solution.py:482
  138.5 22.3 %collective-permute-start.26 = (bf16[704,384]{1,0:T(8,128)(2,1)S(1)}, bf16[704,384]{1,0:T(8,128)(2,1)S(1)}, u32[]{:S(2)}, u32[]{:S(2)}) collective-permute-start(bf16[704,384]{1,0:T(8,128)(2,1)S(1)} %add_convert_fusion.5), channel_id=1, source_target_pairs={{8,16},{12,20},{16,8},{20,12},{9,17},{13,21},{17,9},{21,13},{10,18... | collective-permute-start | bytes 1622024 | tf_op jit(solution)/shard_map/ppermute | solution.py:482
  139.3 17.0 %collective-permute-start.21 = (bf16[12,80,384]{2,1,0:T(8,128)(2,1)S(1)}, bf16[12,80,384]{2,1,0:T(8,128)(2,1)S(1)}, u32[]{:S(2)}, u32[]{:S(2)}) collective-permute-start(bf16[12,80,384]{2,1,0:T(8,128)(2,1)S(1)} %spread_blocks.4), channel_id=1, source_target_pairs={{0,4},{4,0},{8,12},{12,8},{16,20},{20,16},{24,28},{28,24},{1,5},{5... | collective-permute-start | bytes 2211848 | tf_op jit(solution)/shard_map/ppermute | solution.py:482
  144.7 17.5 %collective-permute-start.44 = (bf16[704,384]{1,0:T(8,128)(2,1)S(1)}, bf16[704,384]{1,0:T(8,128)(2,1)S(1)}, u32[]{:S(2)}, u32[]{:S(2)}) collective-permute-start(bf16[704,384]{1,0:T(8,128)(2,1)S(1)} %add_convert_fusion.1), channel_id=1, source_target_pairs={{8,16},{12,20},{16,8},{20,12},{9,17},{13,21},{17,9},{21,13},{10,18... | collective-permute-start | bytes 1622024 | tf_op jit(solution)/shard_map/ppermute | solution.py:482
  145.8 19.8 %collective-permute-start.24 = (bf16[704,384]{1,0:T(8,128)(2,1)S(1)}, bf16[704,384]{1,0:T(8,128)(2,1)S(1)}, u32[]{:S(2)}, u32[]{:S(2)}) collective-permute-start(bf16[704,384]{1,0:T(8,128)(2,1)S(1)} %add_convert_fusion.6), channel_id=1, source_target_pairs={{0,8},{4,12},{8,0},{12,4},{16,24},{20,28},{24,16},{28,20},{1,9},{5... | collective-permute-start | bytes 1622024 | tf_op jit(solution)/shard_map/ppermute | solution.py:482
  152.5 21.6 %collective-permute-start.42 = (bf16[704,384]{1,0:T(8,128)(2,1)S(1)}, bf16[704,384]{1,0:T(8,128)(2,1)S(1)}, u32[]{:S(2)}, u32[]{:S(2)}) collective-permute-start(bf16[704,384]{1,0:T(8,128)(2,1)S(1)} %add_convert_fusion.2), channel_id=1, source_target_pairs={{0,8},{4,12},{8,0},{12,4},{16,24},{20,28},{24,16},{28,20},{1,9},{5... | collective-permute-start | bytes 1622024 | tf_op jit(solution)/shard_map/ppermute | solution.py:482
  156.3 20.0 %collective-permute-start.31 = (bf16[2,176,384]{2,1,0:T(8,128)(2,1)S(1)}, bf16[2,176,384]{2,1,0:T(8,128)(2,1)S(1)}, u32[]{:S(2)}, u32[]{:S(2)}) collective-permute-start(bf16[2,176,384]{2,1,0:T(8,128)(2,1)S(1)} %get-tuple-element.70), channel_id=1, source_target_pairs={{0,1},{1,0},{2,3},{3,2},{4,5},{5,4},{6,7},{7,6},{8,9},{9,8},{10,11... | collective-permute-start | bytes 811016 | tf_op jit(solution)/shard_map/ppermute | solution.py:482
  160.7 15.6 %collective-permute-start.32 = (bf16[2,176,384]{2,1,0:T(8,128)(2,1)S(1)}, bf16[2,176,384]{2,1,0:T(8,128)(2,1)S(1)}, u32[]{:S(2)}, u32[]{:S(2)}) collective-permute-start(bf16[2,176,384]{2,1,0:T(8,128)(2,1)S(1)} %get-tuple-element.71), channel_id=1, source_target_pairs={{0,2},{1,3},{2,0},{3,1},{4,6},{5,7},{6,4},{7,5},{8,10},{9,11},{10,... | collective-permute-start | bytes 811016 | tf_op jit(solution)/shard_map/ppermute | solution.py:482
  162.2 14.1 %collective-permute-start.33 = (bf16[2,176,384]{2,1,0:T(8,128)(2,1)S(1)}, bf16[2,176,384]{2,1,0:T(8,128)(2,1)S(1)}, u32[]{:S(2)}, u32[]{:S(2)}) collective-permute-start(bf16[2,176,384]{2,1,0:T(8,128)(2,1)S(1)} %get-tuple-element.72), channel_id=1, source_target_pairs={{0,3},{1,2},{2,1},{3,0},{4,7},{5,6},{6,5},{7,4},{8,11},{9,10},{10,... | collective-permute-start | bytes 811016 | tf_op jit(solution)/shard_map/ppermute | solution.py:482
  165.5 18.6 %collective-permute-start.30 = (bf16[384,768]{1,0:T(8,128)(2,1)S(1)}, bf16[384,768]{1,0:T(8,128)(2,1)S(1)}, u32[]{:S(2)}, u32[]{:S(2)}) collective-permute-start(bf16[384,768]{1,0:T(8,128)(2,1)S(1)} %pad_maximum_fusion.5), channel_id=1, source_target_pairs={{0,1},{1,0},{2,3},{3,2},{4,5},{5,4},{6,7},{7,6},{8,9},{9,8},{10,11... | collective-permute-start | bytes 1769480 | tf_op jit(solution)/shard_map/ppermute | solution.py:482
  176.6 10.5 %collective-permute-start.27 = (bf16[352,384]{1,0:T(8,128)(2,1)S(1)}, bf16[352,384]{1,0:T(8,128)(2,1)S(1)}, u32[]{:S(2)}, u32[]{:S(2)}) collective-permute-start(bf16[352,384]{1,0:T(8,128)(2,1)S(1)} %get-tuple-element.112), channel_id=1, source_target_pairs={{0,2},{1,3},{2,0},{3,1},{4,6},{5,7},{6,4},{7,5},{8,10},{9,11},{10,... | collective-permute-start | bytes 811016 | tf_op jit(solution)/shard_map/ppermute | solution.py:482
  194.1 29.5 %collective-permute-start.59 = (f32[2,192,768]{2,1,0:T(8,128)S(1)}, f32[2,192,768]{2,1,0:T(8,128)S(1)}, u32[]{:S(2)}, u32[]{:S(2)}) collective-permute-start(f32[2,192,768]{2,1,0:T(8,128)S(1)} %bitcast.139), channel_id=1, source_target_pairs={{0,1},{1,0},{2,3},{3,2},{4,5},{5,4},{6,7},{7,6},{8,9},{9,8},{10,11... | collective-permute-start | bytes 3538952 | tf_op jit(solution)/shard_map/ppermute | solution.py:482
  197.5 12.5 %collective-permute-start.35 = (bf16[352,384]{1,0:T(8,128)(2,1)S(1)}, bf16[352,384]{1,0:T(8,128)(2,1)S(1)}, u32[]{:S(2)}, u32[]{:S(2)}) collective-permute-start(bf16[352,384]{1,0:T(8,128)(2,1)S(1)} %maximum_select_fusion.5), channel_id=1, source_target_pairs={{0,2},{1,3},{2,0},{3,1},{4,6},{5,7},{6,4},{7,5},{8,10},{9,11},{10,... | collective-permute-start | bytes 811016 | tf_op jit(solution)/shard_map/ppermute | solution.py:482
  204.9 17.5 %collective-permute-start.50 = (bf16[704,384]{1,0:T(8,128)(2,1)S(1)}, bf16[704,384]{1,0:T(8,128)(2,1)S(1)}, u32[]{:S(2)}, u32[]{:S(2)}) collective-permute-start(bf16[704,384]{1,0:T(8,128)(2,1)S(1)} %maximum_select_fusion.2.rest_1_.refs_19_), channel_id=1, source_target_pairs={{0,8},{4,12},{8,0},{12,4},{16,24},{20,28},{24,16},{28,20},{1,9},{5... | collective-permute-start | bytes 1622024 | tf_op jit(solution)/shard_map/ppermute | solution.py:482
  209.3 24.3 %collective-permute-start.49 = (bf16[704,384]{1,0:T(8,128)(2,1)S(1)}, bf16[704,384]{1,0:T(8,128)(2,1)S(1)}, u32[]{:S(2)}, u32[]{:S(2)}) collective-permute-start(bf16[704,384]{1,0:T(8,128)(2,1)S(1)} %maximum_select_fusion.2.rest_1_.refs_19_), channel_id=1, source_target_pairs={{8,16},{12,20},{16,8},{20,12},{9,17},{13,21},{17,9},{21,13},{10,18... | collective-permute-start | bytes 1622024 | tf_op jit(solution)/shard_map/ppermute | solution.py:482
  210.2 22.0 %collective-permute-start.37 = (bf16[704,384]{1,0:T(8,128)(2,1)S(1)}, bf16[704,384]{1,0:T(8,128)(2,1)S(1)}, u32[]{:S(2)}, u32[]{:S(2)}) collective-permute-start(bf16[704,384]{1,0:T(8,128)(2,1)S(1)} %maximum_select_fusion.1.rest_0_.refs_18_), channel_id=1, source_target_pairs={{0,8},{4,12},{8,0},{12,4},{16,24},{20,28},{24,16},{28,20},{1,9},{5... | collective-permute-start | bytes 1622024 | tf_op jit(solution)/shard_map/ppermute | solution.py:482
  216.3 20.4 %collective-permute-start.36 = (bf16[704,384]{1,0:T(8,128)(2,1)S(1)}, bf16[704,384]{1,0:T(8,128)(2,1)S(1)}, u32[]{:S(2)}, u32[]{:S(2)}) collective-permute-start(bf16[704,384]{1,0:T(8,128)(2,1)S(1)} %maximum_select_fusion.1.rest_0_.refs_18_), channel_id=1, source_target_pairs={{8,16},{12,20},{16,8},{20,12},{9,17},{13,21},{17,9},{21,13},{10,18... | collective-permute-start | bytes 1622024 | tf_op jit(solution)/shard_map/ppermute | solution.py:482
  222.4 15.1 %collective-permute-start.55 = (bf16[12,80,384]{2,1,0:T(8,128)(2,1)S(1)}, bf16[12,80,384]{2,1,0:T(8,128)(2,1)S(1)}, u32[]{:S(2)}, u32[]{:S(2)}) collective-permute-start(bf16[12,80,384]{2,1,0:T(8,128)(2,1)S(1)} %pick_bands.7), channel_id=1, source_target_pairs={{0,4},{4,0},{8,12},{12,8},{16,20},{20,16},{24,28},{28,24},{1,5},{5... | collective-permute-start | bytes 2211848 | tf_op jit(solution)/shard_map/ppermute | solution.py:482
  223.6 15.2 %collective-permute-start.51 = (bf16[704,384]{1,0:T(8,128)(2,1)S(1)}, bf16[704,384]{1,0:T(8,128)(2,1)S(1)}, u32[]{:S(2)}, u32[]{:S(2)}) collective-permute-start(bf16[704,384]{1,0:T(8,128)(2,1)S(1)} %collective-permute-done.50.rest_1_.refs_23_), channel_id=1, source_target_pairs={{8,16},{12,20},{16,8},{20,12},{9,17},{13,21},{17,9},{21,13},{10,18... | collective-permute-start | bytes 1622024 | tf_op jit(solution)/shard_map/ppermute | solution.py:482
  232.2 13.6 %collective-permute-start.60 = (f32[192,768]{1,0:T(8,128)S(1)}, f32[192,768]{1,0:T(8,128)S(1)}, u32[]{:S(2)}, u32[]{:S(2)}) collective-permute-start(f32[192,768]{1,0:T(8,128)S(1)} %slice_bitcast_fusion), channel_id=1, source_target_pairs={{0,2},{1,3},{2,0},{3,1},{4,6},{5,7},{6,4},{7,5},{8,10},{9,11},{10,... | collective-permute-start | bytes 1769480 | tf_op jit(solution)/shard_map/ppermute | solution.py:482
  233.6 17.1 %collective-permute-start.54 = (bf16[704,384]{1,0:T(8,128)(2,1)S(1)}, bf16[704,384]{1,0:T(8,128)(2,1)S(1)}, u32[]{:S(2)}, u32[]{:S(2)}) collective-permute-start(bf16[704,384]{1,0:T(8,128)(2,1)S(1)} %collective-permute-done.49), channel_id=1, source_target_pairs={{8,0},{12,4},{16,24},{20,28},{9,1},{13,5},{17,25},{21,29},{10,2},{... | collective-permute-start | bytes 1622024 | tf_op jit(solution)/shard_map/ppermute | solution.py:482
  236.8 15.2 %collective-permute-start.38 = (bf16[704,384]{1,0:T(8,128)(2,1)S(1)}, bf16[704,384]{1,0:T(8,128)(2,1)S(1)}, u32[]{:S(2)}, u32[]{:S(2)}) collective-permute-start(bf16[704,384]{1,0:T(8,128)(2,1)S(1)} %collective-permute-done.37.rest_0_.refs_22_), channel_id=1, source_target_pairs={{8,16},{12,20},{16,8},{20,12},{9,17},{13,21},{17,9},{21,13},{10,18... | collective-permute-start | bytes 1622024 | tf_op jit(solution)/shard_map/ppermute | solution.py:482
  237.5 24.8 %collective-permute-start.53 = (bf16[704,384]{1,0:T(8,128)(2,1)S(1)}, bf16[704,384]{1,0:T(8,128)(2,1)S(1)}, u32[]{:S(2)}, u32[]{:S(2)}) collective-permute-start(bf16[704,384]{1,0:T(8,128)(2,1)S(1)} %collective-permute-done.36), channel_id=1, source_target_pairs={{8,0},{12,4},{16,24},{20,28},{9,1},{13,5},{17,25},{21,29},{10,2},{... | collective-permute-start | bytes 1622024 | tf_op jit(solution)/shard_map/ppermute | solution.py:482
  238.8 34.8 %collective-permute-start.56 = (bf16[12,80,384]{2,1,0:T(8,128)(2,1)S(1)}, bf16[12,80,384]{2,1,0:T(8,128)(2,1)S(1)}, u32[]{:S(2)}, u32[]{:S(2)}) collective-permute-start(bf16[12,80,384]{2,1,0:T(8,128)(2,1)S(1)} %pick_bands.6), channel_id=1, source_target_pairs={{0,4},{4,0},{8,12},{12,8},{16,20},{20,16},{24,28},{28,24},{1,5},{5... | collective-permute-start | bytes 2211848 | tf_op jit(solution)/shard_map/ppermute | solution.py:482
  245.8 32.0 %collective-permute-start.52 = (bf16[704,384]{1,0:T(8,128)(2,1)S(1)}, bf16[704,384]{1,0:T(8,128)(2,1)S(1)}, u32[]{:S(2)}, u32[]{:S(2)}) collective-permute-start(bf16[704,384]{1,0:T(8,128)(2,1)S(1)} %collective-permute-done.51), channel_id=1, source_target_pairs={{8,0},{12,4},{16,24},{20,28},{9,1},{13,5},{17,25},{21,29},{10,2},{... | collective-permute-start | bytes 1622024 | tf_op jit(solution)/shard_map/ppermute | solution.py:482
  250.7 11.7 %collective-permute-start.61 = (f32[96,768]{1,0:T(8,128)S(1)}, f32[96,768]{1,0:T(8,128)S(1)}, u32[]{:S(2)}, u32[]{:S(2)}) collective-permute-start(f32[96,768]{1,0:T(8,128)S(1)} %constant_dynamic-slice_fusion.2), channel_id=1, source_target_pairs={{0,4},{4,0},{8,12},{12,8},{16,20},{20,16},{24,28},{28,24},{1,5},{5... | collective-permute-start | bytes 884744 | tf_op jit(solution)/shard_map/ppermute | solution.py:482
  262.5 12.6 %collective-permute-start.62 = (f32[48,768]{1,0:T(8,128)S(1)}, f32[48,768]{1,0:T(8,128)S(1)}, u32[]{:S(2)}, u32[]{:S(2)}) collective-permute-start(f32[48,768]{1,0:T(8,128)S(1)} %constant_dynamic-slice_fusion.1), channel_id=1, source_target_pairs={{0,16},{4,20},{8,24},{12,28},{16,0},{20,4},{24,8},{28,12},{1,17},{... | collective-permute-start | bytes 442376 | tf_op jit(solution)/shard_map/ppermute | solution.py:482
  272.3 15.8 %collective-permute-start.39 = (bf16[704,384]{1,0:T(8,128)(2,1)S(1)}, bf16[704,384]{1,0:T(8,128)(2,1)S(1)}, u32[]{:S(2)}, u32[]{:S(2)}) collective-permute-start(bf16[704,384]{1,0:T(8,128)(2,1)S(1)} %collective-permute-done.38), channel_id=1, source_target_pairs={{8,0},{12,4},{16,24},{20,28},{9,1},{13,5},{17,25},{21,29},{10,2},{... | collective-permute-start | bytes 1622024 | tf_op jit(solution)/shard_map/ppermute | solution.py:482
  273.6 28.4 %collective-permute-start.57 = (bf16[12,80,384]{2,1,0:T(8,128)(2,1)S(1)}, bf16[12,80,384]{2,1,0:T(8,128)(2,1)S(1)}, u32[]{:S(2)}, u32[]{:S(2)}) collective-permute-start(bf16[12,80,384]{2,1,0:T(8,128)(2,1)S(1)} %pick_bands.5), channel_id=1, source_target_pairs={{0,4},{4,0},{8,12},{12,8},{16,20},{20,16},{24,28},{28,24},{1,5},{5... | collective-permute-start | bytes 2211848 | tf_op jit(solution)/shard_map/ppermute | solution.py:482
  275.1 13.0 %collective-permute-start.63 = (f32[24,768]{1,0:T(8,128)S(1)}, f32[24,768]{1,0:T(8,128)S(1)}, u32[]{:S(2)}, u32[]{:S(2)}) collective-permute-start(f32[24,768]{1,0:T(8,128)S(1)} %constant_dynamic-slice_fusion), channel_id=1, source_target_pairs={{0,8},{4,12},{8,0},{12,4},{16,24},{20,28},{24,16},{28,20},{1,9},{5... | collective-permute-start | bytes 221192 | tf_op jit(solution)/shard_map/ppermute | solution.py:482
  300.4 22.4 %collective-permute-start.66 = (f32[96,768]{1,0:T(8,128)S(1)}, f32[96,768]{1,0:T(8,128)S(1)}, u32[]{:S(2)}, u32[]{:S(2)}) collective-permute-start(f32[96,768]{1,0:T(8,128)S(1)} %maximum_select_fusion.3), channel_id=1, source_target_pairs={{0,4},{4,0},{8,12},{12,8},{16,20},{20,16},{24,28},{28,24},{1,5},{5... | collective-permute-start | bytes 884744 | tf_op jit(solution)/shard_map/ppermute | solution.py:482
  302.0 21.7 %collective-permute-start.58 = (bf16[12,80,384]{2,1,0:T(8,128)(2,1)S(1)}, bf16[12,80,384]{2,1,0:T(8,128)(2,1)S(1)}, u32[]{:S(2)}, u32[]{:S(2)}) collective-permute-start(bf16[12,80,384]{2,1,0:T(8,128)(2,1)S(1)} %pick_bands.4), channel_id=1, source_target_pairs={{0,4},{4,0},{8,12},{12,8},{16,20},{20,16},{24,28},{28,24},{1,5},{5... | collective-permute-start | bytes 2211848 | tf_op jit(solution)/shard_map/ppermute | solution.py:482
  (27 other events, 169.8 us)
where the time goes:
time: 333 us
  waiting for transfers between devices  144 us (43%)
  starting transfers between devices  95.3 us (29%)
  Pallas kernels  71.7 us (22%)
  local copies, waits for them, and re-layouts  13.4 us (4%)
  other arithmetic  7.36 us (2%)
    ppermute x67, waiting for transfers between devices, hop(): return lax.ppermute(value, axis, pairs)  144 us
    ppermute x67, starting transfers between devices, hop(): return lax.ppermute(value, axis, pairs)  95.3 us
    pallas_call x18, Pallas kernels, call(): pl.pallas_call(body, out_shape=out_shape, in_specs=[smem] * n_scalars + [...  71.7 us
    unnamed x21, local copies, waits for them, and re-layouts  9.86 us
  transfers between devices with their start and end apart: 67, of which 30 were waited for; matrix products, arithmetic and copies ran while one was open for 4% of the time, Pallas kernels for 18%

commit v1 on v0

--- a/solution.py
+++ b/solution.py
@@ -199,7 +199,7 @@
         lax.fori_loop(0, rounds(count_ref[0], 4), group, 0)
 
     out = jax.ShapeDtypeStruct((slots // 2, band_rows, 2 * width), jnp.bfloat16)
-    return call(body, out, (count, block, where, weight, points), 3, 3, "spread_blocks")
+    return call(body, out, (count, block, where, weight, points), 3, 0.1, "spread_blocks")
 
 
 def render(count, block, place, where, other_count, other_place, weight, points, other, views, half_rows):
@@ -210,7 +210,7 @@
         count_ref, block_ref, place_ref, where_ref, other_count_ref, other_place_ref,
         weight_ref, points_ref, other_ref, *rest
     ):
-        outs, acc = rest[:-1], rest[-1]
+        out, acc = rest
         acc[...] = jnp.zeros_like(acc)
 
         def group(step, carry):
@@ -239,32 +239,30 @@
 
         lax.fori_loop(0, rounds(count_ref[0], GROUP), group, 0)
         lax.fori_loop(0, rounds(other_count_ref[0], 4), other_group, 0)
-        for u, out in enumerate(outs):
+        for u in range(views):
             first = acc[2 * u * half_rows : (2 * u + 1) * half_rows, :]
             second = acc[(2 * u + 1) * half_rows : (2 * u + 2) * half_rows, :]
-            out[...] = beside(first, second).astype(out.dtype)
-
-    image = jax.ShapeDtypeStruct((half_rows, 2 * width), jnp.bfloat16)
+            out[u * half_rows : (u + 1) * half_rows, :] = beside(first, second).astype(out.dtype)
+
+    images = jax.ShapeDtypeStruct((views * half_rows, 2 * width), jnp.bfloat16)
     args = (count, block, place, where, other_count, other_place, weight, points, other)
     scratch = [pltpu.VMEM((2 * views * half_rows + band_rows + 8, 256), jnp.float32)]
-    return call(body, [image] * views, args, 6, 5, "render_blocks", scratch)
-
-
-def unpack_images(image_refs, image, half_rows):
-    for u, ref in enumerate(image_refs):
-        first, second = apart(ref[...].astype(jnp.float32))
+    return call(body, images, args, 6, 5, "render_blocks", scratch)
+
+
+def unpack_images(images_ref, image, half_rows):
+    for u in range(images_ref.shape[0] // half_rows):
+        first, second = apart(images_ref[u * half_rows : (u + 1) * half_rows, :].astype(jnp.float32))
         image[2 * u * half_rows : (2 * u + 1) * half_rows, :] = first
         image[(2 * u + 1) * half_rows : (2 * u + 2) * half_rows, :] = second
 
 
-def pick(count, place, images, slots, band_rows):
-    half_rows, packed = images[0].shape
-    views = len(images)
-
-    def body(count_ref, place_ref, *rest):
-        image_refs, (out_ref, image) = rest[:views], rest[views:]
-        unpack_images(image_refs, image, half_rows)
-        image[2 * views * half_rows :, :] = jnp.zeros((band_rows + 8, 256), jnp.float32)
+def pick(count, place, images, slots, band_rows, half_rows):
+    pixels, packed = 2 * images.shape[0], images.shape[1]
+
+    def body(count_ref, place_ref, images_ref, out_ref, image):
+        unpack_images(images_ref, image, half_rows)
+        image[pixels:, :] = jnp.zeros((band_rows + 8, 256), jnp.float32)
 
         def group(step, carry):
             for t in range(2):
@@ -281,25 +279,24 @@
         lax.fori_loop(0, rounds(count_ref[0], 4), group, 0)
 
     out = jax.ShapeDtypeStruct((slots // 2, band_rows, packed), jnp.bfloat16)
-    scratch = [pltpu.VMEM((2 * views * half_rows + band_rows + 8, 256), jnp.float32)]
-    return call(body, out, (count, place) + tuple(images), 2, 4, "pick_bands", scratch)
-
-
-def pull(parts, where, old, blocks, last):
-    views = len(parts[0]["images"])
-    half_rows, packed = parts[0]["images"][0].shape
-    width = packed // 2
-    band_rows = parts[0]["weights"].shape[2]
+    scratch = [pltpu.VMEM((pixels + band_rows + 8, 256), jnp.float32)]
+    return call(body, out, (count, place, images), 2, 1, "pick_bands", scratch)
+
+
+def pull(jobs, where, old, blocks, half_rows, last):
+    band_rows = jobs[0]["weights"].shape[1]
+    pixels = max([2 * job["images"].shape[0] for job in jobs if "place" in job], default=0)
+    width = jobs[0]["width"]
     first = old is None
-    scalars = ("count", "block", "place", "other_count", "other_block")
-    tables, arrays = [where], []
-    for part in parts:
-        tables += [part[name] for name in scalars]
-        arrays += [part["weights"], part["bands"]] + list(part["images"])
+    tables, arrays, layout = [where], [], []
+    for job in jobs:
+        layout.append((len(tables), len(arrays), "place" in job))
+        tables += [job["count"], job["block"]] + ([job["place"]] if "place" in job else [])
+        arrays += [job["weights"], job["images"] if "place" in job else job["bands"]]
     arrays += [] if first else [old]
 
     def body(*refs):
-        where_ref, table_refs = refs[0], refs[1 : len(tables)]
+        where_ref = refs[0]
         array_refs = refs[len(tables) : len(tables) + len(arrays)]
         out_ref, image, acc = refs[len(tables) + len(arrays) :]
         if first:
@@ -307,10 +304,11 @@
         else:
             acc[0:blocks] = array_refs[-1][...]
 
-        for i in range(len(parts)):
-            count_ref, block_ref, place_ref, other_count_ref, other_block_ref = table_refs[5 * i : 5 * i + 5]
-            weight_ref, other_ref, *image_refs = array_refs[(2 + views) * i : (2 + views) * (i + 1)]
-            unpack_images(image_refs, image, half_rows)
+        for table, array, own in layout:
+            count_ref, block_ref, weight_ref = refs[table], refs[table + 1], array_refs[array]
+            place_ref, other_ref = refs[table + 2], array_refs[array + 1]
+            if own:
+                unpack_images(other_ref, image, half_rows)
 
             def group(step, carry):
                 terms = []
@@ -320,7 +318,7 @@
                     terms.append(
                         lax.dot_general(
                             image[rows_at(start, band_rows), 0:width].astype(jnp.bfloat16),
-                            shifted(weight_ref[0, where_ref[slot]], start).astype(jnp.bfloat16),
+                            shifted(weight_ref[where_ref[slot]], start).astype(jnp.bfloat16),
                             (((0,), (0,)), ((), ())),
                             preferred_element_type=jnp.float32,
                         )
@@ -333,7 +331,7 @@
                 terms = []
                 for t in range(2):
                     pair = 2 * step + t
-                    both = [weight_ref[1, where_ref[2 * pair + s]] for s in range(2)]
+                    both = [weight_ref[where_ref[2 * pair + s]] for s in range(2)]
                     terms.append(
                         lax.dot_general(
                             other_ref[pair],
@@ -344,25 +342,25 @@
                     )
                 for t in range(2):
                     pair = 2 * step + t
-                    acc[other_block_ref[2 * pair]] += terms[t][0:width, 0:BLOCK]
-                    acc[other_block_ref[2 * pair + 1]] += terms[t][width:, BLOCK:]
+                    acc[block_ref[2 * pair]] += terms[t][0:width, 0:BLOCK]
+                    acc[block_ref[2 * pair + 1]] += terms[t][width:, BLOCK:]
                 return carry
 
-            lax.fori_loop(0, rounds(count_ref[0], GROUP), group, 0)
-            lax.fori_loop(0, rounds(other_count_ref[0], 4), other_group, 0)
+            lax.fori_loop(0, rounds(count_ref[0], GROUP), group if own else other_group, 0)
         out_ref[...] = acc[0:blocks].astype(out_ref.dtype)
 
     out = jax.ShapeDtypeStruct((blocks, width, BLOCK), jnp.bfloat16 if last else jnp.float32)
     scratch = [
-        pltpu.VMEM((2 * views * half_rows + band_rows + 8, 256), jnp.float32),
+        pltpu.VMEM((pixels + band_rows + 8, 256), jnp.float32),
         pltpu.VMEM((blocks + 1, width, BLOCK), jnp.float32),
     ]
-    us = 3 + 5 * len(parts)
+    us = 1
     return call(body, out, tuple(tables + arrays), len(tables), us, "pull_blocks", scratch)
 
 
-def loss_kernel(u, teacher_width, side_ref, parts_ref, head_ref, teacher_ref, image_ref, grad_ref):
-    rows, packed = parts_ref.shape[1], parts_ref.shape[2]
+def loss_kernel(u, teacher_width, side_ref, head_ref, teacher_ref, *rest):
+    parts_refs, image_refs, grad_ref = rest[0:4], rest[-5:-1], rest[-1]
+    rows, packed = parts_refs[0].shape
     width = packed // 2
     lane = lax.broadcasted_iota(jnp.int32, (rows, packed), 1)
     head = head_ref[...]
@@ -375,7 +373,7 @@
             halves[1].append(jnp.where(lane < width, pltpu.roll(one, width, 1), two))
         return [jnp.concatenate(half, axis=1) for half in halves]
 
-    halves = halves_of([parts_ref[d] for d in range(4)])
+    halves = halves_of([ref[...] for ref in parts_refs])
     targets = halves_of([teacher_ref[side_ref[0] ^ g, u] for g in range(4)])
     rendered_all, grad_all, images = [], [], []
     for half in range(2):
@@ -388,37 +386,66 @@
         inner = jnp.sum(residual * normed, axis=1, keepdims=True) / teacher_width
         grad_proj = ((residual - normed * inner) / scale).astype(jnp.bfloat16)
         images.append(
-            lax.dot_general(
-                grad_proj, head, (((1,), (1,)), ((), ())), preferred_element_type=jnp.float32
-            )
+            lax.dot_general(grad_proj, head, (((1,), (1,)), ((), ())), preferred_element_type=jnp.float32)
         )
         rendered_all.append(rendered)
         grad_all.append(grad_proj)
     for pair in range(2):
         cols = slice(2 * pair * width, 2 * (pair + 1) * width)
         first, second = images[0][:, cols], images[1][:, cols]
-        image_ref[2 * pair] = jnp.where(lane < width, first, pltpu.roll(second, width, 1)).astype(
-            image_ref.dtype
-        )
-        image_ref[2 * pair + 1] = jnp.where(
-            lane < width, pltpu.roll(first, width, 1), second
-        ).astype(image_ref.dtype)
-    grad_ref[...] = lax.dot_general(
+        one = jnp.where(lane < width, first, pltpu.roll(second, width, 1))
+        two = jnp.where(lane < width, pltpu.roll(first, width, 1), second)
+        image_refs[2 * pair][...] = one.astype(jnp.bfloat16)
+        image_refs[2 * pair + 1][...] = two.astype(jnp.bfloat16)
+    grad = lax.dot_general(
         jnp.concatenate(rendered_all, axis=0),
         jnp.concatenate(grad_all, axis=0),
         (((0,), (0,)), ((), ())),
         preferred_element_type=jnp.float32,
     )
-
-
-def loss(u, side, parts, head, teacher):
+    grad_ref[...] = grad if len(rest) == 9 else grad + rest[4][...]
+
+
+def loss(u, side, parts, head, teacher, grad):
     teacher_width = head.shape[1]
-    outs = [
-        jax.ShapeDtypeStruct(parts.shape, jnp.bfloat16),
-        jax.ShapeDtypeStruct(head.shape, jnp.float32),
-    ]
+    outs = [jax.ShapeDtypeStruct(parts[0].shape, jnp.bfloat16)] * len(parts)
+    outs += [jax.ShapeDtypeStruct(head.shape, jnp.float32)]
     body = lambda *refs: loss_kernel(u, teacher_width, *refs)
-    return call(body, outs, (side, parts, head, teacher), 1, 3, "loss_rows")
+    args = (side, head, teacher) + tuple(parts) + (() if grad is None else (grad,))
+    *images, grad = call(body, outs, args, 1, 3, "loss_rows")
+    return images, grad
+
+
+def deal(side, terms, sides, half_rows):
+    rows = half_rows // sides
+    views = terms[0].shape[0] // half_rows
+
+    def body(side_ref, *refs):
+        for u in range(views):
+            for d in range(sides):
+                start = pl.multiple_of(u * half_rows + (side_ref[0] ^ d) * rows, 16)
+                value = refs[0][pl.ds(start, rows), :].astype(jnp.float32)
+                for ref in refs[1 : len(terms)]:
+                    value = value + ref[pl.ds(start, rows), :].astype(jnp.float32)
+                refs[len(terms) + u * sides + d][...] = value.astype(jnp.bfloat16)
+
+    out = jax.ShapeDtypeStruct((rows, terms[0].shape[1]), jnp.bfloat16)
+    parts = call(body, [out] * (views * sides), (side,) + tuple(terms), 1, 2, "deal_rows")
+    return [parts[u * sides : (u + 1) * sides] for u in range(views)]
+
+
+def gather(side, parts, half_rows):
+    views, sides = len(parts), len(parts[0])
+    rows, lanes = parts[0][0].shape
+
+    def body(side_ref, *refs):
+        for u in range(views):
+            for d in range(sides):
+                start = pl.multiple_of(u * half_rows + (side_ref[0] ^ d) * rows, 16)
+                refs[-1][pl.ds(start, rows), :] = refs[u * sides + d][...]
+
+    out = jax.ShapeDtypeStruct((views * half_rows, lanes), jnp.bfloat16)
+    return call(body, out, (side,) + tuple(sum(parts, [])), 1, 2, "gather_rows")
 
 
 def turn_teacher(side, teacher, sides, padded):
@@ -526,25 +553,31 @@
     turn = (turn % 2) * 2 + turn // 2
     where_of = turn * quarter + slot_ids % quarter
 
-    weights, hops = {}, None
+    weights, kept, given, arrived = {}, {}, {}, {}
+    hops = []
     for j in (3, 2, 1, 0):
         got = []
         for k in (2 * j + 1, 2 * j):
-            value = packed[k] if hops is None else after(packed[k], hops)
+            value = packed[k]
             got.append(swap(value, "view", k) if k else value)
-        got = hops = jnp.stack(got[::-1])
+        got = jnp.stack(got[::-1])
+        if j >= 2:
+            hops.append(got)
+        else:
+            got = after(got, given[3])
         got = jnp.concatenate([got, swap(got, "feat", 2)], axis=1)
         weights[j] = jnp.concatenate([got, swap(got, "feat", 1)], axis=1)
-
-    kept, arrived = {}, None
+        k = 2 * j + 1
+        given[j] = spread(counts[k : k + 1], block_of[k], where_of, weights[j][1], points)
+        arrived[j] = given[j]
+    arrived[3] = after(swap(given[3], "view", 1), given[2], weights[1], weights[0])
     for j in (3, 2, 1, 0):
-        k = 2 * j + 1
-        given = spread(counts[k : k + 1], block_of[k], where_of, weights[j][1], points)
-        arrived = swap(given if arrived is None else after(given, arrived), "view", 1)
+        if j < 3:
+            arrived[j] = swap(after(given[j], arrived[j + 1]), "view", 1)
         k = 2 * j
         kept[j] = render(
-            counts[k : k + 1], block_of[k], place_of[k], where_of,
-            pair_counts[j : j + 1], pair_places[j], weights[j][0], points, arrived, view_count, half_rows,
+            counts[k : k + 1], block_of[k], place_of[k], where_of, pair_counts[j : j + 1], pair_places[j],
+            weights[j][0], points, arrived[j], view_count, half_rows,
         )
 
     side_id = side.reshape(1).astype(ints)
@@ -555,80 +588,66 @@
     head = jnp.concatenate([head_weight, swap(head_weight, "feat", 2)], axis=0)
     head = jnp.concatenate([head, swap(head, "feat", 1)], axis=0)
 
-    rendered = []
+    far = along(kept[3], [(0, 1), (3, 2)])
+    mid = total(kept[2], far)
+    inward = along(mid, [(0, 1), (3, 2)])
+    between = along(mid, [(1, 2), (2, 1)])
+    near = along(total(kept[1], between), [(0, 1), (1, 0), (2, 3), (3, 2)])
+    centre = along(total(kept[3], inward), [(1, 2), (2, 1)])
+
+    parts = deal(side_id, (kept[0], near, centre), sides, half_rows)
+    parts = [[swap(of[d], "feat", d) if d else of[d] for d in (0, 2, 1, 3)] for of in parts]
+    back, grad = [], None
     for u in range(view_count):
-        far = along(kept[3][u], [(0, 1), (3, 2)])
-        mid = total(kept[2][u], far)
-        inward = along(mid, [(0, 1), (3, 2)])
-        between = along(mid, [(1, 2), (2, 1)])
-        near = along(total(kept[1][u], between), [(0, 1), (1, 0), (2, 3), (3, 2)])
-        centre = along(total(kept[3][u], inward), [(1, 2), (2, 1)])
-        rendered.append(total(kept[0][u], near, centre))
-
-    grads, images = [], []
-    side_rows, seventh = half_rows // 2, half_rows // sides
-    for u in range(view_count):
-        whole = rendered[u]
-        mine = lax.dynamic_slice_in_dim(whole, across * side_rows, side_rows, 0)
-        other = lax.dynamic_slice_in_dim(whole, (1 - across) * side_rows, side_rows, 0)
-        both = jnp.stack([mine, swap(other, "feat", 2)])
-        mine = lax.dynamic_slice_in_dim(both, core * seventh, seventh, 1)
-        other = lax.dynamic_slice_in_dim(both, (1 - core) * seventh, seventh, 1)
-        parts = jnp.concatenate([mine, swap(other, "feat", 1)], axis=0)
-        image, grad = loss(u, side_id, parts, head, target)
-        grads.append(grad)
-        back = swap(image[2:4], "feat", 1)
-        rows = [in_order((core, image[i]), back[i]) for i in range(2)]
-        images.append(in_order((across, rows[0]), swap(rows[1], "feat", 2)))
+        images, grad = loss(u, side_id, parts[u], head, target, grad)
+        images = [swap(image, "feat", d) if d else image for d, image in zip((0, 2, 1, 3), images)]
+        back.append([images[i] for i in (0, 2, 1, 3)])
+    own = gather(side_id, back, half_rows)
 
     middle = (line == 1) | (line == 2)
-    chunks = {j: [] for j in range(4)}
-    marks = []
-    for u in range(view_count):
-        own = images[u]
-        near = along(own, [(0, 1), (1, 0), (2, 3), (3, 2)])
-        centre = along(own, [(1, 2), (2, 1)])
-        out_near = along(centre, [(1, 0), (2, 3)])
-        cross = along(near, [(1, 2), (2, 1)])
-        out_far = along(cross, [(1, 0), (2, 3)])
-        marks.append((near, cross, out_far))
-        for j, value in enumerate(
-            (own, near, jnp.where(middle, cross, out_near), jnp.where(middle, centre, out_far))
-        ):
-            chunks[j].append(value)
-    parts, bands = [], None
+    near = along(own, [(0, 1), (1, 0), (2, 3), (3, 2)])
+    centre = along(own, [(1, 2), (2, 1)])
+    out_near = along(centre, [(1, 0), (2, 3)])
+    cross = along(near, [(1, 2), (2, 1)])
+    out_far = along(cross, [(1, 0), (2, 3)])
+    chunks = [own, near, jnp.where(middle, cross, out_near), jnp.where(middle, centre, out_far)]
+    jobs, marks, bands, sums = {}, [], None, None
     for j in range(4):
-        bands = pick(pair_counts[j : j + 1], pair_places[j], chunks[j], slots, aligned)
-        bands = swap(bands if not parts else after(bands, parts[-1]["bands"]), "view", 1)
+        if j >= 2:
+            ready = [jobs[k] for k in ((0, 1, 2), (3, 4))[j - 2]]
+            sums = pull(ready, after(where_of, picked), sums, blocks, half_rows, False)
+            if j == 3:
+                chunks[j] = after(chunks[j], sums)
+        picked = pick(pair_counts[j : j + 1], pair_places[j], chunks[j], slots, aligned, half_rows)
+        marks.append(picked)
+        bands = swap(picked if bands is None else after(picked, bands), "view", 1)
         own, other = 2 * j, 2 * j + 1
-        parts.append(
-            dict(
-                count=counts[own : own + 1], block=pull_of[own], place=place_of[own],
-                other_count=counts[other : other + 1], other_block=pull_of[other],
-                weights=weights[j], images=chunks[j], bands=bands,
-            )
+        jobs[own] = dict(
+            count=counts[own : own + 1], block=pull_of[own], place=place_of[own],
+            weights=weights[j][0], images=chunks[j], width=width,
         )
-    early = pull(parts[:3], where_of, None, blocks, False)
-    grad_points = pull(parts[3:], where_of, early, blocks, True)
-
-    grad = grads[0]
-    for more in grads[1:]:
-        grad = grad + more
-    grad = grad.reshape(2, 2, width, grad.shape[1])
+        jobs[other] = dict(
+            count=counts[other : other + 1], block=pull_of[other],
+            weights=weights[j][1], bands=bands, width=width,
+        )
+    sums = pull([jobs[5], jobs[6]], after(where_of, picked), sums, blocks, half_rows, False)
+    grad_points = pull([jobs[7]], where_of, sums, blocks, half_rows, True)
+
+    grad = after(grad, chunks[0]).reshape(2, 2, width, grad.shape[1])
     grad = grad[0] + swap(grad[1], "feat", 1)
-    grad = grad[0] + swap(grad[1], "feat", 2)
-    marks = [marks[u][i] for i in range(3) for u in range(view_count)]
-    bits = [(1, me % 2), (4, me // 4), (2, line % 2)]
-    for (k, bit), mark in zip(bits, marks):
-        rows = grad.shape[0] // 2
-        grad = after(grad, mark)
-        mine = lax.dynamic_slice_in_dim(grad, bit * rows, rows, 0)
-        other = lax.dynamic_slice_in_dim(grad, (1 - bit) * rows, rows, 0)
-        grad = mine + swap(other, "view", k)
+    grad = grad[0] + after(swap(grad[1], "feat", 2), near)
+    rows = width // 2
+    low = me % 2
+    mine = lax.dynamic_slice_in_dim(grad, low * rows, rows, 0)
+    other = lax.dynamic_slice_in_dim(grad, (1 - low) * rows, rows, 0)
+    grad = mine + after(swap(other, "view", 1), marks[2])
+    sent = grad.astype(jnp.bfloat16)
+    grad = grad + after(swap(sent, "view", 2), marks[3]).astype(jnp.float32)
+    sent = grad.astype(jnp.bfloat16)
+    grad = grad + after(swap(sent, "view", 4), sums).astype(jnp.float32)
     grad = grad / (view_count * peers * GRID)
-    for (k, bit), mark in zip(bits[::-1], marks[3:]):
-        grad = after(grad, mark)
-        grad = in_order((bit, grad), swap(grad, "view", k))
+    far = swap(grad.astype(jnp.bfloat16), "view", 1).astype(jnp.float32)
+    grad = in_order((low, grad), far)
     return (grad_points, grad)
 
 

time: 333 us -> 302 us (0.907)
  waiting for transfers between devices: 144 us -> 114 us
  starting transfers between devices: 95.3 us -> 77.3 us
  other arithmetic: 7.36 us -> 15.3 us
  Pallas kernels: 71.7 us -> 77.9 us
    ppermute x67 -> x59, waiting for transfers between devices: 144 us -> 114 us  [hop(): return lax.ppermute(value, axis, pairs)]
    ppermute x67 -> x59, starting transfers between devices: 95.3 us -> 77.3 us  [hop(): return lax.ppermute(value, axis, pairs)]
    pallas_call x18 -> x22, Pallas kernels: 71.7 us -> 77.9 us  [call(): pl.pallas_call(body, out_shape=out_shape, in_specs=[smem] * n_scalars + [...]
    convert_element_type x7 -> x3, other arithmetic: 1.33 us -> 6.5 us  [total(): return acc.astype(jnp.bfloat16)]
    unnamed x21 -> x29, local copies, waits for them, and re-layouts: 9.86 us -> 8.44 us
  transfers between devices with their start and end apart: 67 -> 59, of which waited for: 30 -> 24; matrix products, arithmetic and copies ran while one was open for 4% -> 7% of each run, Pallas kernels for 18% -> 22%
where the time goes in v1:
time: 302 us; the launch traced here: 300 us
  waiting for transfers between devices  114 us (38%)
  Pallas kernels  77.9 us (26%)
  starting transfers between devices  77.3 us (26%)
  other arithmetic  15.3 us (5%)
  local copies, waits for them, and re-layouts  13.6 us (5%)
    ppermute x59, waiting for transfers between devices, hop(): return lax.ppermute(value, axis, pairs)  114 us
    pallas_call x22, Pallas kernels, call(): pl.pallas_call(body, out_shape=out_shape, in_specs=[smem] * n_scalars + [...  77.9 us
    ppermute x59, starting transfers between devices, hop(): return lax.ppermute(value, axis, pairs)  77.3 us
    unnamed x29, local copies, waits for them, and re-layouts  8.44 us
    convert_element_type x3, other arithmetic, total(): return acc.astype(jnp.bfloat16)  6.5 us
  transfers between devices with their start and end apart: 59, of which 24 were waited for; matrix products, arithmetic and copies ran while one was open for 7% of the time, Pallas kernels for 22%

profile of v1, /device:TPU:0, one launch (start us, length us, event | category | flops | bytes accessed | tf_op | source)
XLA Modules:
  0.0 299.7 jit_solution(17844412166558581228)
XLA Ops:
  3.3 4.1 %collective-permute-start = (s32[1,4,128]{2,1,0:T(4,128)S(1)}, s32[1,4,128]{2,1,0:T(4,128)S(1)}, u32[]{:S(2)}, u32[]{:S(2)}) collective-permute-start(s32[1,4,128]{2,1,0:T(4,128)S(1)} %add_bitcast_fusion), channel_id=1, source_target_pairs={{0,16},{4,20},{8,24},{12,28},{16,0},{20,4},{24,8},{28,12},{1,17},{... | collective-permute-start | bytes 6152 | tf_op jit(solution)/shard_map/ppermute | solution.py:509
  8.0 3.3 %copy.22 = bf16[2,64,74,128]{3,2,1,0:T(8,128)(2,1)S(1)} copy(bf16[2,64,74,128]{3,1,2,0:T(8,128)(2,1)} %param.10) | data formatting | bytes 4849664 | tf_op args[3]
  14.1 4.3 %collective-permute-start.4 = (bf16[6,80,128]{2,1,0:T(8,128)(2,1)S(1)}, bf16[6,80,128]{2,1,0:T(8,128)(2,1)S(1)}, u32[]{:S(2)}, u32[]{:S(2)}) collective-permute-start(bf16[6,80,128]{2,1,0:T(8,128)(2,1)S(1)} %get-tuple-element.53), channel_id=1, source_target_pairs={{0,28},{4,24},{8,20},{12,16},{16,12},{20,8},{24,4},{28,0},{1,29},{... | collective-permute-start | bytes 368648 | tf_op jit(solution)/shard_map/ppermute | solution.py:509
  20.5 4.6 %collective-permute-done.2 = s32[4,4,128]{2,1,0:T(4,128)S(1)} collective-permute-done((s32[4,4,128]{2,1,0:T(4,128)S(1)}, s32[4,4,128]{2,1,0:T(4,128)S(1)}, u32[]{:S(2)}, u32[]{:S(2)}) %collective-permute-start.2) | collective-permute-done | bytes 8224 | tf_op jit(solution)/shard_map/ppermute | solution.py:509
  26.3 2.9 collective-permute-start.20
  30.8 3.5 %collective-permute-done.19 = bf16[6,80,128]{2,1,0:T(8,128)(2,1)S(1)} collective-permute-done((bf16[6,80,128]{2,1,0:T(8,128)(2,1)S(1)}, bf16[6,80,128]{2,1,0:T(8,128)(2,1)S(1)}, u32[]{:S(2)}, u32[]{:S(2)}) %collective-permute-start.19) | collective-permute-done | bytes 122912 | tf_op jit(solution)/shard_map/ppermute | solution.py:509
  34.3 3.1 %collective-permute-done.20 = bf16[6,80,128]{2,1,0:T(8,128)(2,1)S(1)} collective-permute-done((bf16[6,80,128]{2,1,0:T(8,128)(2,1)S(1)}, bf16[6,80,128]{2,1,0:T(8,128)(2,1)S(1)}, u32[]{:S(2)}, u32[]{:S(2)}) %collective-permute-start.20) | collective-permute-done | bytes 122912 | tf_op jit(solution)/shard_map/ppermute | solution.py:509
  40.5 4.2 %collective-permute-done.21 = bf16[2,6,80,128]{3,2,1,0:T(8,128)(2,1)S(1)} collective-permute-done((bf16[2,6,80,128]{3,2,1,0:T(8,128)(2,1)S(1)}, bf16[2,6,80,128]{3,2,1,0:T(8,128)(2,1)S(1)}, u32[]{:S(2)}, u32[]{:S(2)}) %collective-permute-start.21) | collective-permute-done | bytes 245792 | tf_op jit(solution)/shard_map/ppermute | solution.py:509
  46.9 1.9 spread_blocks.4
  52.0 6.6 %collective-permute-done.8 = bf16[2,6,80,128]{3,2,1,0:T(8,128)(2,1)S(1)} collective-permute-done((bf16[2,6,80,128]{3,2,1,0:T(8,128)(2,1)S(1)}, bf16[2,6,80,128]{3,2,1,0:T(8,128)(2,1)S(1)}, u32[]{:S(2)}, u32[]{:S(2)}) %collective-permute-start.8) | collective-permute-done | bytes 245792 | tf_op jit(solution)/shard_map/ppermute | solution.py:509
  58.7 4.4 %collective-permute-done.17 = bf16[2,6,80,128]{3,2,1,0:T(8,128)(2,1)S(1)} collective-permute-done((bf16[2,6,80,128]{3,2,1,0:T(8,128)(2,1)S(1)}, bf16[2,6,80,128]{3,2,1,0:T(8,128)(2,1)S(1)}, u32[]{:S(2)}, u32[]{:S(2)}) %collective-permute-start.17) | collective-permute-done | bytes 245792 | tf_op jit(solution)/shard_map/ppermute | solution.py:509
  63.3 1.9 spread_blocks.7
  65.5 2.3 collective-permute-done.23.other_ref
  68.7 3.9 %render_blocks.7 = bf16[1408,384]{1,0:T(8,128)(2,1)S(1)} custom-call(s32[1]{0:T(128)} %get-tuple-element.155.count_ref.refs_3_, s32[24]{0:T(128)S(1)} %get-tuple-element.136.block_ref, s32[24]{0:T(128)S(1)} %get-tuple-element.166.place_ref.refs_5_, s32[24]{0:T(128)S(1)} %fusion.9.where_ref.refs_0_, s32[1]{0:T(128)} %get-tuple-element.153.other_count_ref.count_ref, ...), custom_call_target="tpu_custom_call" | custom-call | flops 5000000000 | bytes 10000000 | tf_op jit(solution)/shard_map/render_blocks/pallas_call | solution.py:121
  72.5 2.8 collective-permute-start.27
  75.5 1.9 spread_blocks.6
  77.4 8.4 %collective-permute-done.24.other_ref = bf16[12,80,384]{2,1,0:T(8,128)(2,1)S(1)} collective-permute-done((bf16[12,80,384]{2,1,0:T(8,128)(2,1)S(1)}, bf16[12,80,384]{2,1,0:T(8,128)(2,1)S(1)}, u32[]{:S(2)}, u32[]{:S(2)}) %collective-permute-start.24) | collective-permute-done | bytes 737312 | tf_op jit(solution)/shard_map/ppermute | solution.py:509
  86.7 3.8 %render_blocks.6 = bf16[1408,384]{1,0:T(8,128)(2,1)S(1)} custom-call(s32[1]{0:T(128)} %get-tuple-element.156.count_ref.refs_3_, s32[24]{0:T(128)S(1)} %get-tuple-element.137.block_ref, s32[24]{0:T(128)S(1)} %get-tuple-element.165.place_ref.refs_5_, s32[24]{0:T(128)S(1)} %fusion.9.where_ref.refs_0_, s32[1]{0:T(128)} %get-tuple-element.151.other_count_ref.count_ref, ...), custom_call_target="tpu_custom_call" | custom-call | flops 5000000000 | bytes 10000000 | tf_op jit(solution)/shard_map/render_blocks/pallas_call | solution.py:121
  90.6 6.4 %collective-permute-done.27 = bf16[1408,384]{1,0:T(8,128)(2,1)} collective-permute-done((bf16[1408,384]{1,0:T(8,128)(2,1)S(1)}, bf16[1408,384]{1,0:T(8,128)(2,1)}, u32[]{:S(2)}, u32[]{:S(2)}) %collective-permute-start.27) | collective-permute-done | bytes 1081376 | tf_op jit(solution)/shard_map/ppermute | solution.py:509
  97.0 2.5 add_convert_fusion.2
  99.5 5.5 %collective-permute-start.30 = (bf16[1408,384]{1,0:T(8,128)(2,1)}, bf16[1408,384]{1,0:T(8,128)(2,1)}, u32[]{:S(2)}, u32[]{:S(2)}) collective-permute-start(bf16[1408,384]{1,0:T(8,128)(2,1)} %add_convert_fusion.2), channel_id=1, source_target_pairs={{0,8},{4,12},{24,16},{28,20},{1,9},{5,13},{25,17},{29,21},{2,10},{... | collective-permute-start | bytes 3244040 | tf_op jit(solution)/shard_map/ppermute | solution.py:509
  109.3 1.9 spread_blocks.5
  112.5 3.5 %render_blocks.5 = bf16[1408,384]{1,0:T(8,128)(2,1)S(1)} custom-call(s32[1]{0:T(128)} %get-tuple-element.154.count_ref.refs_6_, s32[24]{0:T(128)S(1)} %get-tuple-element.135.block_ref, s32[24]{0:T(128)S(1)} %get-tuple-element.167.place_ref.refs_8_, s32[24]{0:T(128)S(1)} %fusion.9.where_ref.refs_0_, s32[1]{0:T(128)} %get-tuple-element.150.other_count_ref.count_ref, ...), custom_call_target="tpu_custom_call" | custom-call | flops 5000000000 | bytes 10000000 | tf_op jit(solution)/shard_map/render_blocks/pallas_call | solution.py:121
  116.0 10.0 %collective-permute-done.30 = bf16[1408,384]{1,0:T(8,128)(2,1)} collective-permute-done((bf16[1408,384]{1,0:T(8,128)(2,1)}, bf16[1408,384]{1,0:T(8,128)(2,1)}, u32[]{:S(2)}, u32[]{:S(2)}) %collective-permute-start.30) | collective-permute-done | bytes 1081376 | tf_op jit(solution)/shard_map/ppermute | solution.py:509
  128.6 2.5 add_convert_fusion.1
  131.1 5.4 %collective-permute-start.29 = (bf16[1408,384]{1,0:T(8,128)(2,1)}, bf16[1408,384]{1,0:T(8,128)(2,1)S(1)}, u32[]{:S(2)}, u32[]{:S(2)}) collective-permute-start(bf16[1408,384]{1,0:T(8,128)(2,1)} %add_convert_fusion.1), channel_id=1, source_target_pairs={{0,8},{4,12},{8,0},{12,4},{16,24},{20,28},{24,16},{28,20},{1,9},{5... | collective-permute-start | bytes 3244040 | tf_op jit(solution)/shard_map/ppermute | solution.py:509
  138.1 7.2 %collective-permute-done.14 = bf16[2,176,384]{2,1,0:T(8,128)(2,1)S(1)} collective-permute-done((bf16[2,176,384]{2,1,0:T(8,128)(2,1)S(1)}, bf16[2,176,384]{2,1,0:T(8,128)(2,1)S(1)}, u32[]{:S(2)}, u32[]{:S(2)}) %collective-permute-start.14) | collective-permute-done | bytes 270368 | tf_op jit(solution)/shard_map/ppermute | solution.py:509
  146.5 5.2 %collective-permute-done.10 = bf16[192,768]{1,0:T(8,128)(2,1)S(1)} collective-permute-done((bf16[192,768]{1,0:T(8,128)(2,1)S(1)}, bf16[192,768]{1,0:T(8,128)(2,1)S(1)}, u32[]{:S(2)}, u32[]{:S(2)}) %collective-permute-start.10) | collective-permute-done | bytes 294944 | tf_op jit(solution)/shard_map/ppermute | solution.py:509
  152.6 3.9 %render_blocks.4.refs_0_ = bf16[1408,384]{1,0:T(8,128)(2,1)S(1)} custom-call(s32[1]{0:T(128)} %get-tuple-element.160.count_ref.refs_1_, s32[24]{0:T(128)S(1)} %get-tuple-element.141.block_ref, s32[24]{0:T(128)S(1)} %get-tuple-element.164.place_ref.refs_3_, s32[24]{0:T(128)S(1)} %fusion.9.where_ref.refs_0_, s32[1]{0:T(128)} %get-tuple-element.152.other_count_ref.count_ref, ...), custom_call_target="tpu_custom_call" | custom-call | flops 5000000000 | bytes 10000000 | tf_op jit(solution)/shard_map/render_blocks/pallas_call | solution.py:121
  164.1 2.8 collective-permute-done.34.refs_6_
  166.9 2.8 loss_rows.2
  171.7 4.4 %loss_rows.3 = (bf16[176,384]{1,0:T(8,128)(2,1)S(1)}, bf16[176,384]{1,0:T(8,128)(2,1)S(1)}, bf16[176,384]{1,0:T(8,128)(2,1)S(1)}, bf16[176,384]{1,0:T(8,128)(2,1)S(1)}, f32[768,768]{1,0:T(8,128)S(1)}) custom-call(s32[1]{0:T(128)} %bitcast.18.side_ref.refs_0_, bf16[768,768]{1,0:T(8,128)(2,1)S(1)} %constant_dynamic-update-slice_fusion.3.refs_1_, ...), custom_call_target="tpu_custom_call" | custom-call | flops 3000000000 | bytes 6000000 | tf_op jit(solution)/shard_map/loss_rows/pallas_call | solution.py:121
  180.1 2.8 collective-permute-done.42.refs_6_
  183.0 1.9 collective-permute-done.43.refs_7_
  184.8 3.9 %collective-permute-done.36.refs_2_ = bf16[176,384]{1,0:T(8,128)(2,1)S(1)} collective-permute-done((bf16[176,384]{1,0:T(8,128)(2,1)S(1)}, bf16[176,384]{1,0:T(8,128)(2,1)S(1)}, u32[]{:S(2)}, u32[]{:S(2)}) %collective-permute-start.36) | collective-permute-done | bytes 135200 | tf_op jit(solution)/shard_map/ppermute | solution.py:509
  194.4 2.8 pick_bands.6
  198.1 18.9 %collective-permute-done.45.images_ref.refs_14_ = bf16[1408,384]{1,0:T(8,128)(2,1)} collective-permute-done((bf16[1408,384]{1,0:T(8,128)(2,1)S(1)}, bf16[1408,384]{1,0:T(8,128)(2,1)}, u32[]{:S(2)}, u32[]{:S(2)}) %collective-permute-start.45) | collective-permute-done | bytes 1081376 | tf_op jit(solution)/shard_map/ppermute | solution.py:509
  223.4 2.6 pick_bands.5
  227.2 10.5 %pull_blocks.4.refs_10_ = f32[64,192,128]{2,1,0:T(8,128)} custom-call(s32[24]{0:T(128)S(1)} %fusion.9.where_ref.refs_0_, s32[1]{0:T(128)} %get-tuple-element.160.count_ref.refs_1_, s32[24]{0:T(128)S(1)} %get-tuple-element.127.refs_2_, s32[24]{0:T(128)S(1)} %get-tuple-element.164.place_ref.refs_3_, s32[1]{0:T(128)} %get-tuple-element.159.count_ref.refs_4_, ...), custom_call_target="tpu_custom_call" | custom-call | flops 1000000000 | bytes 2000000 | tf_op jit(solution)/shard_map/pull_blocks/pallas_call | solution.py:121
  241.5 4.4 %collective-permute-done.48 = bf16[1408,384]{1,0:T(8,128)(2,1)} collective-permute-done((bf16[1408,384]{1,0:T(8,128)(2,1)}, bf16[1408,384]{1,0:T(8,128)(2,1)}, u32[]{:S(2)}, u32[]{:S(2)}) %collective-permute-start.48) | collective-permute-done | bytes 1081376 | tf_op jit(solution)/shard_map/ppermute | solution.py:509
  247.2 2.1 pick_bands.4
  250.2 6.2 %collective-permute-start.56 = (bf16[96,768]{1,0:T(8,128)(2,1)S(1)}, bf16[96,768]{1,0:T(8,128)(2,1)S(1)}, u32[]{:S(2)}, u32[]{:S(2)}) collective-permute-start(bf16[96,768]{1,0:T(8,128)(2,1)S(1)} %get-tuple-element.106), channel_id=1, source_target_pairs={{0,8},{4,12},{8,0},{12,4},{16,24},{20,28},{24,16},{28,20},{1,9},{5... | collective-permute-start | bytes 442376 | tf_op jit(solution)/shard_map/ppermute | solution.py:509
  256.5 9.6 %pull_blocks.5.refs_10_ = f32[64,192,128]{2,1,0:T(8,128)} custom-call(s32[24]{0:T(128)S(1)} %fusion.9.where_ref.refs_0_, s32[1]{0:T(128)} %get-tuple-element.158.count_ref.refs_1_, s32[24]{0:T(128)S(1)} %get-tuple-element.129.refs_2_, s32[1]{0:T(128)} %get-tuple-element.156.count_ref.refs_3_, s32[24]{0:T(128)S(1)} %get-tuple-element.128.refs_4_, ...), custom_call_target="tpu_custom_call" | custom-call | flops 1000000000 | bytes 2000000 | tf_op jit(solution)/shard_map/pull_blocks/pallas_call | solution.py:121
  266.1 5.2 %collective-permute-done.47 = bf16[1408,384]{1,0:T(8,128)(2,1)S(1)} collective-permute-done((bf16[1408,384]{1,0:T(8,128)(2,1)}, bf16[1408,384]{1,0:T(8,128)(2,1)S(1)}, u32[]{:S(2)}, u32[]{:S(2)}) %collective-permute-start.47) | collective-permute-done | bytes 1081376 | tf_op jit(solution)/shard_map/ppermute | solution.py:509
  271.5 2.0 pick_bands.7
  276.1 9.6 %pull_blocks.6.refs_5_ = f32[64,192,128]{2,1,0:T(8,128)} custom-call(s32[24]{0:T(128)S(1)} %fusion.9.where_ref.refs_0_, s32[1]{0:T(128)} %get-tuple-element.157.count_ref.refs_1_, s32[24]{0:T(128)S(1)} %get-tuple-element.124.refs_2_, s32[1]{0:T(128)} %get-tuple-element.155.count_ref.refs_3_, s32[24]{0:T(128)S(1)} %get-tuple-element.123.refs_4_, ...), custom_call_target="tpu_custom_call" | custom-call | flops 1000000000 | bytes 2000000 | tf_op jit(solution)/shard_map/pull_blocks/pallas_call | solution.py:121
  287.6 4.5 %collective-permute-done.58 = bf16[96,768]{1,0:T(8,128)(2,1)S(1)} collective-permute-done((bf16[96,768]{1,0:T(8,128)(2,1)S(1)}, bf16[96,768]{1,0:T(8,128)(2,1)S(1)}, u32[]{:S(2)}, u32[]{:S(2)}) %collective-permute-start.58) | collective-permute-done | bytes 147488 | tf_op jit(solution)/shard_map/ppermute | solution.py:509
  293.0 6.7 %pull_blocks.7 = bf16[64,192,128]{2,1,0:T(8,128)(2,1)} custom-call(s32[24]{0:T(128)S(1)} %fusion.9.where_ref.refs_0_, s32[1]{0:T(128)} %get-tuple-element.161.count_ref.refs_1_, s32[24]{0:T(128)S(1)} %get-tuple-element.130.refs_2_, bf16[24,80,128]{2,1,0:T(8,128)(2,1)S(1)} %get-tuple-element.115.weight_ref.refs_3_, ...), custom_call_target="tpu_custom_call" | custom-call | flops 1000000000 | bytes 2000000 | tf_op jit(solution)/shard_map/pull_blocks/pallas_call | solution.py:121
  (191 shorter events, 72.9 us)
Async XLA Ops:
  3.3 7.9 %collective-permute-start = (s32[1,4,128]{2,1,0:T(4,128)S(1)}, s32[1,4,128]{2,1,0:T(4,128)S(1)}, u32[]{:S(2)}, u32[]{:S(2)}) collective-permute-start(s32[1,4,128]{2,1,0:T(4,128)S(1)} %add_bitcast_fusion), channel_id=1, source_target_pairs={{0,16},{4,20},{8,24},{12,28},{16,0},{20,4},{24,8},{28,12},{1,17},{... | collective-permute-start | bytes 6152 | tf_op jit(solution)/shard_map/ppermute | solution.py:509
  11.3 7.7 %collective-permute-start.1 = (s32[2,4,128]{2,1,0:T(4,128)S(1)}, s32[2,4,128]{2,1,0:T(4,128)S(1)}, u32[]{:S(2)}, u32[]{:S(2)}) collective-permute-start(s32[2,4,128]{2,1,0:T(4,128)S(1)} %pad_add_fusion.2), channel_id=1, source_target_pairs={{0,8},{4,12},{8,0},{12,4},{16,24},{20,28},{24,16},{28,20},{1,9},{5... | collective-permute-start | bytes 12296 | tf_op jit(solution)/shard_map/ppermute | solution.py:509
  13.5 12.8 %collective-permute-start.3 = (bf16[6,80,128]{2,1,0:T(8,128)(2,1)S(1)}, bf16[6,80,128]{2,1,0:T(8,128)(2,1)S(1)}, u32[]{:S(2)}, u32[]{:S(2)}) collective-permute-start(bf16[6,80,128]{2,1,0:T(8,128)(2,1)S(1)} %get-tuple-element.52), channel_id=1, source_target_pairs={{0,24},{4,28},{8,16},{12,20},{16,8},{20,12},{24,0},{28,4},{1,25},{... | collective-permute-start | bytes 368648 | tf_op jit(solution)/shard_map/ppermute | solution.py:509
  14.1 15.1 %collective-permute-start.4 = (bf16[6,80,128]{2,1,0:T(8,128)(2,1)S(1)}, bf16[6,80,128]{2,1,0:T(8,128)(2,1)S(1)}, u32[]{:S(2)}, u32[]{:S(2)}) collective-permute-start(bf16[6,80,128]{2,1,0:T(8,128)(2,1)S(1)} %get-tuple-element.53), channel_id=1, source_target_pairs={{0,28},{4,24},{8,20},{12,16},{16,12},{20,8},{24,4},{28,0},{1,29},{... | collective-permute-start | bytes 368648 | tf_op jit(solution)/shard_map/ppermute | solution.py:509
  18.4 22.1 %collective-permute-start.7 = (bf16[6,80,128]{2,1,0:T(8,128)(2,1)S(1)}, bf16[6,80,128]{2,1,0:T(8,128)(2,1)S(1)}, u32[]{:S(2)}, u32[]{:S(2)}) collective-permute-start(bf16[6,80,128]{2,1,0:T(8,128)(2,1)S(1)} %get-tuple-element.55), channel_id=1, source_target_pairs={{0,4},{4,0},{8,12},{12,8},{16,20},{20,16},{24,28},{28,24},{1,5},{5... | collective-permute-start | bytes 368648 | tf_op jit(solution)/shard_map/ppermute | solution.py:509
  18.9 26.0 %collective-permute-start.15 = (bf16[6,80,128]{2,1,0:T(8,128)(2,1)S(1)}, bf16[6,80,128]{2,1,0:T(8,128)(2,1)S(1)}, u32[]{:S(2)}, u32[]{:S(2)}) collective-permute-start(bf16[6,80,128]{2,1,0:T(8,128)(2,1)S(1)} %get-tuple-element.63), channel_id=1, source_target_pairs={{0,8},{4,12},{8,0},{12,4},{16,24},{20,28},{24,16},{28,20},{1,9},{5... | collective-permute-start | bytes 368648 | tf_op jit(solution)/shard_map/ppermute | solution.py:509
  25.1 9.2 %collective-permute-start.19 = (bf16[6,80,128]{2,1,0:T(8,128)(2,1)S(1)}, bf16[6,80,128]{2,1,0:T(8,128)(2,1)S(1)}, u32[]{:S(2)}, u32[]{:S(2)}) collective-permute-start(bf16[6,80,128]{2,1,0:T(8,128)(2,1)S(1)} %get-tuple-element.66), channel_id=1, source_target_pairs={{0,16},{4,20},{8,24},{12,28},{16,0},{20,4},{24,8},{28,12},{1,17},{... | collective-permute-start | bytes 368648 | tf_op jit(solution)/shard_map/ppermute | solution.py:509
  26.3 11.1 %collective-permute-start.20 = (bf16[6,80,128]{2,1,0:T(8,128)(2,1)S(1)}, bf16[6,80,128]{2,1,0:T(8,128)(2,1)S(1)}, u32[]{:S(2)}, u32[]{:S(2)}) collective-permute-start(bf16[6,80,128]{2,1,0:T(8,128)(2,1)S(1)} %get-tuple-element.67), channel_id=1, source_target_pairs={{0,20},{4,16},{8,28},{12,24},{16,4},{20,0},{24,12},{28,8},{1,21},{... | collective-permute-start | bytes 368648 | tf_op jit(solution)/shard_map/ppermute | solution.py:509
  29.3 9.7 %collective-permute-start.5 = (bf16[2,6,80,128]{3,2,1,0:T(8,128)(2,1)S(1)}, bf16[2,6,80,128]{3,2,1,0:T(8,128)(2,1)S(1)}, u32[]{:S(2)}, u32[]{:S(2)}) collective-permute-start(bf16[2,6,80,128]{3,2,1,0:T(8,128)(2,1)S(1)} %pad_maximum_fusion.8), channel_id=1, source_target_pairs={{0,2},{1,3},{2,0},{3,1},{4,6},{5,7},{6,4},{7,5},{8,10},{9,11},{10,... | collective-permute-start | bytes 737288 | tf_op jit(solution)/shard_map/ppermute | solution.py:509
  34.3 10.6 %collective-permute-start.16 = (bf16[6,80,128]{2,1,0:T(8,128)(2,1)S(1)}, bf16[6,80,128]{2,1,0:T(8,128)(2,1)S(1)}, u32[]{:S(2)}, u32[]{:S(2)}) collective-permute-start(bf16[6,80,128]{2,1,0:T(8,128)(2,1)S(1)} %get-tuple-element.64), channel_id=1, source_target_pairs={{0,12},{4,8},{8,4},{12,0},{16,28},{20,24},{24,20},{28,16},{1,13},{... | collective-permute-start | bytes 368648 | tf_op jit(solution)/shard_map/ppermute | solution.py:509
  37.5 7.3 %collective-permute-start.21 = (bf16[2,6,80,128]{3,2,1,0:T(8,128)(2,1)S(1)}, bf16[2,6,80,128]{3,2,1,0:T(8,128)(2,1)S(1)}, u32[]{:S(2)}, u32[]{:S(2)}) collective-permute-start(bf16[2,6,80,128]{3,2,1,0:T(8,128)(2,1)S(1)} %pad_maximum_fusion.11), channel_id=1, source_target_pairs={{0,2},{1,3},{2,0},{3,1},{4,6},{5,7},{6,4},{7,5},{8,10},{9,11},{10,... | collective-permute-start | bytes 737288 | tf_op jit(solution)/shard_map/ppermute | solution.py:509
  44.8 7.0 %collective-permute-start.22 = (bf16[2,12,80,128]{3,2,1,0:T(8,128)(2,1)S(1)}, bf16[2,12,80,128]{3,2,1,0:T(8,128)(2,1)S(1)}, u32[]{:S(2)}, u32[]{:S(2)}) collective-permute-start(bf16[2,12,80,128]{3,2,1,0:T(8,128)(2,1)S(1)} %pad_maximum_fusion.7), channel_id=1, source_target_pairs={{0,1},{1,0},{2,3},{3,2},{4,5},{5,4},{6,7},{7,6},{8,9},{9,8},{10,11... | collective-permute-start | bytes 1474568 | tf_op jit(solution)/shard_map/ppermute | solution.py:509
  48.8 18.9 %collective-permute-start.23 = (bf16[12,80,384]{2,1,0:T(8,128)(2,1)S(1)}, bf16[12,80,384]{2,1,0:T(8,128)(2,1)S(1)}, u32[]{:S(2)}, u32[]{:S(2)}) collective-permute-start(bf16[12,80,384]{2,1,0:T(8,128)(2,1)S(1)} %spread_blocks.4), channel_id=1, source_target_pairs={{0,4},{4,0},{8,12},{12,8},{16,20},{20,16},{24,28},{28,24},{1,5},{5... | collective-permute-start | bytes 2211848 | tf_op jit(solution)/shard_map/ppermute | solution.py:509
  49.8 8.8 %collective-permute-start.8 = (bf16[2,6,80,128]{3,2,1,0:T(8,128)(2,1)S(1)}, bf16[2,6,80,128]{3,2,1,0:T(8,128)(2,1)S(1)}, u32[]{:S(2)}, u32[]{:S(2)}) collective-permute-start(bf16[2,6,80,128]{3,2,1,0:T(8,128)(2,1)S(1)} %pad_maximum_fusion.9), channel_id=1, source_target_pairs={{0,2},{1,3},{2,0},{3,1},{4,6},{5,7},{6,4},{7,5},{8,10},{9,11},{10,... | collective-permute-start | bytes 737288 | tf_op jit(solution)/shard_map/ppermute | solution.py:509
  51.3 11.8 %collective-permute-start.17 = (bf16[2,6,80,128]{3,2,1,0:T(8,128)(2,1)S(1)}, bf16[2,6,80,128]{3,2,1,0:T(8,128)(2,1)S(1)}, u32[]{:S(2)}, u32[]{:S(2)}) collective-permute-start(bf16[2,6,80,128]{3,2,1,0:T(8,128)(2,1)S(1)} %pad_maximum_fusion.10), channel_id=1, source_target_pairs={{0,2},{1,3},{2,0},{3,1},{4,6},{5,7},{6,4},{7,5},{8,10},{9,11},{10,... | collective-permute-start | bytes 737288 | tf_op jit(solution)/shard_map/ppermute | solution.py:509
  67.7 18.1 %collective-permute-start.24 = (bf16[12,80,384]{2,1,0:T(8,128)(2,1)S(1)}, bf16[12,80,384]{2,1,0:T(8,128)(2,1)S(1)}, u32[]{:S(2)}, u32[]{:S(2)}) collective-permute-start(bf16[12,80,384]{2,1,0:T(8,128)(2,1)S(1)} %spread_blocks.7), channel_id=1, source_target_pairs={{0,4},{4,0},{8,12},{12,8},{16,20},{20,16},{24,28},{28,24},{1,5},{5... | collective-permute-start | bytes 2211848 | tf_op jit(solution)/shard_map/ppermute | solution.py:509
  72.5 24.4 %collective-permute-start.27 = (bf16[1408,384]{1,0:T(8,128)(2,1)S(1)}, bf16[1408,384]{1,0:T(8,128)(2,1)}, u32[]{:S(2)}, u32[]{:S(2)}) collective-permute-start(bf16[1408,384]{1,0:T(8,128)(2,1)S(1)} %render_blocks.7), channel_id=1, source_target_pairs={{0,8},{4,12},{24,16},{28,20},{1,9},{5,13},{25,17},{29,21},{2,10},{... | collective-permute-start | bytes 3244040 | tf_op jit(solution)/shard_map/ppermute | solution.py:509
  85.8 25.4 %collective-permute-start.25 = (bf16[12,80,384]{2,1,0:T(8,128)(2,1)S(1)}, bf16[12,80,384]{2,1,0:T(8,128)(2,1)S(1)}, u32[]{:S(2)}, u32[]{:S(2)}) collective-permute-start(bf16[12,80,384]{2,1,0:T(8,128)(2,1)S(1)} %spread_blocks.6), channel_id=1, source_target_pairs={{0,4},{4,0},{8,12},{12,8},{16,20},{20,16},{24,28},{28,24},{1,5},{5... | collective-permute-start | bytes 2211848 | tf_op jit(solution)/shard_map/ppermute | solution.py:509
  99.5 26.6 %collective-permute-start.30 = (bf16[1408,384]{1,0:T(8,128)(2,1)}, bf16[1408,384]{1,0:T(8,128)(2,1)}, u32[]{:S(2)}, u32[]{:S(2)}) collective-permute-start(bf16[1408,384]{1,0:T(8,128)(2,1)} %add_convert_fusion.2), channel_id=1, source_target_pairs={{0,8},{4,12},{24,16},{28,20},{1,9},{5,13},{25,17},{29,21},{2,10},{... | collective-permute-start | bytes 3244040 | tf_op jit(solution)/shard_map/ppermute | solution.py:509
  105.8 22.8 %collective-permute-start.28 = (bf16[1408,384]{1,0:T(8,128)(2,1)}, bf16[1408,384]{1,0:T(8,128)(2,1)}, u32[]{:S(2)}, u32[]{:S(2)}) collective-permute-start(bf16[1408,384]{1,0:T(8,128)(2,1)} %add_convert_fusion.2), channel_id=1, source_target_pairs={{8,16},{12,20},{16,8},{20,12},{9,17},{13,21},{17,9},{21,13},{10,18... | collective-permute-start | bytes 3244040 | tf_op jit(solution)/shard_map/ppermute | solution.py:509
  107.6 28.9 %collective-permute-start.12 = (bf16[2,176,384]{2,1,0:T(8,128)(2,1)S(1)}, bf16[2,176,384]{2,1,0:T(8,128)(2,1)}, u32[]{:S(2)}, u32[]{:S(2)}) collective-permute-start(bf16[2,176,384]{2,1,0:T(8,128)(2,1)S(1)} %get-tuple-element.60), channel_id=1, source_target_pairs={{0,1},{1,0},{2,3},{3,2},{4,5},{5,4},{6,7},{7,6},{8,9},{9,8},{10,11... | collective-permute-start | bytes 811016 | tf_op jit(solution)/shard_map/ppermute | solution.py:509
  107.7 28.9 %collective-permute-start.13 = (bf16[2,176,384]{2,1,0:T(8,128)(2,1)S(1)}, bf16[2,176,384]{2,1,0:T(8,128)(2,1)}, u32[]{:S(2)}, u32[]{:S(2)}) collective-permute-start(bf16[2,176,384]{2,1,0:T(8,128)(2,1)S(1)} %get-tuple-element.61), channel_id=1, source_target_pairs={{0,2},{1,3},{2,0},{3,1},{4,6},{5,7},{6,4},{7,5},{8,10},{9,11},{10,... | collective-permute-start | bytes 811016 | tf_op jit(solution)/shard_map/ppermute | solution.py:509
  111.3 41.3 %collective-permute-start.26 = (bf16[12,80,384]{2,1,0:T(8,128)(2,1)S(1)}, bf16[12,80,384]{2,1,0:T(8,128)(2,1)S(1)}, u32[]{:S(2)}, u32[]{:S(2)}) collective-permute-start(bf16[12,80,384]{2,1,0:T(8,128)(2,1)S(1)} %spread_blocks.5), channel_id=1, source_target_pairs={{0,4},{4,0},{8,12},{12,8},{16,20},{20,16},{24,28},{28,24},{1,5},{5... | collective-permute-start | bytes 2211848 | tf_op jit(solution)/shard_map/ppermute | solution.py:509
  127.6 28.9 %collective-permute-start.31 = (bf16[1408,384]{1,0:T(8,128)(2,1)S(1)}, bf16[1408,384]{1,0:T(8,128)(2,1)S(1)}, u32[]{:S(2)}, u32[]{:S(2)}) collective-permute-start(bf16[1408,384]{1,0:T(8,128)(2,1)S(1)} %add_convert_fusion), channel_id=1, source_target_pairs={{8,16},{12,20},{16,8},{20,12},{9,17},{13,21},{17,9},{21,13},{10,18... | collective-permute-start | bytes 3244040 | tf_op jit(solution)/shard_map/ppermute | solution.py:509
  131.1 26.9 %collective-permute-start.29 = (bf16[1408,384]{1,0:T(8,128)(2,1)}, bf16[1408,384]{1,0:T(8,128)(2,1)S(1)}, u32[]{:S(2)}, u32[]{:S(2)}) collective-permute-start(bf16[1408,384]{1,0:T(8,128)(2,1)} %add_convert_fusion.1), channel_id=1, source_target_pairs={{0,8},{4,12},{8,0},{12,4},{16,24},{20,28},{24,16},{28,20},{1,9},{5... | collective-permute-start | bytes 3244040 | tf_op jit(solution)/shard_map/ppermute | solution.py:509
  136.5 8.7 %collective-permute-start.14 = (bf16[2,176,384]{2,1,0:T(8,128)(2,1)S(1)}, bf16[2,176,384]{2,1,0:T(8,128)(2,1)S(1)}, u32[]{:S(2)}, u32[]{:S(2)}) collective-permute-start(bf16[2,176,384]{2,1,0:T(8,128)(2,1)S(1)} %get-tuple-element.62), channel_id=1, source_target_pairs={{0,3},{1,2},{2,1},{3,0},{4,7},{5,6},{6,5},{7,4},{8,11},{9,10},{10,... | collective-permute-start | bytes 811016 | tf_op jit(solution)/shard_map/ppermute | solution.py:509
  136.5 15.1 %collective-permute-start.10 = (bf16[192,768]{1,0:T(8,128)(2,1)S(1)}, bf16[192,768]{1,0:T(8,128)(2,1)S(1)}, u32[]{:S(2)}, u32[]{:S(2)}) collective-permute-start(bf16[192,768]{1,0:T(8,128)(2,1)S(1)} %copy-done.8), channel_id=1, source_target_pairs={{0,2},{1,3},{2,0},{3,1},{4,6},{5,7},{6,4},{7,5},{8,10},{9,11},{10,... | collective-permute-start | bytes 884744 | tf_op jit(solution)/shard_map/ppermute | solution.py:509
  152.5 8.2 %collective-permute-start.11 = (bf16[384,768]{1,0:T(8,128)(2,1)}, bf16[384,768]{1,0:T(8,128)(2,1)}, u32[]{:S(2)}, u32[]{:S(2)}) collective-permute-start(bf16[384,768]{1,0:T(8,128)(2,1)} %pad_maximum_fusion.3), channel_id=1, source_target_pairs={{0,1},{1,0},{2,3},{3,2},{4,5},{5,4},{6,7},{7,6},{8,9},{9,8},{10,11... | collective-permute-start | bytes 1769480 | tf_op jit(solution)/shard_map/ppermute | solution.py:509
  160.0 6.9 %collective-permute-start.34 = (bf16[176,384]{1,0:T(8,128)(2,1)S(1)}, bf16[176,384]{1,0:T(8,128)(2,1)S(1)}, u32[]{:S(2)}, u32[]{:S(2)}) collective-permute-start(bf16[176,384]{1,0:T(8,128)(2,1)S(1)} %get-tuple-element.75), channel_id=1, source_target_pairs={{0,3},{1,2},{2,1},{3,0},{4,7},{5,6},{6,5},{7,4},{8,11},{9,10},{10,... | collective-permute-start | bytes 405512 | tf_op jit(solution)/shard_map/ppermute | solution.py:509
  161.8 9.3 %collective-permute-start.38 = (bf16[176,384]{1,0:T(8,128)(2,1)S(1)}, bf16[176,384]{1,0:T(8,128)(2,1)S(1)}, u32[]{:S(2)}, u32[]{:S(2)}) collective-permute-start(bf16[176,384]{1,0:T(8,128)(2,1)S(1)} %get-tuple-element.81), channel_id=1, source_target_pairs={{0,2},{1,3},{2,0},{3,1},{4,6},{5,7},{6,4},{7,5},{8,10},{9,11},{10,... | collective-permute-start | bytes 405512 | tf_op jit(solution)/shard_map/ppermute | solution.py:509
  163.3 7.7 %collective-permute-start.39 = (bf16[176,384]{1,0:T(8,128)(2,1)S(1)}, bf16[176,384]{1,0:T(8,128)(2,1)S(1)}, u32[]{:S(2)}, u32[]{:S(2)}) collective-permute-start(bf16[176,384]{1,0:T(8,128)(2,1)S(1)} %get-tuple-element.82), channel_id=1, source_target_pairs={{0,1},{1,0},{2,3},{3,2},{4,5},{5,4},{6,7},{7,6},{8,9},{9,8},{10,11... | collective-permute-start | bytes 405512 | tf_op jit(solution)/shard_map/ppermute | solution.py:509
  164.1 7.6 %collective-permute-start.40 = (bf16[176,384]{1,0:T(8,128)(2,1)S(1)}, bf16[176,384]{1,0:T(8,128)(2,1)S(1)}, u32[]{:S(2)}, u32[]{:S(2)}) collective-permute-start(bf16[176,384]{1,0:T(8,128)(2,1)S(1)} %get-tuple-element.83), channel_id=1, source_target_pairs={{0,3},{1,2},{2,1},{3,0},{4,7},{5,6},{6,5},{7,4},{8,11},{9,10},{10,... | collective-permute-start | bytes 405512 | tf_op jit(solution)/shard_map/ppermute | solution.py:509
  178.7 10.1 %collective-permute-start.36 = (bf16[176,384]{1,0:T(8,128)(2,1)S(1)}, bf16[176,384]{1,0:T(8,128)(2,1)S(1)}, u32[]{:S(2)}, u32[]{:S(2)}) collective-permute-start(bf16[176,384]{1,0:T(8,128)(2,1)S(1)} %get-tuple-element.78), channel_id=1, source_target_pairs={{0,2},{1,3},{2,0},{3,1},{4,6},{5,7},{6,4},{7,5},{8,10},{9,11},{10,... | collective-permute-start | bytes 405512 | tf_op jit(solution)/shard_map/ppermute | solution.py:509
  180.1 9.9 %collective-permute-start.37 = (bf16[176,384]{1,0:T(8,128)(2,1)S(1)}, bf16[176,384]{1,0:T(8,128)(2,1)S(1)}, u32[]{:S(2)}, u32[]{:S(2)}) collective-permute-start(bf16[176,384]{1,0:T(8,128)(2,1)S(1)} %get-tuple-element.79), channel_id=1, source_target_pairs={{0,3},{1,2},{2,1},{3,0},{4,7},{5,6},{6,5},{7,4},{8,11},{9,10},{10,... | collective-permute-start | bytes 405512 | tf_op jit(solution)/shard_map/ppermute | solution.py:509
  190.3 29.6 %collective-permute-start.53 = (f32[2,192,768]{2,1,0:T(8,128)S(1)}, f32[2,192,768]{2,1,0:T(8,128)S(1)}, u32[]{:S(2)}, u32[]{:S(2)}) collective-permute-start(f32[2,192,768]{2,1,0:T(8,128)S(1)} %bitcast.115), channel_id=1, source_target_pairs={{0,1},{1,0},{2,3},{3,2},{4,5},{5,4},{6,7},{7,6},{8,9},{9,8},{10,11... | collective-permute-start | bytes 3538952 | tf_op jit(solution)/shard_map/ppermute | solution.py:509
  191.0 26.0 %collective-permute-start.45 = (bf16[1408,384]{1,0:T(8,128)(2,1)S(1)}, bf16[1408,384]{1,0:T(8,128)(2,1)}, u32[]{:S(2)}, u32[]{:S(2)}) collective-permute-start(bf16[1408,384]{1,0:T(8,128)(2,1)S(1)} %gather_rows.1.images_ref.refs_10_), channel_id=1, source_target_pairs={{0,8},{4,12},{8,0},{12,4},{16,24},{20,28},{24,16},{28,20},{1,9},{5... | collective-permute-start | bytes 3244040 | tf_op jit(solution)/shard_map/ppermute | solution.py:509
  192.8 25.9 %collective-permute-start.44 = (bf16[1408,384]{1,0:T(8,128)(2,1)S(1)}, bf16[1408,384]{1,0:T(8,128)(2,1)}, u32[]{:S(2)}, u32[]{:S(2)}) collective-permute-start(bf16[1408,384]{1,0:T(8,128)(2,1)S(1)} %gather_rows.1.images_ref.refs_10_), channel_id=1, source_target_pairs={{8,16},{12,20},{16,8},{20,12},{9,17},{13,21},{17,9},{21,13},{10,18... | collective-permute-start | bytes 3244040 | tf_op jit(solution)/shard_map/ppermute | solution.py:509
  197.2 28.8 %collective-permute-start.49 = (bf16[12,80,384]{2,1,0:T(8,128)(2,1)}, bf16[12,80,384]{2,1,0:T(8,128)(2,1)}, u32[]{:S(2)}, u32[]{:S(2)}) collective-permute-start(bf16[12,80,384]{2,1,0:T(8,128)(2,1)} %pick_bands.6), channel_id=1, source_target_pairs={{0,4},{4,0},{8,12},{12,8},{16,20},{20,16},{24,28},{28,24},{1,5},{5... | collective-permute-start | bytes 2211848 | tf_op jit(solution)/shard_map/ppermute | solution.py:509
  217.0 21.9 %collective-permute-start.46 = (bf16[1408,384]{1,0:T(8,128)(2,1)}, bf16[1408,384]{1,0:T(8,128)(2,1)}, u32[]{:S(2)}, u32[]{:S(2)}) collective-permute-start(bf16[1408,384]{1,0:T(8,128)(2,1)} %collective-permute-done.45.images_ref.refs_14_), channel_id=1, source_target_pairs={{8,16},{12,20},{16,8},{20,12},{9,17},{13,21},{17,9},{21,13},{10,18... | collective-permute-start | bytes 3244040 | tf_op jit(solution)/shard_map/ppermute | solution.py:509
  218.6 27.2 %collective-permute-start.48 = (bf16[1408,384]{1,0:T(8,128)(2,1)}, bf16[1408,384]{1,0:T(8,128)(2,1)}, u32[]{:S(2)}, u32[]{:S(2)}) collective-permute-start(bf16[1408,384]{1,0:T(8,128)(2,1)} %collective-permute-done.44), channel_id=1, source_target_pairs={{8,0},{12,4},{16,24},{20,28},{9,1},{13,5},{17,25},{21,29},{10,2},{... | collective-permute-start | bytes 3244040 | tf_op jit(solution)/shard_map/ppermute | solution.py:509
  222.0 15.7 %collective-permute-start.54 = (f32[192,768]{1,0:T(8,128)}, f32[192,768]{1,0:T(8,128)}, u32[]{:S(2)}, u32[]{:S(2)}) collective-permute-start(f32[192,768]{1,0:T(8,128)} %slice_bitcast_fusion), channel_id=1, source_target_pairs={{0,2},{1,3},{2,0},{3,1},{4,6},{5,7},{6,4},{7,5},{8,10},{9,11},{10,... | collective-permute-start | bytes 1769480 | tf_op jit(solution)/shard_map/ppermute | solution.py:509
  226.0 23.4 %collective-permute-start.50 = (bf16[12,80,384]{2,1,0:T(8,128)(2,1)S(1)}, bf16[12,80,384]{2,1,0:T(8,128)(2,1)S(1)}, u32[]{:S(2)}, u32[]{:S(2)}) collective-permute-start(bf16[12,80,384]{2,1,0:T(8,128)(2,1)S(1)} %pick_bands.5), channel_id=1, source_target_pairs={{0,4},{4,0},{8,12},{12,8},{16,20},{20,16},{24,28},{28,24},{1,5},{5... | collective-permute-start | bytes 2211848 | tf_op jit(solution)/shard_map/ppermute | solution.py:509
  238.8 32.5 %collective-permute-start.47 = (bf16[1408,384]{1,0:T(8,128)(2,1)}, bf16[1408,384]{1,0:T(8,128)(2,1)S(1)}, u32[]{:S(2)}, u32[]{:S(2)}) collective-permute-start(bf16[1408,384]{1,0:T(8,128)(2,1)} %collective-permute-done.46), channel_id=1, source_target_pairs={{8,0},{12,4},{16,24},{20,28},{9,1},{13,5},{17,25},{21,29},{10,2},{... | collective-permute-start | bytes 3244040 | tf_op jit(solution)/shard_map/ppermute | solution.py:509
  240.2 10.0 %collective-permute-start.55 = (f32[96,768]{1,0:T(8,128)S(1)}, f32[96,768]{1,0:T(8,128)S(1)}, u32[]{:S(2)}, u32[]{:S(2)}) collective-permute-start(f32[96,768]{1,0:T(8,128)S(1)} %constant_dynamic-slice_fusion), channel_id=1, source_target_pairs={{0,4},{4,0},{8,12},{12,8},{16,20},{20,16},{24,28},{28,24},{1,5},{5... | collective-permute-start | bytes 884744 | tf_op jit(solution)/shard_map/ppermute | solution.py:509
  249.3 24.2 %collective-permute-start.51 = (bf16[12,80,384]{2,1,0:T(8,128)(2,1)S(1)}, bf16[12,80,384]{2,1,0:T(8,128)(2,1)S(1)}, u32[]{:S(2)}, u32[]{:S(2)}) collective-permute-start(bf16[12,80,384]{2,1,0:T(8,128)(2,1)S(1)} %pick_bands.4), channel_id=1, source_target_pairs={{0,4},{4,0},{8,12},{12,8},{16,20},{20,16},{24,28},{28,24},{1,5},{5... | collective-permute-start | bytes 2211848 | tf_op jit(solution)/shard_map/ppermute | solution.py:509
  250.2 23.3 %collective-permute-start.56 = (bf16[96,768]{1,0:T(8,128)(2,1)S(1)}, bf16[96,768]{1,0:T(8,128)(2,1)S(1)}, u32[]{:S(2)}, u32[]{:S(2)}) collective-permute-start(bf16[96,768]{1,0:T(8,128)(2,1)S(1)} %get-tuple-element.106), channel_id=1, source_target_pairs={{0,8},{4,12},{8,0},{12,4},{16,24},{20,28},{24,16},{28,20},{1,9},{5... | collective-permute-start | bytes 442376 | tf_op jit(solution)/shard_map/ppermute | solution.py:509
  273.5 19.5 %collective-permute-start.52 = (bf16[12,80,384]{2,1,0:T(8,128)(2,1)S(1)}, bf16[12,80,384]{2,1,0:T(8,128)(2,1)S(1)}, u32[]{:S(2)}, u32[]{:S(2)}) collective-permute-start(bf16[12,80,384]{2,1,0:T(8,128)(2,1)S(1)} %pick_bands.7), channel_id=1, source_target_pairs={{0,4},{4,0},{8,12},{12,8},{16,20},{20,16},{24,28},{28,24},{1,5},{5... | collective-permute-start | bytes 2211848 | tf_op jit(solution)/shard_map/ppermute | solution.py:509
  274.5 11.1 %collective-permute-start.57 = (bf16[96,768]{1,0:T(8,128)(2,1)S(1)}, bf16[96,768]{1,0:T(8,128)(2,1)S(1)}, u32[]{:S(2)}, u32[]{:S(2)}) collective-permute-start(bf16[96,768]{1,0:T(8,128)(2,1)S(1)} %fusion.1), channel_id=1, source_target_pairs={{0,16},{4,20},{8,24},{12,28},{16,0},{20,4},{24,8},{28,12},{1,17},{... | collective-permute-start | bytes 442376 | tf_op jit(solution)/shard_map/ppermute | solution.py:509
  (21 other events, 148.5 us)

commit v2 on v1

--- a/solution.py
+++ b/solution.py
@@ -9,7 +9,6 @@
 BAND = 2
 BLOCK = 128
 GROUP = 4
-VMEM_BYTES = 48 * 1024 * 1024
 
 
 def slot_plan(owners, peer_count, capacity):
@@ -114,7 +113,7 @@
     return pl.CostEstimate(flops=int(us * 1e9), bytes_accessed=int(us * 2e6), transcendentals=0)
 
 
-def call(body, out_shape, args, n_scalars, us, name, scratch=(), aliases=None):
+def call(body, out_shape, args, n_scalars, us, name, scratch=(), mib=12):
     smem = pl.BlockSpec(memory_space=pltpu.SMEM)
     vmem = pl.BlockSpec(memory_space=pltpu.VMEM)
     many = isinstance(out_shape, list)
@@ -124,7 +123,7 @@
         in_specs=[smem] * n_scalars + [vmem] * (len(args) - n_scalars),
         out_specs=[vmem] * len(out_shape) if many else vmem,
         scratch_shapes=list(scratch),
-        compiler_params=pltpu.CompilerParams(vmem_limit_bytes=VMEM_BYTES),
+        compiler_params=pltpu.CompilerParams(vmem_limit_bytes=mib * 1024 * 1024),
         cost_estimate=price(us),
         name=name,
     )(*args)
@@ -250,18 +249,24 @@
     return call(body, images, args, 6, 5, "render_blocks", scratch)
 
 
-def unpack_images(images_ref, image, half_rows):
-    for u in range(images_ref.shape[0] // half_rows):
-        first, second = apart(images_ref[u * half_rows : (u + 1) * half_rows, :].astype(jnp.float32))
+def unpack_images(image_refs, image, half_rows):
+    views = [
+        ref[i * half_rows : (i + 1) * half_rows, :]
+        for ref in image_refs
+        for i in range(ref.shape[0] // half_rows)
+    ]
+    for u, view in enumerate(views):
+        first, second = apart(view.astype(jnp.float32))
         image[2 * u * half_rows : (2 * u + 1) * half_rows, :] = first
         image[(2 * u + 1) * half_rows : (2 * u + 2) * half_rows, :] = second
 
 
 def pick(count, place, images, slots, band_rows, half_rows):
-    pixels, packed = 2 * images.shape[0], images.shape[1]
-
-    def body(count_ref, place_ref, images_ref, out_ref, image):
-        unpack_images(images_ref, image, half_rows)
+    pixels, packed = 2 * sum(part.shape[0] for part in images), images[0].shape[1]
+
+    def body(count_ref, place_ref, *rest):
+        image_refs, (out_ref, image) = rest[:-2], rest[-2:]
+        unpack_images(image_refs, image, half_rows)
         image[pixels:, :] = jnp.zeros((band_rows + 8, 256), jnp.float32)
 
         def group(step, carry):
@@ -280,35 +285,33 @@
 
     out = jax.ShapeDtypeStruct((slots // 2, band_rows, packed), jnp.bfloat16)
     scratch = [pltpu.VMEM((pixels + band_rows + 8, 256), jnp.float32)]
-    return call(body, out, (count, place, images), 2, 1, "pick_bands", scratch)
+    return call(body, out, (count, place) + tuple(images), 2, 1, "pick_bands", scratch)
 
 
 def pull(jobs, where, old, blocks, half_rows, last):
     band_rows = jobs[0]["weights"].shape[1]
-    pixels = max([2 * job["images"].shape[0] for job in jobs if "place" in job], default=0)
+    pixels = max([2 * sum(part.shape[0] for part in job.get("images", ())) for job in jobs])
     width = jobs[0]["width"]
     first = old is None
     tables, arrays, layout = [where], [], []
     for job in jobs:
-        layout.append((len(tables), len(arrays), "place" in job))
+        layout.append((len(tables), len(arrays), len(job.get("images", ()))))
         tables += [job["count"], job["block"]] + ([job["place"]] if "place" in job else [])
-        arrays += [job["weights"], job["images"] if "place" in job else job["bands"]]
+        arrays += [job["weights"]] + (list(job["images"]) if "place" in job else [job["bands"]])
     arrays += [] if first else [old]
 
     def body(*refs):
         where_ref = refs[0]
         array_refs = refs[len(tables) : len(tables) + len(arrays)]
-        out_ref, image, acc = refs[len(tables) + len(arrays) :]
-        if first:
-            acc[...] = jnp.zeros_like(acc)
-        else:
-            acc[0:blocks] = array_refs[-1][...]
+        out_ref, image, *rest = refs[len(tables) + len(arrays) :]
+        acc = rest[0] if last else out_ref
+        acc[...] = jnp.zeros_like(acc) if first else array_refs[-1][...]
 
         for table, array, own in layout:
             count_ref, block_ref, weight_ref = refs[table], refs[table + 1], array_refs[array]
             place_ref, other_ref = refs[table + 2], array_refs[array + 1]
             if own:
-                unpack_images(other_ref, image, half_rows)
+                unpack_images(array_refs[array + 1 : array + 1 + own], image, half_rows)
 
             def group(step, carry):
                 terms = []
@@ -347,15 +350,16 @@
                 return carry
 
             lax.fori_loop(0, rounds(count_ref[0], GROUP), group if own else other_group, 0)
-        out_ref[...] = acc[0:blocks].astype(out_ref.dtype)
-
-    out = jax.ShapeDtypeStruct((blocks, width, BLOCK), jnp.bfloat16 if last else jnp.float32)
-    scratch = [
-        pltpu.VMEM((pixels + band_rows + 8, 256), jnp.float32),
-        pltpu.VMEM((blocks + 1, width, BLOCK), jnp.float32),
-    ]
+        if last:
+            out_ref[...] = acc[0:blocks].astype(out_ref.dtype)
+
+    sums = (blocks + 1, width, BLOCK)
+    out = jax.ShapeDtypeStruct((blocks, width, BLOCK), jnp.bfloat16)
+    out = out if last else jax.ShapeDtypeStruct(sums, jnp.float32)
+    scratch = [pltpu.VMEM((pixels + band_rows + 8, 256), jnp.float32)]
+    scratch += [pltpu.VMEM(sums, jnp.float32)] if last else []
     us = 1
-    return call(body, out, tuple(tables + arrays), len(tables), us, "pull_blocks", scratch)
+    return call(body, out, tuple(tables + arrays), len(tables), us, "pull_blocks", scratch, 24)
 
 
 def loss_kernel(u, teacher_width, side_ref, head_ref, teacher_ref, *rest):
@@ -412,40 +416,35 @@
     outs += [jax.ShapeDtypeStruct(head.shape, jnp.float32)]
     body = lambda *refs: loss_kernel(u, teacher_width, *refs)
     args = (side, head, teacher) + tuple(parts) + (() if grad is None else (grad,))
-    *images, grad = call(body, outs, args, 1, 3, "loss_rows")
+    *images, grad = call(body, outs, args, 1, 3, "loss_rows", (), 20)
     return images, grad
 
 
-def deal(side, terms, sides, half_rows):
+def deal(side, terms, starts, sides, half_rows):
     rows = half_rows // sides
-    views = terms[0].shape[0] // half_rows
 
     def body(side_ref, *refs):
-        for u in range(views):
-            for d in range(sides):
-                start = pl.multiple_of(u * half_rows + (side_ref[0] ^ d) * rows, 16)
-                value = refs[0][pl.ds(start, rows), :].astype(jnp.float32)
-                for ref in refs[1 : len(terms)]:
-                    value = value + ref[pl.ds(start, rows), :].astype(jnp.float32)
-                refs[len(terms) + u * sides + d][...] = value.astype(jnp.bfloat16)
+        for d in range(sides):
+            here = (side_ref[0] ^ d) * rows
+            value = 0.0
+            for ref, start in zip(refs, starts):
+                value = value + ref[pl.ds(pl.multiple_of(start + here, 16), rows), :].astype(jnp.float32)
+            refs[len(terms) + d][...] = value.astype(jnp.bfloat16)
 
     out = jax.ShapeDtypeStruct((rows, terms[0].shape[1]), jnp.bfloat16)
-    parts = call(body, [out] * (views * sides), (side,) + tuple(terms), 1, 2, "deal_rows")
-    return [parts[u * sides : (u + 1) * sides] for u in range(views)]
-
-
-def gather(side, parts, half_rows):
-    views, sides = len(parts), len(parts[0])
-    rows, lanes = parts[0][0].shape
+    return call(body, [out] * sides, (side,) + tuple(terms), 1, 1, "deal_rows")
+
+
+def gather(side, parts):
+    rows, lanes = parts[0].shape
 
     def body(side_ref, *refs):
-        for u in range(views):
-            for d in range(sides):
-                start = pl.multiple_of(u * half_rows + (side_ref[0] ^ d) * rows, 16)
-                refs[-1][pl.ds(start, rows), :] = refs[u * sides + d][...]
-
-    out = jax.ShapeDtypeStruct((views * half_rows, lanes), jnp.bfloat16)
-    return call(body, out, (side,) + tuple(sum(parts, [])), 1, 2, "gather_rows")
+        for d in range(len(parts)):
+            here = pl.ds(pl.multiple_of((side_ref[0] ^ d) * rows, 16), rows)
+            refs[-1][here, :] = refs[d][...]
+
+    out = jax.ShapeDtypeStruct((rows * len(parts), lanes), jnp.bfloat16)
+    return call(body, out, (side,) + tuple(parts), 1, 1, "gather_rows")
 
 
 def turn_teacher(side, teacher, sides, padded):
@@ -592,25 +591,35 @@
     mid = total(kept[2], far)
     inward = along(mid, [(0, 1), (3, 2)])
     between = along(mid, [(1, 2), (2, 1)])
-    near = along(total(kept[1], between), [(0, 1), (1, 0), (2, 3), (3, 2)])
-    centre = along(total(kept[3], inward), [(1, 2), (2, 1)])
-
-    parts = deal(side_id, (kept[0], near, centre), sides, half_rows)
-    parts = [[swap(of[d], "feat", d) if d else of[d] for d in (0, 2, 1, 3)] for of in parts]
-    back, grad = [], None
+    back, grad, held = [], None, None
     for u in range(view_count):
-        images, grad = loss(u, side_id, parts[u], head, target, grad)
-        images = [swap(image, "feat", d) if d else image for d, image in zip((0, 2, 1, 3), images)]
-        back.append([images[i] for i in (0, 2, 1, 3)])
-    own = gather(side_id, back, half_rows)
-
+        here = slice(u * half_rows, (u + 1) * half_rows)
+        near = along(total(kept[1][here], between[here]), [(0, 1), (1, 0), (2, 3), (3, 2)])
+        centre = along(total(kept[3][here], inward[here]), [(1, 2), (2, 1)])
+        terms = (kept[0], near, centre)
+        back.append(terms)
     middle = (line == 1) | (line == 2)
-    near = along(own, [(0, 1), (1, 0), (2, 3), (3, 2)])
-    centre = along(own, [(1, 2), (2, 1)])
+    images, nears, centres = [], [], []
+    for u in range(view_count):
+        terms = back[u]
+        parts = deal(side_id, terms, (u * half_rows, 0, 0), sides, half_rows)
+        parts = [swap(parts[d], "feat", d) if d else parts[d] for d in (0, 2, 1, 3)]
+        if u:
+            parts = after(parts, images[-1])
+        parts, grad = loss(u, side_id, parts, head, target, grad)
+        held = parts[0]
+        parts = [swap(part, "feat", d) if d else part for d, part in zip((0, 2, 1, 3), parts)]
+        parts = [parts[i] for i in (0, 2, 1, 3)]
+        if u:
+            parts = after(parts, nears[-1], centres[-1])
+        images.append(gather(side_id, parts))
+        nears.append(along(images[u], [(0, 1), (1, 0), (2, 3), (3, 2)]))
+        centres.append(along(images[u], [(1, 2), (2, 1)]))
+    near, centre = jnp.concatenate(nears, axis=0), jnp.concatenate(centres, axis=0)
     out_near = along(centre, [(1, 0), (2, 3)])
     cross = along(near, [(1, 2), (2, 1)])
     out_far = along(cross, [(1, 0), (2, 3)])
-    chunks = [own, near, jnp.where(middle, cross, out_near), jnp.where(middle, centre, out_far)]
+    chunks = [images, nears, [jnp.where(middle, cross, out_near)], [jnp.where(middle, centre, out_far)]]
     jobs, marks, bands, sums = {}, [], None, None
     for j in range(4):
         if j >= 2:

time: 302 us -> 286 us (0.947)
  local copies, waits for them, and re-layouts: 13.6 us -> 22.2 us
  waiting for transfers between devices: 114 us -> 106 us
  other arithmetic: 15.3 us -> 8.36 us
  Pallas kernels: 77.9 us -> 73.6 us
  starting transfers between devices: 77.3 us -> 74.1 us
    ppermute x59 -> x63, waiting for transfers between devices: 114 us -> 106 us  [hop(): return lax.ppermute(value, axis, pairs)]
    unnamed x29 -> x63, local copies, waits for them, and re-layouts: 8.44 us -> 14.9 us
    convert_element_type x3, other arithmetic: 6.5 us -> 0.9 us  [total(): return acc.astype(jnp.bfloat16)]
    pallas_call x22 -> x24, Pallas kernels: 77.9 us -> 73.6 us  [call(): pl.pallas_call(body, out_shape=out_shape, in_specs=[smem] * n_scalars + [...]
    ppermute x59 -> x63, starting transfers between devices: 77.3 us -> 74.1 us  [hop(): return lax.ppermute(value, axis, pairs)]
  transfers between devices with their start and end apart: 59 -> 63, of which waited for: 24 -> 24; matrix products, arithmetic and copies ran while one was open for 7% -> 7% of each run, Pallas kernels for 22% -> 24%
where the time goes in v2:
time: 286 us
  waiting for transfers between devices  106 us (37%)
  starting transfers between devices  74.1 us (26%)
  Pallas kernels  73.6 us (26%)
  local copies, waits for them, and re-layouts  22.2 us (8%)
  other arithmetic  8.36 us (3%)
    ppermute x63, waiting for transfers between devices, hop(): return lax.ppermute(value, axis, pairs)  106 us
    ppermute x63, starting transfers between devices, hop(): return lax.ppermute(value, axis, pairs)  74.1 us
    pallas_call x24, Pallas kernels, call(): pl.pallas_call(body, out_shape=out_shape, in_specs=[smem] * n_scalars + [...  73.6 us
    unnamed x63, local copies, waits for them, and re-layouts  14.9 us
  transfers between devices with their start and end apart: 63, of which 24 were waited for; matrix products, arithmetic and copies ran while one was open for 7% of the time, Pallas kernels for 24%

profile of v2, /device:TPU:0, one launch (start us, length us, event | category | flops | bytes accessed | tf_op | source)
XLA Modules:
  0.0 285.8 jit_solution(7207479999410699691)
XLA Ops:
  3.3 4.1 %collective-permute-start = (s32[1,4,128]{2,1,0:T(4,128)S(1)}, s32[1,4,128]{2,1,0:T(4,128)S(1)}, u32[]{:S(2)}, u32[]{:S(2)}) collective-permute-start(s32[1,4,128]{2,1,0:T(4,128)S(1)} %add_bitcast_fusion), channel_id=1, source_target_pairs={{0,16},{4,20},{8,24},{12,28},{16,0},{20,4},{24,8},{28,12},{1,17},{... | collective-permute-start | bytes 6152 | tf_op jit(solution)/shard_map/ppermute | solution.py:508
  8.0 3.3 %copy.22 = bf16[2,64,74,128]{3,2,1,0:T(8,128)(2,1)S(1)} copy(bf16[2,64,74,128]{3,1,2,0:T(8,128)(2,1)} %param.10) | data formatting | bytes 4849664 | tf_op args[3]
  14.1 4.3 %collective-permute-start.4 = (bf16[6,80,128]{2,1,0:T(8,128)(2,1)S(1)}, bf16[6,80,128]{2,1,0:T(8,128)(2,1)S(1)}, u32[]{:S(2)}, u32[]{:S(2)}) collective-permute-start(bf16[6,80,128]{2,1,0:T(8,128)(2,1)S(1)} %get-tuple-element.61), channel_id=1, source_target_pairs={{0,28},{4,24},{8,20},{12,16},{16,12},{20,8},{24,4},{28,0},{1,29},{... | collective-permute-start | bytes 368648 | tf_op jit(solution)/shard_map/ppermute | solution.py:508
  20.5 4.6 %collective-permute-done.2 = s32[4,4,128]{2,1,0:T(4,128)S(1)} collective-permute-done((s32[4,4,128]{2,1,0:T(4,128)S(1)}, s32[4,4,128]{2,1,0:T(4,128)S(1)}, u32[]{:S(2)}, u32[]{:S(2)}) %collective-permute-start.2) | collective-permute-done | bytes 8224 | tf_op jit(solution)/shard_map/ppermute | solution.py:508
  26.9 2.9 %collective-permute-start.20 = (bf16[6,80,128]{2,1,0:T(8,128)(2,1)S(1)}, bf16[6,80,128]{2,1,0:T(8,128)(2,1)S(1)}, u32[]{:S(2)}, u32[]{:S(2)}) collective-permute-start(bf16[6,80,128]{2,1,0:T(8,128)(2,1)S(1)} %get-tuple-element.75), channel_id=1, source_target_pairs={{0,20},{4,16},{8,28},{12,24},{16,4},{20,0},{24,12},{28,8},{1,21},{... | collective-permute-start | bytes 368648 | tf_op jit(solution)/shard_map/ppermute | solution.py:508
  31.5 3.0 %collective-permute-done.19 = bf16[6,80,128]{2,1,0:T(8,128)(2,1)S(1)} collective-permute-done((bf16[6,80,128]{2,1,0:T(8,128)(2,1)S(1)}, bf16[6,80,128]{2,1,0:T(8,128)(2,1)S(1)}, u32[]{:S(2)}, u32[]{:S(2)}) %collective-permute-start.19) | collective-permute-done | bytes 122912 | tf_op jit(solution)/shard_map/ppermute | solution.py:508
  34.5 3.0 %collective-permute-done.20 = bf16[6,80,128]{2,1,0:T(8,128)(2,1)S(1)} collective-permute-done((bf16[6,80,128]{2,1,0:T(8,128)(2,1)S(1)}, bf16[6,80,128]{2,1,0:T(8,128)(2,1)S(1)}, u32[]{:S(2)}, u32[]{:S(2)}) %collective-permute-start.20) | collective-permute-done | bytes 122912 | tf_op jit(solution)/shard_map/ppermute | solution.py:508
  40.6 4.2 %collective-permute-done.21 = bf16[2,6,80,128]{3,2,1,0:T(8,128)(2,1)S(1)} collective-permute-done((bf16[2,6,80,128]{3,2,1,0:T(8,128)(2,1)S(1)}, bf16[2,6,80,128]{3,2,1,0:T(8,128)(2,1)S(1)}, u32[]{:S(2)}, u32[]{:S(2)}) %collective-permute-start.21) | collective-permute-done | bytes 245792 | tf_op jit(solution)/shard_map/ppermute | solution.py:508
  46.9 2.6 spread_blocks.4
  52.1 6.6 %collective-permute-done.8 = bf16[2,6,80,128]{3,2,1,0:T(8,128)(2,1)S(1)} collective-permute-done((bf16[2,6,80,128]{3,2,1,0:T(8,128)(2,1)S(1)}, bf16[2,6,80,128]{3,2,1,0:T(8,128)(2,1)S(1)}, u32[]{:S(2)}, u32[]{:S(2)}) %collective-permute-start.8) | collective-permute-done | bytes 245792 | tf_op jit(solution)/shard_map/ppermute | solution.py:508
  58.8 4.5 %collective-permute-done.17 = bf16[2,6,80,128]{3,2,1,0:T(8,128)(2,1)S(1)} collective-permute-done((bf16[2,6,80,128]{3,2,1,0:T(8,128)(2,1)S(1)}, bf16[2,6,80,128]{3,2,1,0:T(8,128)(2,1)S(1)}, u32[]{:S(2)}, u32[]{:S(2)}) %collective-permute-start.17) | collective-permute-done | bytes 245792 | tf_op jit(solution)/shard_map/ppermute | solution.py:508
  63.4 2.7 spread_blocks.7
  66.4 2.1 collective-permute-done.23.other_ref
  68.7 4.7 %render_blocks.7 = bf16[1408,384]{1,0:T(8,128)(2,1)S(1)} custom-call(s32[1]{0:T(128)} %get-tuple-element.175.count_ref.refs_3_, s32[24]{0:T(128)S(1)} %get-tuple-element.156.block_ref, s32[24]{0:T(128)S(1)} %get-tuple-element.186.place_ref.refs_5_, s32[24]{0:T(128)S(1)} %fusion.9.where_ref.refs_0_, s32[1]{0:T(128)} %get-tuple-element.173.other_count_ref.count_ref, ...), custom_call_target="tpu_custom_call" | custom-call | flops 5000000000 | bytes 10000000 | tf_op jit(solution)/shard_map/render_blocks/pallas_call | solution.py:120
  76.8 2.7 spread_blocks.6
  79.5 7.1 %collective-permute-done.24.other_ref = bf16[12,80,384]{2,1,0:T(8,128)(2,1)S(1)} collective-permute-done((bf16[12,80,384]{2,1,0:T(8,128)(2,1)S(1)}, bf16[12,80,384]{2,1,0:T(8,128)(2,1)S(1)}, u32[]{:S(2)}, u32[]{:S(2)}) %collective-permute-start.24) | collective-permute-done | bytes 737312 | tf_op jit(solution)/shard_map/ppermute | solution.py:508
  87.0 4.8 %render_blocks.6 = bf16[1408,384]{1,0:T(8,128)(2,1)S(1)} custom-call(s32[1]{0:T(128)} %get-tuple-element.176.count_ref.refs_3_, s32[24]{0:T(128)S(1)} %get-tuple-element.157.block_ref, s32[24]{0:T(128)S(1)} %get-tuple-element.185.place_ref.refs_5_, s32[24]{0:T(128)S(1)} %fusion.9.where_ref.refs_0_, s32[1]{0:T(128)} %get-tuple-element.171.other_count_ref.count_ref, ...), custom_call_target="tpu_custom_call" | custom-call | flops 5000000000 | bytes 10000000 | tf_op jit(solution)/shard_map/render_blocks/pallas_call | solution.py:120
  91.8 6.3 %collective-permute-done.27 = bf16[1408,384]{1,0:T(8,128)(2,1)S(1)} collective-permute-done((bf16[1408,384]{1,0:T(8,128)(2,1)S(1)}, bf16[1408,384]{1,0:T(8,128)(2,1)S(1)}, u32[]{:S(2)}, u32[]{:S(2)}) %collective-permute-start.27) | collective-permute-done | bytes 1081376 | tf_op jit(solution)/shard_map/ppermute | solution.py:508
  98.4 4.5 %collective-permute-start.30 = (bf16[1408,384]{1,0:T(8,128)(2,1)S(1)}, bf16[1408,384]{1,0:T(8,128)(2,1)S(1)}, u32[]{:S(2)}, u32[]{:S(2)}) collective-permute-start(bf16[1408,384]{1,0:T(8,128)(2,1)S(1)} %add_convert_fusion), channel_id=1, source_target_pairs={{0,8},{4,12},{24,16},{28,20},{1,9},{5,13},{25,17},{29,21},{2,10},{... | collective-permute-start | bytes 3244040 | tf_op jit(solution)/shard_map/ppermute | solution.py:508
  104.6 2.6 spread_blocks.5
  110.7 4.8 %render_blocks.5 = bf16[1408,384]{1,0:T(8,128)(2,1)S(1)} custom-call(s32[1]{0:T(128)} %get-tuple-element.174.count_ref.refs_6_, s32[24]{0:T(128)S(1)} %get-tuple-element.155.block_ref, s32[24]{0:T(128)S(1)} %get-tuple-element.187.place_ref.refs_8_, s32[24]{0:T(128)S(1)} %fusion.9.where_ref.refs_0_, s32[1]{0:T(128)} %get-tuple-element.170.other_count_ref.count_ref, ...), custom_call_target="tpu_custom_call" | custom-call | flops 5000000000 | bytes 10000000 | tf_op jit(solution)/shard_map/render_blocks/pallas_call | solution.py:120
  115.5 9.6 %collective-permute-done.30 = bf16[1408,384]{1,0:T(8,128)(2,1)S(1)} collective-permute-done((bf16[1408,384]{1,0:T(8,128)(2,1)S(1)}, bf16[1408,384]{1,0:T(8,128)(2,1)S(1)}, u32[]{:S(2)}, u32[]{:S(2)}) %collective-permute-start.30) | collective-permute-done | bytes 1081376 | tf_op jit(solution)/shard_map/ppermute | solution.py:508
  128.1 4.2 %collective-permute-start.29 = (bf16[704,384]{1,0:T(8,128)(2,1)S(1)}, bf16[704,384]{1,0:T(8,128)(2,1)S(1)}, u32[]{:S(2)}, u32[]{:S(2)}) collective-permute-start(bf16[704,384]{1,0:T(8,128)(2,1)S(1)} %get-tuple-element.129), channel_id=1, source_target_pairs={{0,8},{4,12},{8,0},{12,4},{16,24},{20,28},{24,16},{28,20},{1,9},{5... | collective-permute-start | bytes 1622024 | tf_op jit(solution)/shard_map/ppermute | solution.py:508
  134.8 3.8 %collective-permute-start.39 = (bf16[704,384]{1,0:T(8,128)(2,1)S(1)}, bf16[704,384]{1,0:T(8,128)(2,1)S(1)}, u32[]{:S(2)}, u32[]{:S(2)}) collective-permute-start(bf16[704,384]{1,0:T(8,128)(2,1)S(1)} %get-tuple-element.128), channel_id=1, source_target_pairs={{0,8},{4,12},{8,0},{12,4},{16,24},{20,28},{24,16},{28,20},{1,9},{5... | collective-permute-start | bytes 1622024 | tf_op jit(solution)/shard_map/ppermute | solution.py:508
  138.6 4.7 %render_blocks.4.refs_0_ = bf16[1408,384]{1,0:T(8,128)(2,1)S(1)} custom-call(s32[1]{0:T(128)} %get-tuple-element.180.count_ref.refs_1_, s32[24]{0:T(128)S(1)} %get-tuple-element.161.block_ref, s32[24]{0:T(128)S(1)} %get-tuple-element.184.place_ref.refs_3_, s32[24]{0:T(128)S(1)} %fusion.9.where_ref.refs_0_, s32[1]{0:T(128)} %get-tuple-element.172.other_count_ref.count_ref, ...), custom_call_target="tpu_custom_call" | custom-call | flops 5000000000 | bytes 10000000 | tf_op jit(solution)/shard_map/render_blocks/pallas_call | solution.py:120
  143.3 2.1 collective-permute-done.29.refs_1_
  147.9 3.4 %collective-permute-done.32.refs_4_ = bf16[176,384]{1,0:T(8,128)(2,1)S(1)} collective-permute-done((bf16[176,384]{1,0:T(8,128)(2,1)S(1)}, bf16[176,384]{1,0:T(8,128)(2,1)S(1)}, u32[]{:S(2)}, u32[]{:S(2)}) %collective-permute-start.32) | collective-permute-done | bytes 135200 | tf_op jit(solution)/shard_map/ppermute | solution.py:508
  153.0 2.8 loss_rows.2
  160.5 2.5 collective-permute-done.36.refs_2_
  163.0 1.9 collective-permute-done.37.refs_3_
  164.9 2.1 collective-permute-start.47
  169.9 2.8 loss_rows.3
  175.3 5.0 %collective-permute-done.45.refs_2_ = bf16[176,384]{1,0:T(8,128)(2,1)S(1)} collective-permute-done((bf16[176,384]{1,0:T(8,128)(2,1)S(1)}, bf16[176,384]{1,0:T(8,128)(2,1)S(1)}, u32[]{:S(2)}, u32[]{:S(2)}) %collective-permute-start.45) | collective-permute-done | bytes 135200 | tf_op jit(solution)/shard_map/ppermute | solution.py:508
  182.4 2.1 collective-permute-start.49
  185.2 3.1 %pick_bands.6 = bf16[12,80,384]{2,1,0:T(8,128)(2,1)} custom-call(s32[1]{0:T(128)} %get-tuple-element.172.other_count_ref.count_ref, s32[24]{0:T(128)S(1)} %get-tuple-element.165.other_place_ref.place_ref, bf16[704,384]{1,0:T(8,128)(2,1)S(1)} %gather_rows.2.rest_0_.refs_10_, bf16[704,384]{1,0:T(8,128)(2,1)S(1)} %gather_rows.3.rest_1_.refs_11_), custom_call_target="tpu_custom_call" | custom-call | flops 1000000000 | bytes 2000000 | tf_op jit(solution)/shard_map/pick_bands/pallas_call | solution.py:120
  190.6 6.7 %collective-permute-done.49.rest_1_.refs_16_ = bf16[704,384]{1,0:T(8,128)(2,1)S(1)} collective-permute-done((bf16[704,384]{1,0:T(8,128)(2,1)S(1)}, bf16[704,384]{1,0:T(8,128)(2,1)S(1)}, u32[]{:S(2)}, u32[]{:S(2)}) %collective-permute-start.49) | collective-permute-done | bytes 540704 | tf_op jit(solution)/shard_map/ppermute | solution.py:508
  208.1 2.5 pick_bands.5
  212.2 9.0 %pull_blocks.4.refs_10_ = f32[65,192,128]{2,1,0:T(8,128)S(1)} custom-call(s32[24]{0:T(128)S(1)} %fusion.9.where_ref.refs_0_, s32[1]{0:T(128)} %get-tuple-element.180.count_ref.refs_1_, s32[24]{0:T(128)S(1)} %get-tuple-element.147.refs_2_, s32[24]{0:T(128)S(1)} %get-tuple-element.184.place_ref.refs_3_, s32[1]{0:T(128)} %get-tuple-element.179.count_ref.refs_4_, ...), custom_call_target="tpu_custom_call" | custom-call | flops 1000000000 | bytes 2000000 | tf_op jit(solution)/shard_map/pull_blocks/pallas_call | solution.py:120
  224.3 7.3 %collective-permute-done.52 = bf16[1408,384]{1,0:T(8,128)(2,1)} collective-permute-done((bf16[1408,384]{1,0:T(8,128)(2,1)}, bf16[1408,384]{1,0:T(8,128)(2,1)}, u32[]{:S(2)}, u32[]{:S(2)}) %collective-permute-start.52) | collective-permute-done | bytes 1081376 | tf_op jit(solution)/shard_map/ppermute | solution.py:508
  232.9 2.2 pick_bands.4
  236.6 6.0 %pull_blocks.5.refs_10_ = f32[65,192,128]{2,1,0:T(8,128)S(1)} custom-call(s32[24]{0:T(128)S(1)} %fusion.9.where_ref.refs_0_, s32[1]{0:T(128)} %get-tuple-element.178.count_ref.refs_1_, s32[24]{0:T(128)S(1)} %get-tuple-element.149.refs_2_, s32[1]{0:T(128)} %get-tuple-element.176.count_ref.refs_3_, s32[24]{0:T(128)S(1)} %get-tuple-element.148.refs_4_, ...), custom_call_target="tpu_custom_call" | custom-call | flops 1000000000 | bytes 2000000 | tf_op jit(solution)/shard_map/pull_blocks/pallas_call | solution.py:120
  242.8 11.9 %collective-permute-done.51 = bf16[1408,384]{1,0:T(8,128)(2,1)S(1)} collective-permute-done((bf16[1408,384]{1,0:T(8,128)(2,1)}, bf16[1408,384]{1,0:T(8,128)(2,1)S(1)}, u32[]{:S(2)}, u32[]{:S(2)}) %collective-permute-start.51) | collective-permute-done | bytes 1081376 | tf_op jit(solution)/shard_map/ppermute | solution.py:508
  254.8 2.1 pick_bands.7
  259.4 6.0 %pull_blocks.6.refs_5_ = f32[65,192,128]{2,1,0:T(8,128)S(1)} custom-call(s32[24]{0:T(128)S(1)} %fusion.9.where_ref.refs_0_, s32[1]{0:T(128)} %get-tuple-element.177.count_ref.refs_1_, s32[24]{0:T(128)S(1)} %get-tuple-element.144.refs_2_, s32[1]{0:T(128)} %get-tuple-element.175.count_ref.refs_3_, s32[24]{0:T(128)S(1)} %get-tuple-element.143.refs_4_, ...), custom_call_target="tpu_custom_call" | custom-call | flops 1000000000 | bytes 2000000 | tf_op jit(solution)/shard_map/pull_blocks/pallas_call | solution.py:120
  265.5 2.6 copy-done.1
  268.9 7.8 %collective-permute-done.62 = bf16[96,768]{1,0:T(8,128)(2,1)S(1)} collective-permute-done((bf16[96,768]{1,0:T(8,128)(2,1)S(1)}, bf16[96,768]{1,0:T(8,128)(2,1)S(1)}, u32[]{:S(2)}, u32[]{:S(2)}) %collective-permute-start.62) | collective-permute-done | bytes 147488 | tf_op jit(solution)/shard_map/ppermute | solution.py:508
  277.6 2.8 copy-done.2
  280.4 5.4 %pull_blocks.7 = bf16[64,192,128]{2,1,0:T(8,128)(2,1)} custom-call(s32[24]{0:T(128)S(1)} %fusion.9.where_ref.refs_0_, s32[1]{0:T(128)} %get-tuple-element.181.count_ref.refs_1_, s32[24]{0:T(128)S(1)} %copy-done.15, bf16[24,80,128]{2,1,0:T(8,128)(2,1)S(1)} %get-tuple-element.135.weight_ref.refs_3_, bf16[12,80,384]{2,1,0:T(8,128)(2,1)S(1)} %collective-permute-done.56.refs_4_, ...), custom_call_target="tpu_custom_call" | custom-call | flops 1000000000 | bytes 2000000 | tf_op jit(solution)/shard_map/pull_blocks/pallas_call | solution.py:120
  (237 shorter events, 76.7 us)
Async XLA Ops:
  3.3 7.9 %collective-permute-start = (s32[1,4,128]{2,1,0:T(4,128)S(1)}, s32[1,4,128]{2,1,0:T(4,128)S(1)}, u32[]{:S(2)}, u32[]{:S(2)}) collective-permute-start(s32[1,4,128]{2,1,0:T(4,128)S(1)} %add_bitcast_fusion), channel_id=1, source_target_pairs={{0,16},{4,20},{8,24},{12,28},{16,0},{20,4},{24,8},{28,12},{1,17},{... | collective-permute-start | bytes 6152 | tf_op jit(solution)/shard_map/ppermute | solution.py:508
  11.3 7.7 %collective-permute-start.1 = (s32[2,4,128]{2,1,0:T(4,128)S(1)}, s32[2,4,128]{2,1,0:T(4,128)S(1)}, u32[]{:S(2)}, u32[]{:S(2)}) collective-permute-start(s32[2,4,128]{2,1,0:T(4,128)S(1)} %pad_add_fusion.2), channel_id=1, source_target_pairs={{0,8},{4,12},{8,0},{12,4},{16,24},{20,28},{24,16},{28,20},{1,9},{5... | collective-permute-start | bytes 12296 | tf_op jit(solution)/shard_map/ppermute | solution.py:508
  13.5 13.4 %collective-permute-start.3 = (bf16[6,80,128]{2,1,0:T(8,128)(2,1)S(1)}, bf16[6,80,128]{2,1,0:T(8,128)(2,1)S(1)}, u32[]{:S(2)}, u32[]{:S(2)}) collective-permute-start(bf16[6,80,128]{2,1,0:T(8,128)(2,1)S(1)} %get-tuple-element.60), channel_id=1, source_target_pairs={{0,24},{4,28},{8,16},{12,20},{16,8},{20,12},{24,0},{28,4},{1,25},{... | collective-permute-start | bytes 368648 | tf_op jit(solution)/shard_map/ppermute | solution.py:508
  14.1 15.8 %collective-permute-start.4 = (bf16[6,80,128]{2,1,0:T(8,128)(2,1)S(1)}, bf16[6,80,128]{2,1,0:T(8,128)(2,1)S(1)}, u32[]{:S(2)}, u32[]{:S(2)}) collective-permute-start(bf16[6,80,128]{2,1,0:T(8,128)(2,1)S(1)} %get-tuple-element.61), channel_id=1, source_target_pairs={{0,28},{4,24},{8,20},{12,16},{16,12},{20,8},{24,4},{28,0},{1,29},{... | collective-permute-start | bytes 368648 | tf_op jit(solution)/shard_map/ppermute | solution.py:508
  18.4 22.2 %collective-permute-start.7 = (bf16[6,80,128]{2,1,0:T(8,128)(2,1)S(1)}, bf16[6,80,128]{2,1,0:T(8,128)(2,1)S(1)}, u32[]{:S(2)}, u32[]{:S(2)}) collective-permute-start(bf16[6,80,128]{2,1,0:T(8,128)(2,1)S(1)} %get-tuple-element.63), channel_id=1, source_target_pairs={{0,4},{4,0},{8,12},{12,8},{16,20},{20,16},{24,28},{28,24},{1,5},{5... | collective-permute-start | bytes 368648 | tf_op jit(solution)/shard_map/ppermute | solution.py:508
  18.9 26.0 %collective-permute-start.15 = (bf16[6,80,128]{2,1,0:T(8,128)(2,1)S(1)}, bf16[6,80,128]{2,1,0:T(8,128)(2,1)S(1)}, u32[]{:S(2)}, u32[]{:S(2)}) collective-permute-start(bf16[6,80,128]{2,1,0:T(8,128)(2,1)S(1)} %get-tuple-element.71), channel_id=1, source_target_pairs={{0,8},{4,12},{8,0},{12,4},{16,24},{20,28},{24,16},{28,20},{1,9},{5... | collective-permute-start | bytes 368648 | tf_op jit(solution)/shard_map/ppermute | solution.py:508
  25.1 9.4 %collective-permute-start.19 = (bf16[6,80,128]{2,1,0:T(8,128)(2,1)S(1)}, bf16[6,80,128]{2,1,0:T(8,128)(2,1)S(1)}, u32[]{:S(2)}, u32[]{:S(2)}) collective-permute-start(bf16[6,80,128]{2,1,0:T(8,128)(2,1)S(1)} %get-tuple-element.74), channel_id=1, source_target_pairs={{0,16},{4,20},{8,24},{12,28},{16,0},{20,4},{24,8},{28,12},{1,17},{... | collective-permute-start | bytes 368648 | tf_op jit(solution)/shard_map/ppermute | solution.py:508
  26.9 10.5 %collective-permute-start.20 = (bf16[6,80,128]{2,1,0:T(8,128)(2,1)S(1)}, bf16[6,80,128]{2,1,0:T(8,128)(2,1)S(1)}, u32[]{:S(2)}, u32[]{:S(2)}) collective-permute-start(bf16[6,80,128]{2,1,0:T(8,128)(2,1)S(1)} %get-tuple-element.75), channel_id=1, source_target_pairs={{0,20},{4,16},{8,28},{12,24},{16,4},{20,0},{24,12},{28,8},{1,21},{... | collective-permute-start | bytes 368648 | tf_op jit(solution)/shard_map/ppermute | solution.py:508
  29.9 9.2 %collective-permute-start.5 = (bf16[2,6,80,128]{3,2,1,0:T(8,128)(2,1)S(1)}, bf16[2,6,80,128]{3,2,1,0:T(8,128)(2,1)S(1)}, u32[]{:S(2)}, u32[]{:S(2)}) collective-permute-start(bf16[2,6,80,128]{3,2,1,0:T(8,128)(2,1)S(1)} %pad_maximum_fusion.8), channel_id=1, source_target_pairs={{0,2},{1,3},{2,0},{3,1},{4,6},{5,7},{6,4},{7,5},{8,10},{9,11},{10,... | collective-permute-start | bytes 737288 | tf_op jit(solution)/shard_map/ppermute | solution.py:508
  34.5 10.5 %collective-permute-start.16 = (bf16[6,80,128]{2,1,0:T(8,128)(2,1)S(1)}, bf16[6,80,128]{2,1,0:T(8,128)(2,1)S(1)}, u32[]{:S(2)}, u32[]{:S(2)}) collective-permute-start(bf16[6,80,128]{2,1,0:T(8,128)(2,1)S(1)} %get-tuple-element.72), channel_id=1, source_target_pairs={{0,12},{4,8},{8,4},{12,0},{16,28},{20,24},{24,20},{28,16},{1,13},{... | collective-permute-start | bytes 368648 | tf_op jit(solution)/shard_map/ppermute | solution.py:508
  49.5 18.9 %collective-permute-start.23 = (bf16[12,80,384]{2,1,0:T(8,128)(2,1)S(1)}, bf16[12,80,384]{2,1,0:T(8,128)(2,1)S(1)}, u32[]{:S(2)}, u32[]{:S(2)}) collective-permute-start(bf16[12,80,384]{2,1,0:T(8,128)(2,1)S(1)} %spread_blocks.4), channel_id=1, source_target_pairs={{0,4},{4,0},{8,12},{12,8},{16,20},{20,16},{24,28},{28,24},{1,5},{5... | collective-permute-start | bytes 2211848 | tf_op jit(solution)/shard_map/ppermute | solution.py:508
  49.8 8.8 %collective-permute-start.8 = (bf16[2,6,80,128]{3,2,1,0:T(8,128)(2,1)S(1)}, bf16[2,6,80,128]{3,2,1,0:T(8,128)(2,1)S(1)}, u32[]{:S(2)}, u32[]{:S(2)}) collective-permute-start(bf16[2,6,80,128]{3,2,1,0:T(8,128)(2,1)S(1)} %pad_maximum_fusion.9), channel_id=1, source_target_pairs={{0,2},{1,3},{2,0},{3,1},{4,6},{5,7},{6,4},{7,5},{8,10},{9,11},{10,... | collective-permute-start | bytes 737288 | tf_op jit(solution)/shard_map/ppermute | solution.py:508
  51.3 11.9 %collective-permute-start.17 = (bf16[2,6,80,128]{3,2,1,0:T(8,128)(2,1)S(1)}, bf16[2,6,80,128]{3,2,1,0:T(8,128)(2,1)S(1)}, u32[]{:S(2)}, u32[]{:S(2)}) collective-permute-start(bf16[2,6,80,128]{3,2,1,0:T(8,128)(2,1)S(1)} %pad_maximum_fusion.10), channel_id=1, source_target_pairs={{0,2},{1,3},{2,0},{3,1},{4,6},{5,7},{6,4},{7,5},{8,10},{9,11},{10,... | collective-permute-start | bytes 737288 | tf_op jit(solution)/shard_map/ppermute | solution.py:508
  68.4 18.1 %collective-permute-start.24 = (bf16[12,80,384]{2,1,0:T(8,128)(2,1)S(1)}, bf16[12,80,384]{2,1,0:T(8,128)(2,1)S(1)}, u32[]{:S(2)}, u32[]{:S(2)}) collective-permute-start(bf16[12,80,384]{2,1,0:T(8,128)(2,1)S(1)} %spread_blocks.7), channel_id=1, source_target_pairs={{0,4},{4,0},{8,12},{12,8},{16,20},{20,16},{24,28},{28,24},{1,5},{5... | collective-permute-start | bytes 2211848 | tf_op jit(solution)/shard_map/ppermute | solution.py:508
  73.5 24.6 %collective-permute-start.27 = (bf16[1408,384]{1,0:T(8,128)(2,1)S(1)}, bf16[1408,384]{1,0:T(8,128)(2,1)S(1)}, u32[]{:S(2)}, u32[]{:S(2)}) collective-permute-start(bf16[1408,384]{1,0:T(8,128)(2,1)S(1)} %render_blocks.7), channel_id=1, source_target_pairs={{0,8},{4,12},{24,16},{28,20},{1,9},{5,13},{25,17},{29,21},{2,10},{... | collective-permute-start | bytes 3244040 | tf_op jit(solution)/shard_map/ppermute | solution.py:508
  75.1 32.2 %collective-permute-start.10 = (bf16[192,768]{1,0:T(8,128)(2,1)S(1)}, bf16[192,768]{1,0:T(8,128)(2,1)S(1)}, u32[]{:S(2)}, u32[]{:S(2)}) collective-permute-start(bf16[192,768]{1,0:T(8,128)(2,1)S(1)} %copy-done.24), channel_id=1, source_target_pairs={{0,2},{1,3},{2,0},{3,1},{4,6},{5,7},{6,4},{7,5},{8,10},{9,11},{10,... | collective-permute-start | bytes 884744 | tf_op jit(solution)/shard_map/ppermute | solution.py:508
  86.5 22.4 %collective-permute-start.25 = (bf16[12,80,384]{2,1,0:T(8,128)(2,1)S(1)}, bf16[12,80,384]{2,1,0:T(8,128)(2,1)S(1)}, u32[]{:S(2)}, u32[]{:S(2)}) collective-permute-start(bf16[12,80,384]{2,1,0:T(8,128)(2,1)S(1)} %spread_blocks.6), channel_id=1, source_target_pairs={{0,4},{4,0},{8,12},{12,8},{16,20},{20,16},{24,28},{28,24},{1,5},{5... | collective-permute-start | bytes 2211848 | tf_op jit(solution)/shard_map/ppermute | solution.py:508
  98.4 26.7 %collective-permute-start.30 = (bf16[1408,384]{1,0:T(8,128)(2,1)S(1)}, bf16[1408,384]{1,0:T(8,128)(2,1)S(1)}, u32[]{:S(2)}, u32[]{:S(2)}) collective-permute-start(bf16[1408,384]{1,0:T(8,128)(2,1)S(1)} %add_convert_fusion), channel_id=1, source_target_pairs={{0,8},{4,12},{24,16},{28,20},{1,9},{5,13},{25,17},{29,21},{2,10},{... | collective-permute-start | bytes 3244040 | tf_op jit(solution)/shard_map/ppermute | solution.py:508
  103.7 21.7 %collective-permute-start.28 = (bf16[1408,384]{1,0:T(8,128)(2,1)S(1)}, bf16[1408,384]{1,0:T(8,128)(2,1)S(1)}, u32[]{:S(2)}, u32[]{:S(2)}) collective-permute-start(bf16[1408,384]{1,0:T(8,128)(2,1)S(1)} %add_convert_fusion), channel_id=1, source_target_pairs={{8,16},{12,20},{16,8},{20,12},{9,17},{13,21},{17,9},{21,13},{10,18... | collective-permute-start | bytes 3244040 | tf_op jit(solution)/shard_map/ppermute | solution.py:508
  104.5 22.9 %collective-permute-start.12 = (bf16[2,176,384]{2,1,0:T(8,128)(2,1)S(1)}, bf16[2,176,384]{2,1,0:T(8,128)(2,1)S(1)}, u32[]{:S(2)}, u32[]{:S(2)}) collective-permute-start(bf16[2,176,384]{2,1,0:T(8,128)(2,1)S(1)} %get-tuple-element.68), channel_id=1, source_target_pairs={{0,1},{1,0},{2,3},{3,2},{4,5},{5,4},{6,7},{7,6},{8,9},{9,8},{10,11... | collective-permute-start | bytes 811016 | tf_op jit(solution)/shard_map/ppermute | solution.py:508
  107.3 20.8 %collective-permute-start.13 = (bf16[2,176,384]{2,1,0:T(8,128)(2,1)S(1)}, bf16[2,176,384]{2,1,0:T(8,128)(2,1)S(1)}, u32[]{:S(2)}, u32[]{:S(2)}) collective-permute-start(bf16[2,176,384]{2,1,0:T(8,128)(2,1)S(1)} %get-tuple-element.69), channel_id=1, source_target_pairs={{0,2},{1,3},{2,0},{3,1},{4,6},{5,7},{6,4},{7,5},{8,10},{9,11},{10,... | collective-permute-start | bytes 811016 | tf_op jit(solution)/shard_map/ppermute | solution.py:508
  108.9 25.9 %collective-permute-start.26 = (bf16[12,80,384]{2,1,0:T(8,128)(2,1)S(1)}, bf16[12,80,384]{2,1,0:T(8,128)(2,1)S(1)}, u32[]{:S(2)}, u32[]{:S(2)}) collective-permute-start(bf16[12,80,384]{2,1,0:T(8,128)(2,1)S(1)} %spread_blocks.5), channel_id=1, source_target_pairs={{0,4},{4,0},{8,12},{12,8},{16,20},{20,16},{24,28},{28,24},{1,5},{5... | collective-permute-start | bytes 2211848 | tf_op jit(solution)/shard_map/ppermute | solution.py:508
  125.1 8.8 %collective-permute-start.14 = (bf16[2,176,384]{2,1,0:T(8,128)(2,1)S(1)}, bf16[2,176,384]{2,1,0:T(8,128)(2,1)S(1)}, u32[]{:S(2)}, u32[]{:S(2)}) collective-permute-start(bf16[2,176,384]{2,1,0:T(8,128)(2,1)S(1)} %get-tuple-element.70), channel_id=1, source_target_pairs={{0,3},{1,2},{2,1},{3,0},{4,7},{5,6},{6,5},{7,4},{8,11},{9,10},{10,... | collective-permute-start | bytes 811016 | tf_op jit(solution)/shard_map/ppermute | solution.py:508
  125.4 21.7 %collective-permute-start.11 = (bf16[384,768]{1,0:T(8,128)(2,1)S(1)}, bf16[384,768]{1,0:T(8,128)(2,1)S(1)}, u32[]{:S(2)}, u32[]{:S(2)}) collective-permute-start(bf16[384,768]{1,0:T(8,128)(2,1)S(1)} %pad_maximum_fusion.3), channel_id=1, source_target_pairs={{0,1},{1,0},{2,3},{3,2},{4,5},{5,4},{6,7},{7,6},{8,9},{9,8},{10,11... | collective-permute-start | bytes 1769480 | tf_op jit(solution)/shard_map/ppermute | solution.py:508
  127.4 15.9 %collective-permute-start.31 = (bf16[704,384]{1,0:T(8,128)(2,1)S(1)}, bf16[704,384]{1,0:T(8,128)(2,1)S(1)}, u32[]{:S(2)}, u32[]{:S(2)}) collective-permute-start(bf16[704,384]{1,0:T(8,128)(2,1)S(1)} %get-tuple-element.127), channel_id=1, source_target_pairs={{8,16},{12,20},{16,8},{20,12},{9,17},{13,21},{17,9},{21,13},{10,18... | collective-permute-start | bytes 1622024 | tf_op jit(solution)/shard_map/ppermute | solution.py:508
  128.1 17.3 %collective-permute-start.29 = (bf16[704,384]{1,0:T(8,128)(2,1)S(1)}, bf16[704,384]{1,0:T(8,128)(2,1)S(1)}, u32[]{:S(2)}, u32[]{:S(2)}) collective-permute-start(bf16[704,384]{1,0:T(8,128)(2,1)S(1)} %get-tuple-element.129), channel_id=1, source_target_pairs={{0,8},{4,12},{8,0},{12,4},{16,24},{20,28},{24,16},{28,20},{1,9},{5... | collective-permute-start | bytes 1622024 | tf_op jit(solution)/shard_map/ppermute | solution.py:508
  134.1 24.0 %collective-permute-start.40 = (bf16[704,384]{1,0:T(8,128)(2,1)S(1)}, bf16[704,384]{1,0:T(8,128)(2,1)S(1)}, u32[]{:S(2)}, u32[]{:S(2)}) collective-permute-start(bf16[704,384]{1,0:T(8,128)(2,1)S(1)} %get-tuple-element.126), channel_id=1, source_target_pairs={{8,16},{12,20},{16,8},{20,12},{9,17},{13,21},{17,9},{21,13},{10,18... | collective-permute-start | bytes 1622024 | tf_op jit(solution)/shard_map/ppermute | solution.py:508
  134.8 23.3 %collective-permute-start.39 = (bf16[704,384]{1,0:T(8,128)(2,1)S(1)}, bf16[704,384]{1,0:T(8,128)(2,1)S(1)}, u32[]{:S(2)}, u32[]{:S(2)}) collective-permute-start(bf16[704,384]{1,0:T(8,128)(2,1)S(1)} %get-tuple-element.128), channel_id=1, source_target_pairs={{0,8},{4,12},{8,0},{12,4},{16,24},{20,28},{24,16},{28,20},{1,9},{5... | collective-permute-start | bytes 1622024 | tf_op jit(solution)/shard_map/ppermute | solution.py:508
  158.3 10.5 %collective-permute-start.41 = (bf16[176,384]{1,0:T(8,128)(2,1)S(1)}, bf16[176,384]{1,0:T(8,128)(2,1)S(1)}, u32[]{:S(2)}, u32[]{:S(2)}) collective-permute-start(bf16[176,384]{1,0:T(8,128)(2,1)S(1)} %get-tuple-element.89), channel_id=1, source_target_pairs={{0,2},{1,3},{2,0},{3,1},{4,6},{5,7},{6,4},{7,5},{8,10},{9,11},{10,... | collective-permute-start | bytes 405512 | tf_op jit(solution)/shard_map/ppermute | solution.py:508
  159.7 9.1 %collective-permute-start.42 = (bf16[176,384]{1,0:T(8,128)(2,1)S(1)}, bf16[176,384]{1,0:T(8,128)(2,1)S(1)}, u32[]{:S(2)}, u32[]{:S(2)}) collective-permute-start(bf16[176,384]{1,0:T(8,128)(2,1)S(1)} %get-tuple-element.90), channel_id=1, source_target_pairs={{0,1},{1,0},{2,3},{3,2},{4,5},{5,4},{6,7},{7,6},{8,9},{9,8},{10,11... | collective-permute-start | bytes 405512 | tf_op jit(solution)/shard_map/ppermute | solution.py:508
  160.2 9.7 %collective-permute-start.43 = (bf16[176,384]{1,0:T(8,128)(2,1)S(1)}, bf16[176,384]{1,0:T(8,128)(2,1)S(1)}, u32[]{:S(2)}, u32[]{:S(2)}) collective-permute-start(bf16[176,384]{1,0:T(8,128)(2,1)S(1)} %get-tuple-element.91), channel_id=1, source_target_pairs={{0,3},{1,2},{2,1},{3,0},{4,7},{5,6},{6,5},{7,4},{8,11},{9,10},{10,... | collective-permute-start | bytes 405512 | tf_op jit(solution)/shard_map/ppermute | solution.py:508
  164.9 16.4 %collective-permute-start.47 = (bf16[704,384]{1,0:T(8,128)(2,1)S(1)}, bf16[704,384]{1,0:T(8,128)(2,1)S(1)}, u32[]{:S(2)}, u32[]{:S(2)}) collective-permute-start(bf16[704,384]{1,0:T(8,128)(2,1)S(1)} %gather_rows.2.rest_0_.refs_10_), channel_id=1, source_target_pairs={{0,8},{4,12},{8,0},{12,4},{16,24},{20,28},{24,16},{28,20},{1,9},{5... | collective-permute-start | bytes 1622024 | tf_op jit(solution)/shard_map/ppermute | solution.py:508
  167.1 14.3 %collective-permute-start.38 = (bf16[704,384]{1,0:T(8,128)(2,1)S(1)}, bf16[704,384]{1,0:T(8,128)(2,1)S(1)}, u32[]{:S(2)}, u32[]{:S(2)}) collective-permute-start(bf16[704,384]{1,0:T(8,128)(2,1)S(1)} %gather_rows.2.rest_0_.refs_10_), channel_id=1, source_target_pairs={{8,16},{12,20},{16,8},{20,12},{9,17},{13,21},{17,9},{21,13},{10,18... | collective-permute-start | bytes 1622024 | tf_op jit(solution)/shard_map/ppermute | solution.py:508
  181.6 21.1 %collective-permute-start.57 = (f32[2,192,768]{2,1,0:T(8,128)S(1)}, f32[2,192,768]{2,1,0:T(8,128)S(1)}, u32[]{:S(2)}, u32[]{:S(2)}) collective-permute-start(f32[2,192,768]{2,1,0:T(8,128)S(1)} %bitcast.115), channel_id=1, source_target_pairs={{0,1},{1,0},{2,3},{3,2},{4,5},{5,4},{6,7},{7,6},{8,9},{9,8},{10,11... | collective-permute-start | bytes 3538952 | tf_op jit(solution)/shard_map/ppermute | solution.py:508
  182.4 14.8 %collective-permute-start.49 = (bf16[704,384]{1,0:T(8,128)(2,1)S(1)}, bf16[704,384]{1,0:T(8,128)(2,1)S(1)}, u32[]{:S(2)}, u32[]{:S(2)}) collective-permute-start(bf16[704,384]{1,0:T(8,128)(2,1)S(1)} %gather_rows.3.rest_1_.refs_11_), channel_id=1, source_target_pairs={{0,8},{4,12},{8,0},{12,4},{16,24},{20,28},{24,16},{28,20},{1,9},{5... | collective-permute-start | bytes 1622024 | tf_op jit(solution)/shard_map/ppermute | solution.py:508
  184.4 16.2 %collective-permute-start.48 = (bf16[704,384]{1,0:T(8,128)(2,1)S(1)}, bf16[704,384]{1,0:T(8,128)(2,1)S(1)}, u32[]{:S(2)}, u32[]{:S(2)}) collective-permute-start(bf16[704,384]{1,0:T(8,128)(2,1)S(1)} %gather_rows.3.rest_1_.refs_11_), channel_id=1, source_target_pairs={{8,16},{12,20},{16,8},{20,12},{9,17},{13,21},{17,9},{21,13},{10,18... | collective-permute-start | bytes 1622024 | tf_op jit(solution)/shard_map/ppermute | solution.py:508
  188.3 22.3 %collective-permute-start.53 = (bf16[12,80,384]{2,1,0:T(8,128)(2,1)}, bf16[12,80,384]{2,1,0:T(8,128)(2,1)}, u32[]{:S(2)}, u32[]{:S(2)}) collective-permute-start(bf16[12,80,384]{2,1,0:T(8,128)(2,1)} %pick_bands.6), channel_id=1, source_target_pairs={{0,4},{4,0},{8,12},{12,8},{16,20},{20,16},{24,28},{28,24},{1,5},{5... | collective-permute-start | bytes 2211848 | tf_op jit(solution)/shard_map/ppermute | solution.py:508
  198.1 23.1 %collective-permute-start.50 = (bf16[1408,384]{1,0:T(8,128)(2,1)}, bf16[1408,384]{1,0:T(8,128)(2,1)}, u32[]{:S(2)}, u32[]{:S(2)}) collective-permute-start(bf16[1408,384]{1,0:T(8,128)(2,1)} %constant_dynamic-update-slice_fusion.11), channel_id=1, source_target_pairs={{8,16},{12,20},{16,8},{20,12},{9,17},{13,21},{17,9},{21,13},{10,18... | collective-permute-start | bytes 3244040 | tf_op jit(solution)/shard_map/ppermute | solution.py:508
  201.5 30.1 %collective-permute-start.52 = (bf16[1408,384]{1,0:T(8,128)(2,1)}, bf16[1408,384]{1,0:T(8,128)(2,1)}, u32[]{:S(2)}, u32[]{:S(2)}) collective-permute-start(bf16[1408,384]{1,0:T(8,128)(2,1)} %constant_dynamic-update-slice_fusion.9), channel_id=1, source_target_pairs={{8,0},{12,4},{16,24},{20,28},{9,1},{13,5},{17,25},{21,29},{10,2},{... | collective-permute-start | bytes 3244040 | tf_op jit(solution)/shard_map/ppermute | solution.py:508
  204.8 17.7 %collective-permute-start.58 = (f32[192,768]{1,0:T(8,128)}, f32[192,768]{1,0:T(8,128)}, u32[]{:S(2)}, u32[]{:S(2)}) collective-permute-start(f32[192,768]{1,0:T(8,128)} %slice_bitcast_fusion), channel_id=1, source_target_pairs={{0,2},{1,3},{2,0},{3,1},{4,6},{5,7},{6,4},{7,5},{8,10},{9,11},{10,... | collective-permute-start | bytes 1769480 | tf_op jit(solution)/shard_map/ppermute | solution.py:508
  210.6 24.6 %collective-permute-start.54 = (bf16[12,80,384]{2,1,0:T(8,128)(2,1)S(1)}, bf16[12,80,384]{2,1,0:T(8,128)(2,1)S(1)}, u32[]{:S(2)}, u32[]{:S(2)}) collective-permute-start(bf16[12,80,384]{2,1,0:T(8,128)(2,1)S(1)} %pick_bands.5), channel_id=1, source_target_pairs={{0,4},{4,0},{8,12},{12,8},{16,20},{20,16},{24,28},{28,24},{1,5},{5... | collective-permute-start | bytes 2211848 | tf_op jit(solution)/shard_map/ppermute | solution.py:508
  221.2 33.4 %collective-permute-start.51 = (bf16[1408,384]{1,0:T(8,128)(2,1)}, bf16[1408,384]{1,0:T(8,128)(2,1)S(1)}, u32[]{:S(2)}, u32[]{:S(2)}) collective-permute-start(bf16[1408,384]{1,0:T(8,128)(2,1)} %collective-permute-done.50), channel_id=1, source_target_pairs={{8,0},{12,4},{16,24},{20,28},{9,1},{13,5},{17,25},{21,29},{10,2},{... | collective-permute-start | bytes 3244040 | tf_op jit(solution)/shard_map/ppermute | solution.py:508
  223.7 18.9 %collective-permute-start.59 = (f32[96,768]{1,0:T(8,128)S(1)}, f32[96,768]{1,0:T(8,128)S(1)}, u32[]{:S(2)}, u32[]{:S(2)}) collective-permute-start(f32[96,768]{1,0:T(8,128)S(1)} %constant_dynamic-slice_fusion), channel_id=1, source_target_pairs={{0,4},{4,0},{8,12},{12,8},{16,20},{20,16},{24,28},{28,24},{1,5},{5... | collective-permute-start | bytes 884744 | tf_op jit(solution)/shard_map/ppermute | solution.py:508
  235.2 21.7 %collective-permute-start.55 = (bf16[12,80,384]{2,1,0:T(8,128)(2,1)S(1)}, bf16[12,80,384]{2,1,0:T(8,128)(2,1)S(1)}, u32[]{:S(2)}, u32[]{:S(2)}) collective-permute-start(bf16[12,80,384]{2,1,0:T(8,128)(2,1)S(1)} %pick_bands.4), channel_id=1, source_target_pairs={{0,4},{4,0},{8,12},{12,8},{16,20},{20,16},{24,28},{28,24},{1,5},{5... | collective-permute-start | bytes 2211848 | tf_op jit(solution)/shard_map/ppermute | solution.py:508
  242.7 14.2 %collective-permute-start.60 = (bf16[96,768]{1,0:T(8,128)(2,1)S(1)}, bf16[96,768]{1,0:T(8,128)(2,1)S(1)}, u32[]{:S(2)}, u32[]{:S(2)}) collective-permute-start(bf16[96,768]{1,0:T(8,128)(2,1)S(1)} %get-tuple-element.122), channel_id=1, source_target_pairs={{0,8},{4,12},{8,0},{12,4},{16,24},{20,28},{24,16},{28,20},{1,9},{5... | collective-permute-start | bytes 442376 | tf_op jit(solution)/shard_map/ppermute | solution.py:508
  256.9 20.8 %collective-permute-start.56 = (bf16[12,80,384]{2,1,0:T(8,128)(2,1)S(1)}, bf16[12,80,384]{2,1,0:T(8,128)(2,1)S(1)}, u32[]{:S(2)}, u32[]{:S(2)}) collective-permute-start(bf16[12,80,384]{2,1,0:T(8,128)(2,1)S(1)} %pick_bands.7), channel_id=1, source_target_pairs={{0,4},{4,0},{8,12},{12,8},{16,20},{20,16},{24,28},{28,24},{1,5},{5... | collective-permute-start | bytes 2211848 | tf_op jit(solution)/shard_map/ppermute | solution.py:508
  258.5 9.7 %collective-permute-start.61 = (bf16[96,768]{1,0:T(8,128)(2,1)S(1)}, bf16[96,768]{1,0:T(8,128)(2,1)S(1)}, u32[]{:S(2)}, u32[]{:S(2)}) collective-permute-start(bf16[96,768]{1,0:T(8,128)(2,1)S(1)} %fusion.1), channel_id=1, source_target_pairs={{0,16},{4,20},{8,24},{12,28},{16,0},{20,4},{24,8},{28,12},{1,17},{... | collective-permute-start | bytes 442376 | tf_op jit(solution)/shard_map/ppermute | solution.py:508
  268.2 8.5 %collective-permute-start.62 = (bf16[96,768]{1,0:T(8,128)(2,1)S(1)}, bf16[96,768]{1,0:T(8,128)(2,1)S(1)}, u32[]{:S(2)}, u32[]{:S(2)}) collective-permute-start(bf16[96,768]{1,0:T(8,128)(2,1)S(1)} %get-tuple-element.120), channel_id=1, source_target_pairs={{0,4},{4,0},{8,12},{12,8},{16,20},{20,16},{24,28},{28,24},{1,5},{5... | collective-permute-start | bytes 442376 | tf_op jit(solution)/shard_map/ppermute | solution.py:508
  (41 other events, 563.9 us)

commit v3 on v2

--- a/solution.py
+++ b/solution.py
@@ -362,7 +362,7 @@
     return call(body, out, tuple(tables + arrays), len(tables), us, "pull_blocks", scratch, 24)
 
 
-def loss_kernel(u, teacher_width, side_ref, head_ref, teacher_ref, *rest):
+def loss_kernel(u, teacher_width, half_rows, side_ref, head_ref, teacher_ref, *rest):
     parts_refs, image_refs, grad_ref = rest[0:4], rest[-5:-1], rest[-1]
     rows, packed = parts_refs[0].shape
     width = packed // 2
@@ -379,6 +379,8 @@
 
     halves = halves_of([ref[...] for ref in parts_refs])
     targets = halves_of([teacher_ref[side_ref[0] ^ g, u] for g in range(4)])
+    twice = side_ref[0] * rows - first_row(side_ref[0], half_rows, 4)
+    counted = lax.broadcasted_iota(jnp.int32, (rows, 1), 0) >= twice
     rendered_all, grad_all, images = [], [], []
     for half in range(2):
         rendered = halves[half].astype(jnp.bfloat16)
@@ -392,7 +394,7 @@
         images.append(
             lax.dot_general(grad_proj, head, (((1,), (1,)), ((), ())), preferred_element_type=jnp.float32)
         )
-        rendered_all.append(rendered)
+        rendered_all.append(jnp.where(counted, rendered, jnp.zeros_like(rendered)))
         grad_all.append(grad_proj)
     for pair in range(2):
         cols = slice(2 * pair * width, 2 * (pair + 1) * width)
@@ -410,22 +412,31 @@
     grad_ref[...] = grad if len(rest) == 9 else grad + rest[4][...]
 
 
-def loss(u, side, parts, head, teacher, grad):
+def loss(u, side, parts, head, teacher, grad, half_rows):
     teacher_width = head.shape[1]
     outs = [jax.ShapeDtypeStruct(parts[0].shape, jnp.bfloat16)] * len(parts)
     outs += [jax.ShapeDtypeStruct(head.shape, jnp.float32)]
-    body = lambda *refs: loss_kernel(u, teacher_width, *refs)
+    body = lambda *refs: loss_kernel(u, teacher_width, half_rows, *refs)
     args = (side, head, teacher) + tuple(parts) + (() if grad is None else (grad,))
     *images, grad = call(body, outs, args, 1, 3, "loss_rows", (), 20)
     return images, grad
 
 
+def share_of(half_rows, sides):
+    return -(-half_rows // (16 * sides)) * 16
+
+
+def first_row(side, half_rows, sides):
+    rows = share_of(half_rows, sides)
+    return jnp.minimum(side * rows, half_rows - rows)
+
+
 def deal(side, terms, starts, sides, half_rows):
-    rows = half_rows // sides
+    rows = share_of(half_rows, sides)
 
     def body(side_ref, *refs):
         for d in range(sides):
-            here = (side_ref[0] ^ d) * rows
+            here = first_row(side_ref[0] ^ d, half_rows, sides)
             value = 0.0
             for ref, start in zip(refs, starts):
                 value = value + ref[pl.ds(pl.multiple_of(start + here, 16), rows), :].astype(jnp.float32)
@@ -435,39 +446,41 @@
     return call(body, [out] * sides, (side,) + tuple(terms), 1, 1, "deal_rows")
 
 
-def gather(side, parts):
+def gather(side, parts, half_rows):
     rows, lanes = parts[0].shape
 
     def body(side_ref, *refs):
         for d in range(len(parts)):
-            here = pl.ds(pl.multiple_of((side_ref[0] ^ d) * rows, 16), rows)
+            start = first_row(side_ref[0] ^ d, half_rows, len(parts))
+            here = pl.ds(pl.multiple_of(start, 16), rows)
             refs[-1][here, :] = refs[d][...]
 
-    out = jax.ShapeDtypeStruct((rows * len(parts), lanes), jnp.bfloat16)
+    out = jax.ShapeDtypeStruct((half_rows, lanes), jnp.bfloat16)
     return call(body, out, (side,) + tuple(parts), 1, 1, "gather_rows")
 
 
 def turn_teacher(side, teacher, sides, padded):
     views, width, pixels = teacher.shape
     half_rows = padded // 2
-    rows = half_rows // sides
+    rows = share_of(half_rows, sides)
     whole = pixels // 128 * 128
+    lanes = -(-padded // 128) * 128
 
     def body(side_ref, teacher_ref, *rest):
         outs, (across, turned) = rest[:sides], rest[sides:]
         for u in range(views):
-            across[width:, :] = jnp.zeros((256 - width, padded), jnp.float32)
-            across[0:width, whole:] = jnp.zeros((width, padded - whole), jnp.float32)
+            across[width:, :] = jnp.zeros((256 - width, lanes), jnp.float32)
+            across[0:width, whole:] = jnp.zeros((width, lanes - whole), jnp.float32)
             across[0:width, 0:pixels] = teacher_ref[u].astype(jnp.float32)
             turned[...] = across[...].T
             for d in range(sides):
-                start = pl.multiple_of((side_ref[0] ^ d) * rows, 16)
+                start = pl.multiple_of(first_row(side_ref[0] ^ d, half_rows, sides), 16)
                 first = turned[pl.ds(start, rows), :]
                 second = turned[pl.ds(half_rows + start, rows), :]
                 outs[d][u] = beside(first, second).astype(jnp.bfloat16)
 
     out = jax.ShapeDtypeStruct((views, rows, 2 * width), jnp.bfloat16)
-    scratch = [pltpu.VMEM((256, padded), jnp.float32), pltpu.VMEM((padded, 256), jnp.float32)]
+    scratch = [pltpu.VMEM((256, lanes), jnp.float32), pltpu.VMEM((lanes, 256), jnp.float32)]
     return call(body, [out] * sides, (side, teacher), 1, 6, "turn_teacher", scratch)
 
 
@@ -498,9 +511,8 @@
     quarter = -(-capacity // sides)
     slots = quarter * sides
     pixels = teacher.shape[2]
-    unit = 2 * sides * 16
-    padded = -(-pixels // unit) * unit
-    half_rows = padded // 2
+    half_rows = -(-pixels // 32) * 16
+    padded = 2 * half_rows
     me, side = lax.axis_index("view"), lax.axis_index("feat")
     line, across, core = me // 2, side // 2, side % 2
 
@@ -606,13 +618,13 @@
         parts = [swap(parts[d], "feat", d) if d else parts[d] for d in (0, 2, 1, 3)]
         if u:
             parts = after(parts, images[-1])
-        parts, grad = loss(u, side_id, parts, head, target, grad)
+        parts, grad = loss(u, side_id, parts, head, target, grad, half_rows)
         held = parts[0]
         parts = [swap(part, "feat", d) if d else part for d, part in zip((0, 2, 1, 3), parts)]
         parts = [parts[i] for i in (0, 2, 1, 3)]
         if u:
             parts = after(parts, nears[-1], centres[-1])
-        images.append(gather(side_id, parts))
+        images.append(gather(side_id, parts, half_rows))
         nears.append(along(images[u], [(0, 1), (1, 0), (2, 3), (3, 2)]))
         centres.append(along(images[u], [(1, 2), (2, 1)]))
     near, centre = jnp.concatenate(nears, axis=0), jnp.concatenate(centres, axis=0)
@@ -655,7 +667,7 @@
     sent = grad.astype(jnp.bfloat16)
     grad = grad + after(swap(sent, "view", 4), sums).astype(jnp.float32)
     grad = grad / (view_count * peers * GRID)
-    far = swap(grad.astype(jnp.bfloat16), "view", 1).astype(jnp.float32)
+    far = swap(after(grad.astype(jnp.bfloat16), bands), "view", 1).astype(jnp.float32)
     grad = in_order((low, grad), far)
     return (grad_points, grad)
 

time: 286 us -> 282 us (0.986)
  Pallas kernels: 73.6 us -> 60.5 us
  starting transfers between devices: 74.1 us -> 78.9 us
  waiting for transfers between devices: 106 us -> 110 us
    pallas_call x24, Pallas kernels: 73.6 us -> 60.5 us  [call(): pl.pallas_call(body, out_shape=out_shape, in_specs=[smem] * n_scalars + [...]
    ppermute x63, starting transfers between devices: 74.1 us -> 78.9 us  [hop(): return lax.ppermute(value, axis, pairs)]
    ppermute x63, waiting for transfers between devices: 106 us -> 110 us  [hop(): return lax.ppermute(value, axis, pairs)]
    unnamed x63 -> x45, local copies, waits for them, and re-layouts: 14.9 us -> 14.3 us
  transfers between devices with their start and end apart: 63 -> 63, of which waited for: 24 -> 25; matrix products, arithmetic and copies ran while one was open for 7% -> 6% of each run, Pallas kernels for 24% -> 22%
where the time goes in v3:
time: 282 us; the launch traced here: 280 us
  waiting for transfers between devices  110 us (39%)
  starting transfers between devices  78.9 us (28%)
  Pallas kernels  60.5 us (21%)
  local copies, waits for them, and re-layouts  20.1 us (7%)
  other arithmetic  8.63 us (3%)
    ppermute x63, waiting for transfers between devices, hop(): return lax.ppermute(value, axis, pairs)  110 us
    ppermute x63, starting transfers between devices, hop(): return lax.ppermute(value, axis, pairs)  78.9 us
    pallas_call x24, Pallas kernels, call(): pl.pallas_call(body, out_shape=out_shape, in_specs=[smem] * n_scalars + [...  60.5 us
    unnamed x45, local copies, waits for them, and re-layouts  14.3 us
  transfers between devices with their start and end apart: 63, of which 25 were waited for; matrix products, arithmetic and copies ran while one was open for 6% of the time, Pallas kernels for 22%

profile of v3, /device:TPU:0, one launch (start us, length us, event | category | flops | bytes accessed | tf_op | source)
XLA Modules:
  0.0 279.8 jit_solution(5416415803145832674)
XLA Ops:
  3.3 4.1 %collective-permute-start = (s32[1,4,128]{2,1,0:T(4,128)S(1)}, s32[1,4,128]{2,1,0:T(4,128)S(1)}, u32[]{:S(2)}, u32[]{:S(2)}) collective-permute-start(s32[1,4,128]{2,1,0:T(4,128)S(1)} %add_bitcast_fusion), channel_id=1, source_target_pairs={{0,16},{4,20},{8,24},{12,28},{16,0},{20,4},{24,8},{28,12},{1,17},{... | collective-permute-start | bytes 6152 | tf_op jit(solution)/shard_map/ppermute | solution.py:520
  8.0 3.3 %copy.22 = bf16[2,64,74,128]{3,2,1,0:T(8,128)(2,1)S(1)} copy(bf16[2,64,74,128]{3,1,2,0:T(8,128)(2,1)} %param.10) | data formatting | bytes 4849664 | tf_op args[3]
  14.1 4.3 %collective-permute-start.4 = (bf16[6,80,128]{2,1,0:T(8,128)(2,1)S(1)}, bf16[6,80,128]{2,1,0:T(8,128)(2,1)S(1)}, u32[]{:S(2)}, u32[]{:S(2)}) collective-permute-start(bf16[6,80,128]{2,1,0:T(8,128)(2,1)S(1)} %get-tuple-element.62), channel_id=1, source_target_pairs={{0,28},{4,24},{8,20},{12,16},{16,12},{20,8},{24,4},{28,0},{1,29},{... | collective-permute-start | bytes 368648 | tf_op jit(solution)/shard_map/ppermute | solution.py:520
  20.5 4.6 %collective-permute-done.2 = s32[4,4,128]{2,1,0:T(4,128)S(1)} collective-permute-done((s32[4,4,128]{2,1,0:T(4,128)S(1)}, s32[4,4,128]{2,1,0:T(4,128)S(1)}, u32[]{:S(2)}, u32[]{:S(2)}) %collective-permute-start.2) | collective-permute-done | bytes 8224 | tf_op jit(solution)/shard_map/ppermute | solution.py:520
  26.3 2.9 %collective-permute-start.20 = (bf16[6,80,128]{2,1,0:T(8,128)(2,1)S(1)}, bf16[6,80,128]{2,1,0:T(8,128)(2,1)S(1)}, u32[]{:S(2)}, u32[]{:S(2)}) collective-permute-start(bf16[6,80,128]{2,1,0:T(8,128)(2,1)S(1)} %get-tuple-element.76), channel_id=1, source_target_pairs={{0,20},{4,16},{8,28},{12,24},{16,4},{20,0},{24,12},{28,8},{1,21},{... | collective-permute-start | bytes 368648 | tf_op jit(solution)/shard_map/ppermute | solution.py:520
  30.8 3.5 %collective-permute-done.19 = bf16[6,80,128]{2,1,0:T(8,128)(2,1)S(1)} collective-permute-done((bf16[6,80,128]{2,1,0:T(8,128)(2,1)S(1)}, bf16[6,80,128]{2,1,0:T(8,128)(2,1)S(1)}, u32[]{:S(2)}, u32[]{:S(2)}) %collective-permute-start.19) | collective-permute-done | bytes 122912 | tf_op jit(solution)/shard_map/ppermute | solution.py:520
  34.3 3.1 %collective-permute-done.20 = bf16[6,80,128]{2,1,0:T(8,128)(2,1)S(1)} collective-permute-done((bf16[6,80,128]{2,1,0:T(8,128)(2,1)S(1)}, bf16[6,80,128]{2,1,0:T(8,128)(2,1)S(1)}, u32[]{:S(2)}, u32[]{:S(2)}) %collective-permute-start.20) | collective-permute-done | bytes 122912 | tf_op jit(solution)/shard_map/ppermute | solution.py:520
  40.5 4.2 %collective-permute-done.21 = bf16[2,6,80,128]{3,2,1,0:T(8,128)(2,1)S(1)} collective-permute-done((bf16[2,6,80,128]{3,2,1,0:T(8,128)(2,1)S(1)}, bf16[2,6,80,128]{3,2,1,0:T(8,128)(2,1)S(1)}, u32[]{:S(2)}, u32[]{:S(2)}) %collective-permute-start.21) | collective-permute-done | bytes 245792 | tf_op jit(solution)/shard_map/ppermute | solution.py:520
  47.7 2.2 spread_blocks.4
  52.9 6.6 %collective-permute-done.8 = bf16[2,6,80,128]{3,2,1,0:T(8,128)(2,1)S(1)} collective-permute-done((bf16[2,6,80,128]{3,2,1,0:T(8,128)(2,1)S(1)}, bf16[2,6,80,128]{3,2,1,0:T(8,128)(2,1)S(1)}, u32[]{:S(2)}, u32[]{:S(2)}) %collective-permute-start.8) | collective-permute-done | bytes 245792 | tf_op jit(solution)/shard_map/ppermute | solution.py:520
  59.6 4.4 %collective-permute-done.17 = bf16[2,6,80,128]{3,2,1,0:T(8,128)(2,1)S(1)} collective-permute-done((bf16[2,6,80,128]{3,2,1,0:T(8,128)(2,1)S(1)}, bf16[2,6,80,128]{3,2,1,0:T(8,128)(2,1)S(1)}, u32[]{:S(2)}, u32[]{:S(2)}) %collective-permute-start.17) | collective-permute-done | bytes 245792 | tf_op jit(solution)/shard_map/ppermute | solution.py:520
  64.1 1.9 spread_blocks.7
  66.4 2.5 collective-permute-done.23.other_ref
  69.5 4.2 %render_blocks.7 = bf16[1376,384]{1,0:T(8,128)(2,1)S(1)} custom-call(s32[1]{0:T(128)} %get-tuple-element.177.count_ref.refs_3_, s32[24]{0:T(128)S(1)} %get-tuple-element.158.block_ref, s32[24]{0:T(128)S(1)} %get-tuple-element.188.place_ref.refs_5_, s32[24]{0:T(128)S(1)} %fusion.9.where_ref.refs_0_, s32[1]{0:T(128)} %get-tuple-element.175.other_count_ref.count_ref, ...), custom_call_target="tpu_custom_call" | custom-call | flops 5000000000 | bytes 10000000 | tf_op jit(solution)/shard_map/render_blocks/pallas_call | solution.py:120
  73.7 2.2 collective-permute-start.27
  77.7 2.3 spread_blocks.6
  79.9 7.0 %collective-permute-done.24.other_ref = bf16[12,80,384]{2,1,0:T(8,128)(2,1)S(1)} collective-permute-done((bf16[12,80,384]{2,1,0:T(8,128)(2,1)S(1)}, bf16[12,80,384]{2,1,0:T(8,128)(2,1)S(1)}, u32[]{:S(2)}, u32[]{:S(2)}) %collective-permute-start.24) | collective-permute-done | bytes 737312 | tf_op jit(solution)/shard_map/ppermute | solution.py:520
  87.6 3.6 %render_blocks.6 = bf16[1376,384]{1,0:T(8,128)(2,1)S(1)} custom-call(s32[1]{0:T(128)} %get-tuple-element.178.count_ref.refs_3_, s32[24]{0:T(128)S(1)} %get-tuple-element.159.block_ref, s32[24]{0:T(128)S(1)} %get-tuple-element.187.place_ref.refs_5_, s32[24]{0:T(128)S(1)} %fusion.9.where_ref.refs_0_, s32[1]{0:T(128)} %get-tuple-element.173.other_count_ref.count_ref, ...), custom_call_target="tpu_custom_call" | custom-call | flops 5000000000 | bytes 10000000 | tf_op jit(solution)/shard_map/render_blocks/pallas_call | solution.py:120
  91.2 6.8 %collective-permute-done.27 = bf16[1376,384]{1,0:T(8,128)(2,1)S(1)} collective-permute-done((bf16[1376,384]{1,0:T(8,128)(2,1)S(1)}, bf16[1376,384]{1,0:T(8,128)(2,1)S(1)}, u32[]{:S(2)}, u32[]{:S(2)}) %collective-permute-start.27) | collective-permute-done | bytes 1056800 | tf_op jit(solution)/shard_map/ppermute | solution.py:520
  98.3 4.5 %collective-permute-start.30 = (bf16[1376,384]{1,0:T(8,128)(2,1)S(1)}, bf16[1376,384]{1,0:T(8,128)(2,1)S(1)}, u32[]{:S(2)}, u32[]{:S(2)}) collective-permute-start(bf16[1376,384]{1,0:T(8,128)(2,1)S(1)} %add_convert_fusion), channel_id=1, source_target_pairs={{0,8},{4,12},{24,16},{28,20},{1,9},{5,13},{25,17},{29,21},{2,10},{... | collective-permute-start | bytes 3170312 | tf_op jit(solution)/shard_map/ppermute | solution.py:520
  109.4 3.5 %render_blocks.5 = bf16[1376,384]{1,0:T(8,128)(2,1)S(1)} custom-call(s32[1]{0:T(128)} %get-tuple-element.176.count_ref.refs_6_, s32[24]{0:T(128)S(1)} %get-tuple-element.157.block_ref, s32[24]{0:T(128)S(1)} %get-tuple-element.189.place_ref.refs_8_, s32[24]{0:T(128)S(1)} %fusion.9.where_ref.refs_0_, s32[1]{0:T(128)} %get-tuple-element.172.other_count_ref.count_ref, ...), custom_call_target="tpu_custom_call" | custom-call | flops 5000000000 | bytes 10000000 | tf_op jit(solution)/shard_map/render_blocks/pallas_call | solution.py:120
  112.9 11.1 %collective-permute-done.30 = bf16[1376,384]{1,0:T(8,128)(2,1)S(1)} collective-permute-done((bf16[1376,384]{1,0:T(8,128)(2,1)S(1)}, bf16[1376,384]{1,0:T(8,128)(2,1)S(1)}, u32[]{:S(2)}, u32[]{:S(2)}) %collective-permute-start.30) | collective-permute-done | bytes 1056800 | tf_op jit(solution)/shard_map/ppermute | solution.py:520
  127.2 5.0 %collective-permute-start.29 = (bf16[688,384]{1,0:T(8,128)(2,1)S(1)}, bf16[688,384]{1,0:T(8,128)(2,1)S(1)}, u32[]{:S(2)}, u32[]{:S(2)}) collective-permute-start(bf16[688,384]{1,0:T(8,128)(2,1)S(1)} %get-tuple-element.131), channel_id=1, source_target_pairs={{0,8},{4,12},{8,0},{12,4},{16,24},{20,28},{24,16},{28,20},{1,9},{5... | collective-permute-start | bytes 1585160 | tf_op jit(solution)/shard_map/ppermute | solution.py:520
  133.6 4.8 %collective-permute-start.39 = (bf16[688,384]{1,0:T(8,128)(2,1)S(1)}, bf16[688,384]{1,0:T(8,128)(2,1)S(1)}, u32[]{:S(2)}, u32[]{:S(2)}) collective-permute-start(bf16[688,384]{1,0:T(8,128)(2,1)S(1)} %get-tuple-element.130), channel_id=1, source_target_pairs={{0,8},{4,12},{8,0},{12,4},{16,24},{20,28},{24,16},{28,20},{1,9},{5... | collective-permute-start | bytes 1585160 | tf_op jit(solution)/shard_map/ppermute | solution.py:520
  138.4 3.9 %render_blocks.4.refs_0_ = bf16[1376,384]{1,0:T(8,128)(2,1)S(1)} custom-call(s32[1]{0:T(128)} %get-tuple-element.182.count_ref.refs_1_, s32[24]{0:T(128)S(1)} %get-tuple-element.163.block_ref, s32[24]{0:T(128)S(1)} %get-tuple-element.186.place_ref.refs_3_, s32[24]{0:T(128)S(1)} %fusion.9.where_ref.refs_0_, s32[1]{0:T(128)} %get-tuple-element.174.other_count_ref.count_ref, ...), custom_call_target="tpu_custom_call" | custom-call | flops 5000000000 | bytes 10000000 | tf_op jit(solution)/shard_map/render_blocks/pallas_call | solution.py:120
  142.3 2.6 collective-permute-done.29.refs_1_
  147.4 3.3 %collective-permute-done.32.refs_4_ = bf16[176,384]{1,0:T(8,128)(2,1)S(1)} collective-permute-done((bf16[176,384]{1,0:T(8,128)(2,1)S(1)}, bf16[176,384]{1,0:T(8,128)(2,1)S(1)}, u32[]{:S(2)}, u32[]{:S(2)}) %collective-permute-start.32) | collective-permute-done | bytes 135200 | tf_op jit(solution)/shard_map/ppermute | solution.py:520
  152.6 2.8 loss_rows.2
  160.0 2.5 collective-permute-done.36.refs_2_
  164.5 2.1 collective-permute-start.47
  169.4 2.8 %loss_rows.3 = (bf16[176,384]{1,0:T(8,128)(2,1)S(1)}, bf16[176,384]{1,0:T(8,128)(2,1)S(1)}, bf16[176,384]{1,0:T(8,128)(2,1)S(1)}, bf16[176,384]{1,0:T(8,128)(2,1)S(1)}, f32[768,768]{1,0:T(8,128)S(1)}) custom-call(s32[1]{0:T(128)} %bitcast.18.side_ref.refs_0_, bf16[768,768]{1,0:T(8,128)(2,1)S(1)} %constant_dynamic-update-slice_fusion.3.refs_1_, ...), custom_call_target="tpu_custom_call" | custom-call | flops 3000000000 | bytes 6000000 | tf_op jit(solution)/shard_map/loss_rows/pallas_call | solution.py:120
  174.8 5.0 %collective-permute-done.45.refs_2_ = bf16[176,384]{1,0:T(8,128)(2,1)S(1)} collective-permute-done((bf16[176,384]{1,0:T(8,128)(2,1)S(1)}, bf16[176,384]{1,0:T(8,128)(2,1)S(1)}, u32[]{:S(2)}, u32[]{:S(2)}) %collective-permute-start.45) | collective-permute-done | bytes 135200 | tf_op jit(solution)/shard_map/ppermute | solution.py:520
  181.9 2.1 collective-permute-start.49
  184.7 2.9 %pick_bands.6 = bf16[12,80,384]{2,1,0:T(8,128)(2,1)} custom-call(s32[1]{0:T(128)} %get-tuple-element.174.other_count_ref.count_ref, s32[24]{0:T(128)S(1)} %get-tuple-element.167.other_place_ref.place_ref, bf16[688,384]{1,0:T(8,128)(2,1)S(1)} %gather_rows.2.rest_0_.refs_10_, bf16[688,384]{1,0:T(8,128)(2,1)S(1)} %gather_rows.3.rest_1_.refs_11_), custom_call_target="tpu_custom_call" | custom-call | flops 1000000000 | bytes 2000000 | tf_op jit(solution)/shard_map/pick_bands/pallas_call | solution.py:120
  189.0 7.2 %collective-permute-done.49.rest_1_.refs_16_ = bf16[688,384]{1,0:T(8,128)(2,1)S(1)} collective-permute-done((bf16[688,384]{1,0:T(8,128)(2,1)S(1)}, bf16[688,384]{1,0:T(8,128)(2,1)S(1)}, u32[]{:S(2)}, u32[]{:S(2)}) %collective-permute-start.49) | collective-permute-done | bytes 528416 | tf_op jit(solution)/shard_map/ppermute | solution.py:520
  205.3 2.0 pick_bands.5
  208.3 6.7 %pull_blocks.4.refs_10_ = f32[65,192,128]{2,1,0:T(8,128)S(1)} custom-call(s32[24]{0:T(128)S(1)} %fusion.9.where_ref.refs_0_, s32[1]{0:T(128)} %get-tuple-element.182.count_ref.refs_1_, s32[24]{0:T(128)S(1)} %get-tuple-element.149.refs_2_, s32[24]{0:T(128)S(1)} %get-tuple-element.186.place_ref.refs_3_, s32[1]{0:T(128)} %get-tuple-element.181.count_ref.refs_4_, ...), custom_call_target="tpu_custom_call" | custom-call | flops 1000000000 | bytes 2000000 | tf_op jit(solution)/shard_map/pull_blocks/pallas_call | solution.py:120
  216.5 2.5 collective-permute-done.58
  221.0 7.6 %collective-permute-done.52 = bf16[1376,384]{1,0:T(8,128)(2,1)} collective-permute-done((bf16[1376,384]{1,0:T(8,128)(2,1)}, bf16[1376,384]{1,0:T(8,128)(2,1)}, u32[]{:S(2)}, u32[]{:S(2)}) %collective-permute-start.52) | collective-permute-done | bytes 1056800 | tf_op jit(solution)/shard_map/ppermute | solution.py:520
  233.2 4.6 %pull_blocks.5.refs_10_ = f32[65,192,128]{2,1,0:T(8,128)S(1)} custom-call(s32[24]{0:T(128)S(1)} %fusion.9.where_ref.refs_0_, s32[1]{0:T(128)} %get-tuple-element.180.count_ref.refs_1_, s32[24]{0:T(128)S(1)} %get-tuple-element.151.refs_2_, s32[1]{0:T(128)} %get-tuple-element.178.count_ref.refs_3_, s32[24]{0:T(128)S(1)} %get-tuple-element.150.refs_4_, ...), custom_call_target="tpu_custom_call" | custom-call | flops 1000000000 | bytes 2000000 | tf_op jit(solution)/shard_map/pull_blocks/pallas_call | solution.py:120
  237.8 2.5 collective-permute-start.60
  240.4 11.0 %collective-permute-done.51 = bf16[1376,384]{1,0:T(8,128)(2,1)S(1)} collective-permute-done((bf16[1376,384]{1,0:T(8,128)(2,1)}, bf16[1376,384]{1,0:T(8,128)(2,1)S(1)}, u32[]{:S(2)}, u32[]{:S(2)}) %collective-permute-start.51) | collective-permute-done | bytes 1056800 | tf_op jit(solution)/shard_map/ppermute | solution.py:520
  251.5 2.0 pick_bands.7
  255.8 4.6 %pull_blocks.6.refs_5_ = f32[65,192,128]{2,1,0:T(8,128)S(1)} custom-call(s32[24]{0:T(128)S(1)} %fusion.9.where_ref.refs_0_, s32[1]{0:T(128)} %get-tuple-element.179.count_ref.refs_1_, s32[24]{0:T(128)S(1)} %get-tuple-element.146.refs_2_, s32[1]{0:T(128)} %get-tuple-element.177.count_ref.refs_3_, s32[24]{0:T(128)S(1)} %get-tuple-element.145.refs_4_, ...), custom_call_target="tpu_custom_call" | custom-call | flops 1000000000 | bytes 2000000 | tf_op jit(solution)/shard_map/pull_blocks/pallas_call | solution.py:120
  260.4 2.7 copy-done.1
  263.1 7.1 %collective-permute-done.56.refs_4_ = bf16[12,80,384]{2,1,0:T(8,128)(2,1)S(1)} collective-permute-done((bf16[12,80,384]{2,1,0:T(8,128)(2,1)S(1)}, bf16[12,80,384]{2,1,0:T(8,128)(2,1)S(1)}, u32[]{:S(2)}, u32[]{:S(2)}) %collective-permute-start.56) | collective-permute-done | bytes 737312 | tf_op jit(solution)/shard_map/ppermute | solution.py:520
  271.3 2.8 %copy-done.2 = f32[65,192,128]{2,1,0:T(8,128)S(1)} copy-done((f32[65,192,128]{2,1,0:T(8,128)S(1)}, f32[65,192,128]{2,1,0:T(8,128)}, u32[]{:S(2)}) %copy-start.2) | copy-done | bytes 6389784
  274.1 4.8 %pull_blocks.7 = bf16[64,192,128]{2,1,0:T(8,128)(2,1)} custom-call(s32[24]{0:T(128)S(1)} %fusion.9.where_ref.refs_0_, s32[1]{0:T(128)} %get-tuple-element.183.count_ref.refs_1_, s32[24]{0:T(128)S(1)} %get-tuple-element.152.refs_2_, bf16[24,80,128]{2,1,0:T(8,128)(2,1)S(1)} %get-tuple-element.137.weight_ref.refs_3_, ...), custom_call_target="tpu_custom_call" | custom-call | flops 1000000000 | bytes 2000000 | tf_op jit(solution)/shard_map/pull_blocks/pallas_call | solution.py:120
  (219 shorter events, 78.0 us)
Async XLA Ops:
  3.3 7.9 %collective-permute-start = (s32[1,4,128]{2,1,0:T(4,128)S(1)}, s32[1,4,128]{2,1,0:T(4,128)S(1)}, u32[]{:S(2)}, u32[]{:S(2)}) collective-permute-start(s32[1,4,128]{2,1,0:T(4,128)S(1)} %add_bitcast_fusion), channel_id=1, source_target_pairs={{0,16},{4,20},{8,24},{12,28},{16,0},{20,4},{24,8},{28,12},{1,17},{... | collective-permute-start | bytes 6152 | tf_op jit(solution)/shard_map/ppermute | solution.py:520
  13.5 12.8 %collective-permute-start.3 = (bf16[6,80,128]{2,1,0:T(8,128)(2,1)S(1)}, bf16[6,80,128]{2,1,0:T(8,128)(2,1)S(1)}, u32[]{:S(2)}, u32[]{:S(2)}) collective-permute-start(bf16[6,80,128]{2,1,0:T(8,128)(2,1)S(1)} %get-tuple-element.61), channel_id=1, source_target_pairs={{0,24},{4,28},{8,16},{12,20},{16,8},{20,12},{24,0},{28,4},{1,25},{... | collective-permute-start | bytes 368648 | tf_op jit(solution)/shard_map/ppermute | solution.py:520
  14.1 15.1 %collective-permute-start.4 = (bf16[6,80,128]{2,1,0:T(8,128)(2,1)S(1)}, bf16[6,80,128]{2,1,0:T(8,128)(2,1)S(1)}, u32[]{:S(2)}, u32[]{:S(2)}) collective-permute-start(bf16[6,80,128]{2,1,0:T(8,128)(2,1)S(1)} %get-tuple-element.62), channel_id=1, source_target_pairs={{0,28},{4,24},{8,20},{12,16},{16,12},{20,8},{24,4},{28,0},{1,29},{... | collective-permute-start | bytes 368648 | tf_op jit(solution)/shard_map/ppermute | solution.py:520
  18.4 22.1 %collective-permute-start.7 = (bf16[6,80,128]{2,1,0:T(8,128)(2,1)S(1)}, bf16[6,80,128]{2,1,0:T(8,128)(2,1)S(1)}, u32[]{:S(2)}, u32[]{:S(2)}) collective-permute-start(bf16[6,80,128]{2,1,0:T(8,128)(2,1)S(1)} %get-tuple-element.64), channel_id=1, source_target_pairs={{0,4},{4,0},{8,12},{12,8},{16,20},{20,16},{24,28},{28,24},{1,5},{5... | collective-permute-start | bytes 368648 | tf_op jit(solution)/shard_map/ppermute | solution.py:520
  18.9 26.0 %collective-permute-start.15 = (bf16[6,80,128]{2,1,0:T(8,128)(2,1)S(1)}, bf16[6,80,128]{2,1,0:T(8,128)(2,1)}, u32[]{:S(2)}, u32[]{:S(2)}) collective-permute-start(bf16[6,80,128]{2,1,0:T(8,128)(2,1)S(1)} %get-tuple-element.72), channel_id=1, source_target_pairs={{0,8},{4,12},{8,0},{12,4},{16,24},{20,28},{24,16},{28,20},{1,9},{5... | collective-permute-start | bytes 368648 | tf_op jit(solution)/shard_map/ppermute | solution.py:520
  25.1 9.2 %collective-permute-start.19 = (bf16[6,80,128]{2,1,0:T(8,128)(2,1)S(1)}, bf16[6,80,128]{2,1,0:T(8,128)(2,1)S(1)}, u32[]{:S(2)}, u32[]{:S(2)}) collective-permute-start(bf16[6,80,128]{2,1,0:T(8,128)(2,1)S(1)} %get-tuple-element.75), channel_id=1, source_target_pairs={{0,16},{4,20},{8,24},{12,28},{16,0},{20,4},{24,8},{28,12},{1,17},{... | collective-permute-start | bytes 368648 | tf_op jit(solution)/shard_map/ppermute | solution.py:520
  26.3 11.1 %collective-permute-start.20 = (bf16[6,80,128]{2,1,0:T(8,128)(2,1)S(1)}, bf16[6,80,128]{2,1,0:T(8,128)(2,1)S(1)}, u32[]{:S(2)}, u32[]{:S(2)}) collective-permute-start(bf16[6,80,128]{2,1,0:T(8,128)(2,1)S(1)} %get-tuple-element.76), channel_id=1, source_target_pairs={{0,20},{4,16},{8,28},{12,24},{16,4},{20,0},{24,12},{28,8},{1,21},{... | collective-permute-start | bytes 368648 | tf_op jit(solution)/shard_map/ppermute | solution.py:520
  29.3 9.7 %collective-permute-start.5 = (bf16[2,6,80,128]{3,2,1,0:T(8,128)(2,1)S(1)}, bf16[2,6,80,128]{3,2,1,0:T(8,128)(2,1)S(1)}, u32[]{:S(2)}, u32[]{:S(2)}) collective-permute-start(bf16[2,6,80,128]{3,2,1,0:T(8,128)(2,1)S(1)} %pad_maximum_fusion.8), channel_id=1, source_target_pairs={{0,2},{1,3},{2,0},{3,1},{4,6},{5,7},{6,4},{7,5},{8,10},{9,11},{10,... | collective-permute-start | bytes 737288 | tf_op jit(solution)/shard_map/ppermute | solution.py:520
  34.3 10.6 %collective-permute-start.16 = (bf16[6,80,128]{2,1,0:T(8,128)(2,1)S(1)}, bf16[6,80,128]{2,1,0:T(8,128)(2,1)S(1)}, u32[]{:S(2)}, u32[]{:S(2)}) collective-permute-start(bf16[6,80,128]{2,1,0:T(8,128)(2,1)S(1)} %get-tuple-element.73), channel_id=1, source_target_pairs={{0,12},{4,8},{8,4},{12,0},{16,28},{20,24},{24,20},{28,16},{1,13},{... | collective-permute-start | bytes 368648 | tf_op jit(solution)/shard_map/ppermute | solution.py:520
  44.8 7.9 %collective-permute-start.22 = (bf16[2,12,80,128]{3,2,1,0:T(8,128)(2,1)S(1)}, bf16[2,12,80,128]{3,2,1,0:T(8,128)(2,1)S(1)}, u32[]{:S(2)}, u32[]{:S(2)}) collective-permute-start(bf16[2,12,80,128]{3,2,1,0:T(8,128)(2,1)S(1)} %pad_maximum_fusion.7), channel_id=1, source_target_pairs={{0,1},{1,0},{2,3},{3,2},{4,5},{5,4},{6,7},{7,6},{8,9},{9,8},{10,11... | collective-permute-start | bytes 1474568 | tf_op jit(solution)/shard_map/ppermute | solution.py:520
  49.9 18.9 %collective-permute-start.23 = (bf16[12,80,384]{2,1,0:T(8,128)(2,1)S(1)}, bf16[12,80,384]{2,1,0:T(8,128)(2,1)S(1)}, u32[]{:S(2)}, u32[]{:S(2)}) collective-permute-start(bf16[12,80,384]{2,1,0:T(8,128)(2,1)S(1)} %spread_blocks.4), channel_id=1, source_target_pairs={{0,4},{4,0},{8,12},{12,8},{16,20},{20,16},{24,28},{28,24},{1,5},{5... | collective-permute-start | bytes 2211848 | tf_op jit(solution)/shard_map/ppermute | solution.py:520
  50.7 8.8 %collective-permute-start.8 = (bf16[2,6,80,128]{3,2,1,0:T(8,128)(2,1)S(1)}, bf16[2,6,80,128]{3,2,1,0:T(8,128)(2,1)S(1)}, u32[]{:S(2)}, u32[]{:S(2)}) collective-permute-start(bf16[2,6,80,128]{3,2,1,0:T(8,128)(2,1)S(1)} %pad_maximum_fusion.9), channel_id=1, source_target_pairs={{0,2},{1,3},{2,0},{3,1},{4,6},{5,7},{6,4},{7,5},{8,10},{9,11},{10,... | collective-permute-start | bytes 737288 | tf_op jit(solution)/shard_map/ppermute | solution.py:520
  52.2 11.8 %collective-permute-start.17 = (bf16[2,6,80,128]{3,2,1,0:T(8,128)(2,1)S(1)}, bf16[2,6,80,128]{3,2,1,0:T(8,128)(2,1)S(1)}, u32[]{:S(2)}, u32[]{:S(2)}) collective-permute-start(bf16[2,6,80,128]{3,2,1,0:T(8,128)(2,1)S(1)} %pad_maximum_fusion.10), channel_id=1, source_target_pairs={{0,2},{1,3},{2,0},{3,1},{4,6},{5,7},{6,4},{7,5},{8,10},{9,11},{10,... | collective-permute-start | bytes 737288 | tf_op jit(solution)/shard_map/ppermute | solution.py:520
  68.9 18.1 %collective-permute-start.24 = (bf16[12,80,384]{2,1,0:T(8,128)(2,1)S(1)}, bf16[12,80,384]{2,1,0:T(8,128)(2,1)S(1)}, u32[]{:S(2)}, u32[]{:S(2)}) collective-permute-start(bf16[12,80,384]{2,1,0:T(8,128)(2,1)S(1)} %spread_blocks.7), channel_id=1, source_target_pairs={{0,4},{4,0},{8,12},{12,8},{16,20},{20,16},{24,28},{28,24},{1,5},{5... | collective-permute-start | bytes 2211848 | tf_op jit(solution)/shard_map/ppermute | solution.py:520
  73.7 24.3 %collective-permute-start.27 = (bf16[1376,384]{1,0:T(8,128)(2,1)S(1)}, bf16[1376,384]{1,0:T(8,128)(2,1)S(1)}, u32[]{:S(2)}, u32[]{:S(2)}) collective-permute-start(bf16[1376,384]{1,0:T(8,128)(2,1)S(1)} %render_blocks.7), channel_id=1, source_target_pairs={{0,8},{4,12},{24,16},{28,20},{1,9},{5,13},{25,17},{29,21},{2,10},{... | collective-permute-start | bytes 3170312 | tf_op jit(solution)/shard_map/ppermute | solution.py:520
  76.0 30.5 %collective-permute-start.10 = (bf16[192,768]{1,0:T(8,128)(2,1)S(1)}, bf16[192,768]{1,0:T(8,128)(2,1)S(1)}, u32[]{:S(2)}, u32[]{:S(2)}) collective-permute-start(bf16[192,768]{1,0:T(8,128)(2,1)S(1)} %copy-done.15), channel_id=1, source_target_pairs={{0,2},{1,3},{2,0},{3,1},{4,6},{5,7},{6,4},{7,5},{8,10},{9,11},{10,... | collective-permute-start | bytes 884744 | tf_op jit(solution)/shard_map/ppermute | solution.py:520
  86.9 21.2 %collective-permute-start.25 = (bf16[12,80,384]{2,1,0:T(8,128)(2,1)S(1)}, bf16[12,80,384]{2,1,0:T(8,128)(2,1)S(1)}, u32[]{:S(2)}, u32[]{:S(2)}) collective-permute-start(bf16[12,80,384]{2,1,0:T(8,128)(2,1)S(1)} %spread_blocks.6), channel_id=1, source_target_pairs={{0,4},{4,0},{8,12},{12,8},{16,20},{20,16},{24,28},{28,24},{1,5},{5... | collective-permute-start | bytes 2211848 | tf_op jit(solution)/shard_map/ppermute | solution.py:520
  98.3 25.7 %collective-permute-start.30 = (bf16[1376,384]{1,0:T(8,128)(2,1)S(1)}, bf16[1376,384]{1,0:T(8,128)(2,1)S(1)}, u32[]{:S(2)}, u32[]{:S(2)}) collective-permute-start(bf16[1376,384]{1,0:T(8,128)(2,1)S(1)} %add_convert_fusion), channel_id=1, source_target_pairs={{0,8},{4,12},{24,16},{28,20},{1,9},{5,13},{25,17},{29,21},{2,10},{... | collective-permute-start | bytes 3170312 | tf_op jit(solution)/shard_map/ppermute | solution.py:520
  103.6 20.7 %collective-permute-start.28 = (bf16[1376,384]{1,0:T(8,128)(2,1)S(1)}, bf16[1376,384]{1,0:T(8,128)(2,1)S(1)}, u32[]{:S(2)}, u32[]{:S(2)}) collective-permute-start(bf16[1376,384]{1,0:T(8,128)(2,1)S(1)} %add_convert_fusion), channel_id=1, source_target_pairs={{8,16},{12,20},{16,8},{20,12},{9,17},{13,21},{17,9},{21,13},{10,18... | collective-permute-start | bytes 3170312 | tf_op jit(solution)/shard_map/ppermute | solution.py:520
  104.5 21.8 %collective-permute-start.12 = (bf16[2,176,384]{2,1,0:T(8,128)(2,1)S(1)}, bf16[2,176,384]{2,1,0:T(8,128)(2,1)S(1)}, u32[]{:S(2)}, u32[]{:S(2)}) collective-permute-start(bf16[2,176,384]{2,1,0:T(8,128)(2,1)S(1)} %get-tuple-element.69), channel_id=1, source_target_pairs={{0,1},{1,0},{2,3},{3,2},{4,5},{5,4},{6,7},{7,6},{8,9},{9,8},{10,11... | collective-permute-start | bytes 811016 | tf_op jit(solution)/shard_map/ppermute | solution.py:520
  106.5 20.7 %collective-permute-start.13 = (bf16[2,176,384]{2,1,0:T(8,128)(2,1)S(1)}, bf16[2,176,384]{2,1,0:T(8,128)(2,1)S(1)}, u32[]{:S(2)}, u32[]{:S(2)}) collective-permute-start(bf16[2,176,384]{2,1,0:T(8,128)(2,1)S(1)} %get-tuple-element.70), channel_id=1, source_target_pairs={{0,2},{1,3},{2,0},{3,1},{4,6},{5,7},{6,4},{7,5},{8,10},{9,11},{10,... | collective-permute-start | bytes 811016 | tf_op jit(solution)/shard_map/ppermute | solution.py:520
  108.1 25.5 %collective-permute-start.26 = (bf16[12,80,384]{2,1,0:T(8,128)(2,1)S(1)}, bf16[12,80,384]{2,1,0:T(8,128)(2,1)S(1)}, u32[]{:S(2)}, u32[]{:S(2)}) collective-permute-start(bf16[12,80,384]{2,1,0:T(8,128)(2,1)S(1)} %spread_blocks.5), channel_id=1, source_target_pairs={{0,4},{4,0},{8,12},{12,8},{16,20},{20,16},{24,28},{28,24},{1,5},{5... | collective-permute-start | bytes 2211848 | tf_op jit(solution)/shard_map/ppermute | solution.py:520
  124.0 8.7 %collective-permute-start.14 = (bf16[2,176,384]{2,1,0:T(8,128)(2,1)S(1)}, bf16[2,176,384]{2,1,0:T(8,128)(2,1)S(1)}, u32[]{:S(2)}, u32[]{:S(2)}) collective-permute-start(bf16[2,176,384]{2,1,0:T(8,128)(2,1)S(1)} %get-tuple-element.71), channel_id=1, source_target_pairs={{0,3},{1,2},{2,1},{3,0},{4,7},{5,6},{6,5},{7,4},{8,11},{9,10},{10,... | collective-permute-start | bytes 811016 | tf_op jit(solution)/shard_map/ppermute | solution.py:520
  124.3 22.4 %collective-permute-start.11 = (bf16[384,768]{1,0:T(8,128)(2,1)S(1)}, bf16[384,768]{1,0:T(8,128)(2,1)S(1)}, u32[]{:S(2)}, u32[]{:S(2)}) collective-permute-start(bf16[384,768]{1,0:T(8,128)(2,1)S(1)} %pad_maximum_fusion.3), channel_id=1, source_target_pairs={{0,1},{1,0},{2,3},{3,2},{4,5},{5,4},{6,7},{7,6},{8,9},{9,8},{10,11... | collective-permute-start | bytes 1769480 | tf_op jit(solution)/shard_map/ppermute | solution.py:520
  126.3 16.1 %collective-permute-start.31 = (bf16[688,384]{1,0:T(8,128)(2,1)S(1)}, bf16[688,384]{1,0:T(8,128)(2,1)S(1)}, u32[]{:S(2)}, u32[]{:S(2)}) collective-permute-start(bf16[688,384]{1,0:T(8,128)(2,1)S(1)} %get-tuple-element.129), channel_id=1, source_target_pairs={{8,16},{12,20},{16,8},{20,12},{9,17},{13,21},{17,9},{21,13},{10,18... | collective-permute-start | bytes 1585160 | tf_op jit(solution)/shard_map/ppermute | solution.py:520
  127.2 17.8 %collective-permute-start.29 = (bf16[688,384]{1,0:T(8,128)(2,1)S(1)}, bf16[688,384]{1,0:T(8,128)(2,1)S(1)}, u32[]{:S(2)}, u32[]{:S(2)}) collective-permute-start(bf16[688,384]{1,0:T(8,128)(2,1)S(1)} %get-tuple-element.131), channel_id=1, source_target_pairs={{0,8},{4,12},{8,0},{12,4},{16,24},{20,28},{24,16},{28,20},{1,9},{5... | collective-permute-start | bytes 1585160 | tf_op jit(solution)/shard_map/ppermute | solution.py:520
  132.9 24.6 %collective-permute-start.40 = (bf16[688,384]{1,0:T(8,128)(2,1)S(1)}, bf16[688,384]{1,0:T(8,128)(2,1)S(1)}, u32[]{:S(2)}, u32[]{:S(2)}) collective-permute-start(bf16[688,384]{1,0:T(8,128)(2,1)S(1)} %get-tuple-element.128), channel_id=1, source_target_pairs={{8,16},{12,20},{16,8},{20,12},{9,17},{13,21},{17,9},{21,13},{10,18... | collective-permute-start | bytes 1585160 | tf_op jit(solution)/shard_map/ppermute | solution.py:520
  133.6 23.9 %collective-permute-start.39 = (bf16[688,384]{1,0:T(8,128)(2,1)S(1)}, bf16[688,384]{1,0:T(8,128)(2,1)S(1)}, u32[]{:S(2)}, u32[]{:S(2)}) collective-permute-start(bf16[688,384]{1,0:T(8,128)(2,1)S(1)} %get-tuple-element.130), channel_id=1, source_target_pairs={{0,8},{4,12},{8,0},{12,4},{16,24},{20,28},{24,16},{28,20},{1,9},{5... | collective-permute-start | bytes 1585160 | tf_op jit(solution)/shard_map/ppermute | solution.py:520
  157.8 10.5 %collective-permute-start.41 = (bf16[176,384]{1,0:T(8,128)(2,1)S(1)}, bf16[176,384]{1,0:T(8,128)(2,1)S(1)}, u32[]{:S(2)}, u32[]{:S(2)}) collective-permute-start(bf16[176,384]{1,0:T(8,128)(2,1)S(1)} %get-tuple-element.90), channel_id=1, source_target_pairs={{0,2},{1,3},{2,0},{3,1},{4,6},{5,7},{6,4},{7,5},{8,10},{9,11},{10,... | collective-permute-start | bytes 405512 | tf_op jit(solution)/shard_map/ppermute | solution.py:520
  159.3 9.0 %collective-permute-start.42 = (bf16[176,384]{1,0:T(8,128)(2,1)S(1)}, bf16[176,384]{1,0:T(8,128)(2,1)S(1)}, u32[]{:S(2)}, u32[]{:S(2)}) collective-permute-start(bf16[176,384]{1,0:T(8,128)(2,1)S(1)} %get-tuple-element.91), channel_id=1, source_target_pairs={{0,1},{1,0},{2,3},{3,2},{4,5},{5,4},{6,7},{7,6},{8,9},{9,8},{10,11... | collective-permute-start | bytes 405512 | tf_op jit(solution)/shard_map/ppermute | solution.py:520
  159.7 9.7 %collective-permute-start.43 = (bf16[176,384]{1,0:T(8,128)(2,1)S(1)}, bf16[176,384]{1,0:T(8,128)(2,1)S(1)}, u32[]{:S(2)}, u32[]{:S(2)}) collective-permute-start(bf16[176,384]{1,0:T(8,128)(2,1)S(1)} %get-tuple-element.92), channel_id=1, source_target_pairs={{0,3},{1,2},{2,1},{3,0},{4,7},{5,6},{6,5},{7,4},{8,11},{9,10},{10,... | collective-permute-start | bytes 405512 | tf_op jit(solution)/shard_map/ppermute | solution.py:520
  164.5 16.4 %collective-permute-start.47 = (bf16[688,384]{1,0:T(8,128)(2,1)S(1)}, bf16[688,384]{1,0:T(8,128)(2,1)S(1)}, u32[]{:S(2)}, u32[]{:S(2)}) collective-permute-start(bf16[688,384]{1,0:T(8,128)(2,1)S(1)} %gather_rows.2.rest_0_.refs_10_), channel_id=1, source_target_pairs={{0,8},{4,12},{8,0},{12,4},{16,24},{20,28},{24,16},{28,20},{1,9},{5... | collective-permute-start | bytes 1585160 | tf_op jit(solution)/shard_map/ppermute | solution.py:520
  166.6 14.3 %collective-permute-start.38 = (bf16[688,384]{1,0:T(8,128)(2,1)S(1)}, bf16[688,384]{1,0:T(8,128)(2,1)S(1)}, u32[]{:S(2)}, u32[]{:S(2)}) collective-permute-start(bf16[688,384]{1,0:T(8,128)(2,1)S(1)} %gather_rows.2.rest_0_.refs_10_), channel_id=1, source_target_pairs={{8,16},{12,20},{16,8},{20,12},{9,17},{13,21},{17,9},{21,13},{10,18... | collective-permute-start | bytes 1585160 | tf_op jit(solution)/shard_map/ppermute | solution.py:520
  181.1 20.6 %collective-permute-start.57 = (f32[2,192,768]{2,1,0:T(8,128)S(1)}, f32[2,192,768]{2,1,0:T(8,128)S(1)}, u32[]{:S(2)}, u32[]{:S(2)}) collective-permute-start(f32[2,192,768]{2,1,0:T(8,128)S(1)} %bitcast.115), channel_id=1, source_target_pairs={{0,1},{1,0},{2,3},{3,2},{4,5},{5,4},{6,7},{7,6},{8,9},{9,8},{10,11... | collective-permute-start | bytes 3538952 | tf_op jit(solution)/shard_map/ppermute | solution.py:520
  181.9 14.3 %collective-permute-start.49 = (bf16[688,384]{1,0:T(8,128)(2,1)S(1)}, bf16[688,384]{1,0:T(8,128)(2,1)S(1)}, u32[]{:S(2)}, u32[]{:S(2)}) collective-permute-start(bf16[688,384]{1,0:T(8,128)(2,1)S(1)} %gather_rows.3.rest_1_.refs_11_), channel_id=1, source_target_pairs={{0,8},{4,12},{8,0},{12,4},{16,24},{20,28},{24,16},{28,20},{1,9},{5... | collective-permute-start | bytes 1585160 | tf_op jit(solution)/shard_map/ppermute | solution.py:520
  184.0 15.6 %collective-permute-start.48 = (bf16[688,384]{1,0:T(8,128)(2,1)S(1)}, bf16[688,384]{1,0:T(8,128)(2,1)S(1)}, u32[]{:S(2)}, u32[]{:S(2)}) collective-permute-start(bf16[688,384]{1,0:T(8,128)(2,1)S(1)} %gather_rows.3.rest_1_.refs_11_), channel_id=1, source_target_pairs={{8,16},{12,20},{16,8},{20,12},{9,17},{13,21},{17,9},{21,13},{10,18... | collective-permute-start | bytes 1585160 | tf_op jit(solution)/shard_map/ppermute | solution.py:520
  187.5 19.7 %collective-permute-start.53 = (bf16[12,80,384]{2,1,0:T(8,128)(2,1)}, bf16[12,80,384]{2,1,0:T(8,128)(2,1)}, u32[]{:S(2)}, u32[]{:S(2)}) collective-permute-start(bf16[12,80,384]{2,1,0:T(8,128)(2,1)} %pick_bands.6), channel_id=1, source_target_pairs={{0,4},{4,0},{8,12},{12,8},{16,20},{20,16},{24,28},{28,24},{1,5},{5... | collective-permute-start | bytes 2211848 | tf_op jit(solution)/shard_map/ppermute | solution.py:520
  197.1 17.9 %collective-permute-start.50 = (bf16[1376,384]{1,0:T(8,128)(2,1)}, bf16[1376,384]{1,0:T(8,128)(2,1)}, u32[]{:S(2)}, u32[]{:S(2)}) collective-permute-start(bf16[1376,384]{1,0:T(8,128)(2,1)} %constant_dynamic-update-slice_fusion.11), channel_id=1, source_target_pairs={{8,16},{12,20},{16,8},{20,12},{9,17},{13,21},{17,9},{21,13},{10,18... | collective-permute-start | bytes 3170312 | tf_op jit(solution)/shard_map/ppermute | solution.py:520
  200.4 28.2 %collective-permute-start.52 = (bf16[1376,384]{1,0:T(8,128)(2,1)}, bf16[1376,384]{1,0:T(8,128)(2,1)}, u32[]{:S(2)}, u32[]{:S(2)}) collective-permute-start(bf16[1376,384]{1,0:T(8,128)(2,1)} %constant_dynamic-update-slice_fusion.9), channel_id=1, source_target_pairs={{8,0},{12,4},{16,24},{20,28},{9,1},{13,5},{17,25},{21,29},{10,2},{... | collective-permute-start | bytes 3170312 | tf_op jit(solution)/shard_map/ppermute | solution.py:520
  203.8 15.2 %collective-permute-start.58 = (f32[192,768]{1,0:T(8,128)}, f32[192,768]{1,0:T(8,128)}, u32[]{:S(2)}, u32[]{:S(2)}) collective-permute-start(f32[192,768]{1,0:T(8,128)} %slice_bitcast_fusion), channel_id=1, source_target_pairs={{0,2},{1,3},{2,0},{3,1},{4,6},{5,7},{6,4},{7,5},{8,10},{9,11},{10,... | collective-permute-start | bytes 1769480 | tf_op jit(solution)/shard_map/ppermute | solution.py:520
  207.3 24.6 %collective-permute-start.54 = (bf16[12,80,384]{2,1,0:T(8,128)(2,1)S(1)}, bf16[12,80,384]{2,1,0:T(8,128)(2,1)S(1)}, u32[]{:S(2)}, u32[]{:S(2)}) collective-permute-start(bf16[12,80,384]{2,1,0:T(8,128)(2,1)S(1)} %pick_bands.5), channel_id=1, source_target_pairs={{0,4},{4,0},{8,12},{12,8},{16,20},{20,16},{24,28},{28,24},{1,5},{5... | collective-permute-start | bytes 2211848 | tf_op jit(solution)/shard_map/ppermute | solution.py:520
  215.0 36.4 %collective-permute-start.51 = (bf16[1376,384]{1,0:T(8,128)(2,1)}, bf16[1376,384]{1,0:T(8,128)(2,1)S(1)}, u32[]{:S(2)}, u32[]{:S(2)}) collective-permute-start(bf16[1376,384]{1,0:T(8,128)(2,1)} %collective-permute-done.50), channel_id=1, source_target_pairs={{8,0},{12,4},{16,24},{20,28},{9,1},{13,5},{17,25},{21,29},{10,2},{... | collective-permute-start | bytes 3170312 | tf_op jit(solution)/shard_map/ppermute | solution.py:520
  220.1 17.6 %collective-permute-start.59 = (f32[96,768]{1,0:T(8,128)S(1)}, f32[96,768]{1,0:T(8,128)S(1)}, u32[]{:S(2)}, u32[]{:S(2)}) collective-permute-start(f32[96,768]{1,0:T(8,128)S(1)} %constant_dynamic-slice_fusion), channel_id=1, source_target_pairs={{0,4},{4,0},{8,12},{12,8},{16,20},{20,16},{24,28},{28,24},{1,5},{5... | collective-permute-start | bytes 884744 | tf_op jit(solution)/shard_map/ppermute | solution.py:520
  231.9 21.6 %collective-permute-start.55 = (bf16[12,80,384]{2,1,0:T(8,128)(2,1)S(1)}, bf16[12,80,384]{2,1,0:T(8,128)(2,1)S(1)}, u32[]{:S(2)}, u32[]{:S(2)}) collective-permute-start(bf16[12,80,384]{2,1,0:T(8,128)(2,1)S(1)} %pick_bands.4), channel_id=1, source_target_pairs={{0,4},{4,0},{8,12},{12,8},{16,20},{20,16},{24,28},{28,24},{1,5},{5... | collective-permute-start | bytes 2211848 | tf_op jit(solution)/shard_map/ppermute | solution.py:520
  237.8 16.8 %collective-permute-start.60 = (bf16[96,768]{1,0:T(8,128)(2,1)S(1)}, bf16[96,768]{1,0:T(8,128)(2,1)S(1)}, u32[]{:S(2)}, u32[]{:S(2)}) collective-permute-start(bf16[96,768]{1,0:T(8,128)(2,1)S(1)} %get-tuple-element.124), channel_id=1, source_target_pairs={{0,8},{4,12},{8,0},{12,4},{16,24},{20,28},{24,16},{28,20},{1,9},{5... | collective-permute-start | bytes 442376 | tf_op jit(solution)/shard_map/ppermute | solution.py:520
  253.5 16.7 %collective-permute-start.56 = (bf16[12,80,384]{2,1,0:T(8,128)(2,1)S(1)}, bf16[12,80,384]{2,1,0:T(8,128)(2,1)S(1)}, u32[]{:S(2)}, u32[]{:S(2)}) collective-permute-start(bf16[12,80,384]{2,1,0:T(8,128)(2,1)S(1)} %pick_bands.7), channel_id=1, source_target_pairs={{0,4},{4,0},{8,12},{12,8},{16,20},{20,16},{24,28},{28,24},{1,5},{5... | collective-permute-start | bytes 2211848 | tf_op jit(solution)/shard_map/ppermute | solution.py:520
  254.7 8.4 %collective-permute-start.61 = (bf16[96,768]{1,0:T(8,128)(2,1)S(1)}, bf16[96,768]{1,0:T(8,128)(2,1)S(1)}, u32[]{:S(2)}, u32[]{:S(2)}) collective-permute-start(bf16[96,768]{1,0:T(8,128)(2,1)S(1)} %fusion.1), channel_id=1, source_target_pairs={{0,16},{4,20},{8,24},{12,28},{16,0},{20,4},{24,8},{28,12},{1,17},{... | collective-permute-start | bytes 442376 | tf_op jit(solution)/shard_map/ppermute | solution.py:520
  270.2 8.6 %collective-permute-start.62 = (bf16[96,768]{1,0:T(8,128)(2,1)S(1)}, bf16[96,768]{1,0:T(8,128)(2,1)S(1)}, u32[]{:S(2)}, u32[]{:S(2)}) collective-permute-start(bf16[96,768]{1,0:T(8,128)(2,1)S(1)} %get-tuple-element.119), channel_id=1, source_target_pairs={{0,4},{4,0},{8,12},{12,8},{16,20},{20,16},{24,28},{28,24},{1,5},{5... | collective-permute-start | bytes 442376 | tf_op jit(solution)/shard_map/ppermute | solution.py:520
  (32 other events, 252.5 us)

commit v4 on v3

--- a/solution.py
+++ b/solution.py
@@ -285,7 +285,7 @@
 
     out = jax.ShapeDtypeStruct((slots // 2, band_rows, packed), jnp.bfloat16)
     scratch = [pltpu.VMEM((pixels + band_rows + 8, 256), jnp.float32)]
-    return call(body, out, (count, place) + tuple(images), 2, 1, "pick_bands", scratch)
+    return call(body, out, (count, place) + tuple(images), 2, 0.1, "pick_bands", scratch)
 
 
 def pull(jobs, where, old, blocks, half_rows, last):
@@ -358,7 +358,7 @@
     out = out if last else jax.ShapeDtypeStruct(sums, jnp.float32)
     scratch = [pltpu.VMEM((pixels + band_rows + 8, 256), jnp.float32)]
     scratch += [pltpu.VMEM(sums, jnp.float32)] if last else []
-    us = 1
+    us = 0.1
     return call(body, out, tuple(tables + arrays), len(tables), us, "pull_blocks", scratch, 24)
 
 
@@ -565,22 +565,27 @@
     where_of = turn * quarter + slot_ids % quarter
 
     weights, kept, given, arrived = {}, {}, {}, {}
-    hops = []
     for j in (3, 2, 1, 0):
         got = []
         for k in (2 * j + 1, 2 * j):
             value = packed[k]
             got.append(swap(value, "view", k) if k else value)
         got = jnp.stack(got[::-1])
-        if j >= 2:
-            hops.append(got)
-        else:
+        if j < 2:
             got = after(got, given[3])
         got = jnp.concatenate([got, swap(got, "feat", 2)], axis=1)
         weights[j] = jnp.concatenate([got, swap(got, "feat", 1)], axis=1)
         k = 2 * j + 1
         given[j] = spread(counts[k : k + 1], block_of[k], where_of, weights[j][1], points)
         arrived[j] = given[j]
+    side_id = side.reshape(1).astype(ints)
+    teacher = after(teacher.transpose(1, 0, 2), weights[0])
+    target = turn_teacher(side_id, teacher, sides, padded)
+    target = jnp.stack([swap(target[d], "feat", d) if d else target[d] for d in range(sides)])
+    head_weight = after(head_weight, weights[0])
+    head = jnp.concatenate([head_weight, swap(head_weight, "feat", 2)], axis=0)
+    head = jnp.concatenate([head, swap(head, "feat", 1)], axis=0)
+
     arrived[3] = after(swap(given[3], "view", 1), given[2], weights[1], weights[0])
     for j in (3, 2, 1, 0):
         if j < 3:
@@ -588,16 +593,8 @@
         k = 2 * j
         kept[j] = render(
             counts[k : k + 1], block_of[k], place_of[k], where_of, pair_counts[j : j + 1], pair_places[j],
-            weights[j][0], points, arrived[j], view_count, half_rows,
+            weights[j][0], after(points, *(head,)) if j == 1 else points, arrived[j], view_count, half_rows,
         )
-
-    side_id = side.reshape(1).astype(ints)
-    teacher = after(teacher.transpose(1, 0, 2), weights[0])
-    target = turn_teacher(side_id, teacher, sides, padded)
-    target = jnp.stack([swap(target[d], "feat", d) if d else target[d] for d in range(sides)])
-    head_weight = after(head_weight, weights[0])
-    head = jnp.concatenate([head_weight, swap(head_weight, "feat", 2)], axis=0)
-    head = jnp.concatenate([head, swap(head, "feat", 1)], axis=0)
 
     far = along(kept[3], [(0, 1), (3, 2)])
     mid = total(kept[2], far)

time: 282 us -> 279 us (0.989)
  starting transfers between devices: 78.9 us -> 73.2 us
  local copies, waits for them, and re-layouts: 20.1 us -> 23.5 us
    ppermute x63, starting transfers between devices: 78.9 us -> 73.2 us  [hop(): return lax.ppermute(value, axis, pairs)]
    unnamed x45 -> x75, local copies, waits for them, and re-layouts: 14.3 us -> 16.3 us
where the time goes in v4:
time: 279 us; the launch traced here: 277 us
  waiting for transfers between devices  108 us (39%)
  starting transfers between devices  73.2 us (26%)
  Pallas kernels  62.2 us (22%)
  local copies, waits for them, and re-layouts  23.5 us (8%)
  other arithmetic  8.41 us (3%)
    ppermute x63, waiting for transfers between devices, hop(): return lax.ppermute(value, axis, pairs)  108 us
    ppermute x63, starting transfers between devices, hop(): return lax.ppermute(value, axis, pairs)  73.2 us
    pallas_call x24, Pallas kernels, call(): pl.pallas_call(body, out_shape=out_shape, in_specs=[smem] * n_scalars + [...  62.2 us
    unnamed x75, local copies, waits for them, and re-layouts  16.3 us
  transfers between devices with their start and end apart: 63, of which 25 were waited for; matrix products, arithmetic and copies ran while one was open for 6% of the time, Pallas kernels for 22%

profile of v4, /device:TPU:0, one launch (start us, length us, event | category | flops | bytes accessed | tf_op | source)
XLA Modules:
  0.0 276.9 jit_solution(6463880141182623234)
XLA Ops:
  3.3 4.1 %collective-permute-start = (s32[1,4,128]{2,1,0:T(4,128)S(1)}, s32[1,4,128]{2,1,0:T(4,128)S(1)}, u32[]{:S(2)}, u32[]{:S(2)}) collective-permute-start(s32[1,4,128]{2,1,0:T(4,128)S(1)} %add_bitcast_fusion), channel_id=1, source_target_pairs={{0,16},{4,20},{8,24},{12,28},{16,0},{20,4},{24,8},{28,12},{1,17},{... | collective-permute-start | bytes 6152 | tf_op jit(solution)/shard_map/ppermute | solution.py:520
  8.0 3.3 %copy.22 = bf16[2,64,74,128]{3,2,1,0:T(8,128)(2,1)S(1)} copy(bf16[2,64,74,128]{3,1,2,0:T(8,128)(2,1)} %param.10) | data formatting | bytes 4849664 | tf_op args[3]
  14.1 4.3 %collective-permute-start.4 = (bf16[6,80,128]{2,1,0:T(8,128)(2,1)S(1)}, bf16[6,80,128]{2,1,0:T(8,128)(2,1)S(1)}, u32[]{:S(2)}, u32[]{:S(2)}) collective-permute-start(bf16[6,80,128]{2,1,0:T(8,128)(2,1)S(1)} %get-tuple-element.63), channel_id=1, source_target_pairs={{0,28},{4,24},{8,20},{12,16},{16,12},{20,8},{24,4},{28,0},{1,29},{... | collective-permute-start | bytes 368648 | tf_op jit(solution)/shard_map/ppermute | solution.py:520
  20.5 4.6 %collective-permute-done.2 = s32[4,4,128]{2,1,0:T(4,128)S(1)} collective-permute-done((s32[4,4,128]{2,1,0:T(4,128)S(1)}, s32[4,4,128]{2,1,0:T(4,128)S(1)}, u32[]{:S(2)}, u32[]{:S(2)}) %collective-permute-start.2) | collective-permute-done | bytes 8224 | tf_op jit(solution)/shard_map/ppermute | solution.py:520
  27.0 2.9 %collective-permute-start.20 = (bf16[6,80,128]{2,1,0:T(8,128)(2,1)S(1)}, bf16[6,80,128]{2,1,0:T(8,128)(2,1)S(1)}, u32[]{:S(2)}, u32[]{:S(2)}) collective-permute-start(bf16[6,80,128]{2,1,0:T(8,128)(2,1)S(1)} %get-tuple-element.77), channel_id=1, source_target_pairs={{0,20},{4,16},{8,28},{12,24},{16,4},{20,0},{24,12},{28,8},{1,21},{... | collective-permute-start | bytes 368648 | tf_op jit(solution)/shard_map/ppermute | solution.py:520
  31.5 3.0 %collective-permute-done.19 = bf16[6,80,128]{2,1,0:T(8,128)(2,1)S(1)} collective-permute-done((bf16[6,80,128]{2,1,0:T(8,128)(2,1)S(1)}, bf16[6,80,128]{2,1,0:T(8,128)(2,1)S(1)}, u32[]{:S(2)}, u32[]{:S(2)}) %collective-permute-start.19) | collective-permute-done | bytes 122912 | tf_op jit(solution)/shard_map/ppermute | solution.py:520
  34.5 3.0 %collective-permute-done.20 = bf16[6,80,128]{2,1,0:T(8,128)(2,1)S(1)} collective-permute-done((bf16[6,80,128]{2,1,0:T(8,128)(2,1)S(1)}, bf16[6,80,128]{2,1,0:T(8,128)(2,1)S(1)}, u32[]{:S(2)}, u32[]{:S(2)}) %collective-permute-start.20) | collective-permute-done | bytes 122912 | tf_op jit(solution)/shard_map/ppermute | solution.py:520
  40.6 4.2 %collective-permute-done.21 = bf16[2,6,80,128]{3,2,1,0:T(8,128)(2,1)S(1)} collective-permute-done((bf16[2,6,80,128]{3,2,1,0:T(8,128)(2,1)S(1)}, bf16[2,6,80,128]{3,2,1,0:T(8,128)(2,1)S(1)}, u32[]{:S(2)}, u32[]{:S(2)}) %collective-permute-start.21) | collective-permute-done | bytes 245792 | tf_op jit(solution)/shard_map/ppermute | solution.py:520
  45.2 1.9 copy-done
  52.5 6.6 %collective-permute-done.8 = bf16[2,6,80,128]{3,2,1,0:T(8,128)(2,1)S(1)} collective-permute-done((bf16[2,6,80,128]{3,2,1,0:T(8,128)(2,1)S(1)}, bf16[2,6,80,128]{3,2,1,0:T(8,128)(2,1)S(1)}, u32[]{:S(2)}, u32[]{:S(2)}) %collective-permute-start.8) | collective-permute-done | bytes 245792 | tf_op jit(solution)/shard_map/ppermute | solution.py:520
  59.2 4.4 %collective-permute-done.17 = bf16[2,6,80,128]{3,2,1,0:T(8,128)(2,1)S(1)} collective-permute-done((bf16[2,6,80,128]{3,2,1,0:T(8,128)(2,1)S(1)}, bf16[2,6,80,128]{3,2,1,0:T(8,128)(2,1)S(1)}, u32[]{:S(2)}, u32[]{:S(2)}) %collective-permute-start.17) | collective-permute-done | bytes 245792 | tf_op jit(solution)/shard_map/ppermute | solution.py:520
  63.7 2.2 spread_blocks.7
  69.1 4.7 %render_blocks.7 = bf16[1376,384]{1,0:T(8,128)(2,1)S(1)} custom-call(s32[1]{0:T(128)} %get-tuple-element.179.count_ref.refs_3_, s32[24]{0:T(128)S(1)} %get-tuple-element.160.block_ref, s32[24]{0:T(128)S(1)} %get-tuple-element.190.place_ref.refs_5_, s32[24]{0:T(128)S(1)} %fusion.9.where_ref.refs_0_, s32[1]{0:T(128)} %get-tuple-element.177.other_count_ref.count_ref, ...), custom_call_target="tpu_custom_call" | custom-call | flops 5000000000 | bytes 10000000 | tf_op jit(solution)/shard_map/render_blocks/pallas_call | solution.py:120
  76.9 2.2 spread_blocks.6
  79.1 4.4 %collective-permute-done.10 = bf16[192,768]{1,0:T(8,128)(2,1)S(1)} collective-permute-done((bf16[192,768]{1,0:T(8,128)(2,1)S(1)}, bf16[192,768]{1,0:T(8,128)(2,1)S(1)}, u32[]{:S(2)}, u32[]{:S(2)}) %collective-permute-start.10) | collective-permute-done | bytes 294944 | tf_op jit(solution)/shard_map/ppermute | solution.py:520
  83.6 2.1 collective-permute-done.24.other_ref
  87.1 4.0 %render_blocks.6 = bf16[1376,384]{1,0:T(8,128)(2,1)S(1)} custom-call(s32[1]{0:T(128)} %get-tuple-element.180.count_ref.refs_3_, s32[24]{0:T(128)S(1)} %get-tuple-element.161.block_ref, s32[24]{0:T(128)S(1)} %get-tuple-element.189.place_ref.refs_5_, s32[24]{0:T(128)S(1)} %fusion.9.where_ref.refs_0_, s32[1]{0:T(128)} %get-tuple-element.175.other_count_ref.count_ref, ...), custom_call_target="tpu_custom_call" | custom-call | flops 5000000000 | bytes 10000000 | tf_op jit(solution)/shard_map/render_blocks/pallas_call | solution.py:120
  91.2 6.3 %collective-permute-done.27 = bf16[1376,384]{1,0:T(8,128)(2,1)S(1)} collective-permute-done((bf16[1376,384]{1,0:T(8,128)(2,1)S(1)}, bf16[1376,384]{1,0:T(8,128)(2,1)S(1)}, u32[]{:S(2)}, u32[]{:S(2)}) %collective-permute-start.27) | collective-permute-done | bytes 1056800 | tf_op jit(solution)/shard_map/ppermute | solution.py:520
  97.8 4.5 %collective-permute-start.30 = (bf16[1376,384]{1,0:T(8,128)(2,1)S(1)}, bf16[1376,384]{1,0:T(8,128)(2,1)S(1)}, u32[]{:S(2)}, u32[]{:S(2)}) collective-permute-start(bf16[1376,384]{1,0:T(8,128)(2,1)S(1)} %add_convert_fusion), channel_id=1, source_target_pairs={{0,8},{4,12},{24,16},{28,20},{1,9},{5,13},{25,17},{29,21},{2,10},{... | collective-permute-start | bytes 3170312 | tf_op jit(solution)/shard_map/ppermute | solution.py:520
  103.1 2.0 spread_blocks.5
  106.3 3.8 %render_blocks.5 = bf16[1376,384]{1,0:T(8,128)(2,1)S(1)} custom-call(s32[1]{0:T(128)} %get-tuple-element.178.count_ref.refs_6_, s32[24]{0:T(128)S(1)} %get-tuple-element.159.block_ref, s32[24]{0:T(128)S(1)} %get-tuple-element.191.place_ref.refs_8_, s32[24]{0:T(128)S(1)} %fusion.9.where_ref.refs_0_, s32[1]{0:T(128)} %get-tuple-element.174.other_count_ref.count_ref, ...), custom_call_target="tpu_custom_call" | custom-call | flops 5000000000 | bytes 10000000 | tf_op jit(solution)/shard_map/render_blocks/pallas_call | solution.py:120
  110.2 13.5 %collective-permute-done.30 = bf16[1376,384]{1,0:T(8,128)(2,1)S(1)} collective-permute-done((bf16[1376,384]{1,0:T(8,128)(2,1)S(1)}, bf16[1376,384]{1,0:T(8,128)(2,1)S(1)}, u32[]{:S(2)}, u32[]{:S(2)}) %collective-permute-start.30) | collective-permute-done | bytes 1056800 | tf_op jit(solution)/shard_map/ppermute | solution.py:520
  125.1 4.4 %collective-permute-start.29 = (bf16[688,384]{1,0:T(8,128)(2,1)S(1)}, bf16[688,384]{1,0:T(8,128)(2,1)S(1)}, u32[]{:S(2)}, u32[]{:S(2)}) collective-permute-start(bf16[688,384]{1,0:T(8,128)(2,1)S(1)} %get-tuple-element.133), channel_id=1, source_target_pairs={{0,8},{4,12},{8,0},{12,4},{16,24},{20,28},{24,16},{28,20},{1,9},{5... | collective-permute-start | bytes 1585160 | tf_op jit(solution)/shard_map/ppermute | solution.py:520
  132.3 3.7 %render_blocks.4.refs_0_ = bf16[1376,384]{1,0:T(8,128)(2,1)S(1)} custom-call(s32[1]{0:T(128)} %get-tuple-element.184.count_ref.refs_1_, s32[24]{0:T(128)S(1)} %get-tuple-element.165.block_ref, s32[24]{0:T(128)S(1)} %get-tuple-element.188.place_ref.refs_3_, s32[24]{0:T(128)S(1)} %fusion.9.where_ref.refs_0_, s32[1]{0:T(128)} %get-tuple-element.176.other_count_ref.count_ref, ...), custom_call_target="tpu_custom_call" | custom-call | flops 5000000000 | bytes 10000000 | tf_op jit(solution)/shard_map/render_blocks/pallas_call | solution.py:120
  136.8 2.3 collective-permute-done.29.refs_1_
  139.0 3.4 %collective-permute-start.39 = (bf16[688,384]{1,0:T(8,128)(2,1)S(1)}, bf16[688,384]{1,0:T(8,128)(2,1)S(1)}, u32[]{:S(2)}, u32[]{:S(2)}) collective-permute-start(bf16[688,384]{1,0:T(8,128)(2,1)S(1)} %get-tuple-element.132), channel_id=1, source_target_pairs={{0,8},{4,12},{8,0},{12,4},{16,24},{20,28},{24,16},{28,20},{1,9},{5... | collective-permute-start | bytes 1585160 | tf_op jit(solution)/shard_map/ppermute | solution.py:520
  144.7 2.0 collective-permute-start.34
  148.1 2.0 collective-permute-done.34.refs_6_
  150.1 2.8 %loss_rows.2 = (bf16[176,384]{1,0:T(8,128)(2,1)S(1)}, bf16[176,384]{1,0:T(8,128)(2,1)S(1)}, bf16[176,384]{1,0:T(8,128)(2,1)S(1)}, bf16[176,384]{1,0:T(8,128)(2,1)S(1)}, f32[768,768]{1,0:T(8,128)S(1)}) custom-call(s32[1]{0:T(128)} %bitcast.18.side_ref.refs_0_, bf16[768,768]{1,0:T(8,128)(2,1)S(1)} %constant_dynamic-update-slice_fusion.3.refs_1_, ...), custom_call_target="tpu_custom_call" | custom-call | flops 3000000000 | bytes 6000000 | tf_op jit(solution)/shard_map/loss_rows/pallas_call | solution.py:120
  157.8 2.5 collective-permute-done.36.refs_2_
  163.0 3.1 %collective-permute-done.41.refs_4_ = bf16[176,384]{1,0:T(8,128)(2,1)S(1)} collective-permute-done((bf16[176,384]{1,0:T(8,128)(2,1)S(1)}, bf16[176,384]{1,0:T(8,128)(2,1)S(1)}, u32[]{:S(2)}, u32[]{:S(2)}) %collective-permute-start.41) | collective-permute-done | bytes 135200 | tf_op jit(solution)/shard_map/ppermute | solution.py:520
  167.3 2.8 %loss_rows.3 = (bf16[176,384]{1,0:T(8,128)(2,1)S(1)}, bf16[176,384]{1,0:T(8,128)(2,1)S(1)}, bf16[176,384]{1,0:T(8,128)(2,1)S(1)}, bf16[176,384]{1,0:T(8,128)(2,1)S(1)}, f32[768,768]{1,0:T(8,128)S(1)}) custom-call(s32[1]{0:T(128)} %bitcast.18.side_ref.refs_0_, bf16[768,768]{1,0:T(8,128)(2,1)S(1)} %constant_dynamic-update-slice_fusion.3.refs_1_, ...), custom_call_target="tpu_custom_call" | custom-call | flops 3000000000 | bytes 6000000 | tf_op jit(solution)/shard_map/loss_rows/pallas_call | solution.py:120
  172.6 5.0 %collective-permute-done.45.refs_2_ = bf16[176,384]{1,0:T(8,128)(2,1)S(1)} collective-permute-done((bf16[176,384]{1,0:T(8,128)(2,1)S(1)}, bf16[176,384]{1,0:T(8,128)(2,1)S(1)}, u32[]{:S(2)}, u32[]{:S(2)}) %collective-permute-start.45) | collective-permute-done | bytes 135200 | tf_op jit(solution)/shard_map/ppermute | solution.py:520
  181.8 3.1 %pick_bands.6 = bf16[12,80,384]{2,1,0:T(8,128)(2,1)} custom-call(s32[1]{0:T(128)} %get-tuple-element.176.other_count_ref.count_ref, s32[24]{0:T(128)S(1)} %get-tuple-element.169.other_place_ref.place_ref, bf16[688,384]{1,0:T(8,128)(2,1)S(1)} %gather_rows.2.rest_0_.refs_10_, bf16[688,384]{1,0:T(8,128)(2,1)S(1)} %gather_rows.3.rest_1_.refs_11_), custom_call_target="tpu_custom_call" | custom-call | flops 100000000 | bytes 200000 | tf_op jit(solution)/shard_map/pick_bands/pallas_call | solution.py:120
  186.0 7.8 %collective-permute-done.49.rest_1_.refs_16_ = bf16[688,384]{1,0:T(8,128)(2,1)S(1)} collective-permute-done((bf16[688,384]{1,0:T(8,128)(2,1)S(1)}, bf16[688,384]{1,0:T(8,128)(2,1)S(1)}, u32[]{:S(2)}, u32[]{:S(2)}) %collective-permute-start.49) | collective-permute-done | bytes 528416 | tf_op jit(solution)/shard_map/ppermute | solution.py:520
  204.8 2.4 pick_bands.5
  208.8 6.3 %pull_blocks.4.refs_10_ = f32[65,192,128]{2,1,0:T(8,128)S(1)} custom-call(s32[24]{0:T(128)S(1)} %fusion.9.where_ref.refs_0_, s32[1]{0:T(128)} %get-tuple-element.184.count_ref.refs_1_, s32[24]{0:T(128)S(1)} %get-tuple-element.151.refs_2_, s32[24]{0:T(128)S(1)} %copy-done.22, s32[1]{0:T(128)} %get-tuple-element.183.count_ref.refs_4_, ...), custom_call_target="tpu_custom_call" | custom-call | flops 100000000 | bytes 200000 | tf_op jit(solution)/shard_map/pull_blocks/pallas_call | solution.py:120
  217.6 4.5 %collective-permute-start.59 = (f32[96,768]{1,0:T(8,128)S(1)}, f32[96,768]{1,0:T(8,128)S(1)}, u32[]{:S(2)}, u32[]{:S(2)}) collective-permute-start(f32[96,768]{1,0:T(8,128)S(1)} %constant_dynamic-slice_fusion), channel_id=1, source_target_pairs={{0,4},{4,0},{8,12},{12,8},{16,20},{20,16},{24,28},{28,24},{1,5},{5... | collective-permute-start | bytes 884744 | tf_op jit(solution)/shard_map/ppermute | solution.py:520
  222.2 5.0 %collective-permute-done.52 = bf16[1376,384]{1,0:T(8,128)(2,1)} collective-permute-done((bf16[1376,384]{1,0:T(8,128)(2,1)}, bf16[1376,384]{1,0:T(8,128)(2,1)}, u32[]{:S(2)}, u32[]{:S(2)}) %collective-permute-start.52) | collective-permute-done | bytes 1056800 | tf_op jit(solution)/shard_map/ppermute | solution.py:520
  228.6 2.3 pick_bands.4
  231.0 4.5 %pull_blocks.5.refs_10_ = f32[65,192,128]{2,1,0:T(8,128)S(1)} custom-call(s32[24]{0:T(128)S(1)} %fusion.9.where_ref.refs_0_, s32[1]{0:T(128)} %get-tuple-element.182.count_ref.refs_1_, s32[24]{0:T(128)S(1)} %get-tuple-element.153.refs_2_, s32[1]{0:T(128)} %get-tuple-element.180.count_ref.refs_3_, s32[24]{0:T(128)S(1)} %get-tuple-element.152.refs_4_, ...), custom_call_target="tpu_custom_call" | custom-call | flops 100000000 | bytes 200000 | tf_op jit(solution)/shard_map/pull_blocks/pallas_call | solution.py:120
  236.2 13.5 %collective-permute-done.51 = bf16[1376,384]{1,0:T(8,128)(2,1)S(1)} collective-permute-done((bf16[1376,384]{1,0:T(8,128)(2,1)}, bf16[1376,384]{1,0:T(8,128)(2,1)S(1)}, u32[]{:S(2)}, u32[]{:S(2)}) %collective-permute-start.51) | collective-permute-done | bytes 1056800 | tf_op jit(solution)/shard_map/ppermute | solution.py:520
  249.9 2.3 pick_bands.7
  253.7 5.2 %pull_blocks.6.refs_5_ = f32[65,192,128]{2,1,0:T(8,128)S(1)} custom-call(s32[24]{0:T(128)S(1)} %fusion.9.where_ref.refs_0_, s32[1]{0:T(128)} %get-tuple-element.181.count_ref.refs_1_, s32[24]{0:T(128)S(1)} %get-tuple-element.148.refs_2_, s32[1]{0:T(128)} %get-tuple-element.179.count_ref.refs_3_, s32[24]{0:T(128)S(1)} %get-tuple-element.147.refs_4_, ...), custom_call_target="tpu_custom_call" | custom-call | flops 100000000 | bytes 200000 | tf_op jit(solution)/shard_map/pull_blocks/pallas_call | solution.py:120
  258.9 2.6 copy-done.1
  261.6 7.4 %collective-permute-done.56.refs_4_ = bf16[12,80,384]{2,1,0:T(8,128)(2,1)S(1)} collective-permute-done((bf16[12,80,384]{2,1,0:T(8,128)(2,1)S(1)}, bf16[12,80,384]{2,1,0:T(8,128)(2,1)S(1)}, u32[]{:S(2)}, u32[]{:S(2)}) %collective-permute-start.56) | collective-permute-done | bytes 737312 | tf_op jit(solution)/shard_map/ppermute | solution.py:520
  269.0 2.8 %copy-done.2 = f32[65,192,128]{2,1,0:T(8,128)S(1)} copy-done((f32[65,192,128]{2,1,0:T(8,128)S(1)}, f32[65,192,128]{2,1,0:T(8,128)}, u32[]{:S(2)}) %copy-start.2) | copy-done | bytes 6389784
  271.8 4.2 %pull_blocks.7 = bf16[64,192,128]{2,1,0:T(8,128)(2,1)} custom-call(s32[24]{0:T(128)S(1)} %fusion.9.where_ref.refs_0_, s32[1]{0:T(128)} %get-tuple-element.185.count_ref.refs_1_, s32[24]{0:T(128)S(1)} %copy-done.27, bf16[24,80,128]{2,1,0:T(8,128)(2,1)S(1)} %get-tuple-element.139.weight_ref.refs_3_, bf16[12,80,384]{2,1,0:T(8,128)(2,1)S(1)} %collective-permute-done.56.refs_4_, ...), custom_call_target="tpu_custom_call" | custom-call | flops 100000000 | bytes 200000 | tf_op jit(solution)/shard_map/pull_blocks/pallas_call | solution.py:120
  (249 shorter events, 75.3 us)
Async XLA Ops:
  3.3 7.9 %collective-permute-start = (s32[1,4,128]{2,1,0:T(4,128)S(1)}, s32[1,4,128]{2,1,0:T(4,128)S(1)}, u32[]{:S(2)}, u32[]{:S(2)}) collective-permute-start(s32[1,4,128]{2,1,0:T(4,128)S(1)} %add_bitcast_fusion), channel_id=1, source_target_pairs={{0,16},{4,20},{8,24},{12,28},{16,0},{20,4},{24,8},{28,12},{1,17},{... | collective-permute-start | bytes 6152 | tf_op jit(solution)/shard_map/ppermute | solution.py:520
  11.3 7.7 %collective-permute-start.1 = (s32[2,4,128]{2,1,0:T(4,128)S(1)}, s32[2,4,128]{2,1,0:T(4,128)S(1)}, u32[]{:S(2)}, u32[]{:S(2)}) collective-permute-start(s32[2,4,128]{2,1,0:T(4,128)S(1)} %pad_add_fusion.2), channel_id=1, source_target_pairs={{0,8},{4,12},{8,0},{12,4},{16,24},{20,28},{24,16},{28,20},{1,9},{5... | collective-permute-start | bytes 12296 | tf_op jit(solution)/shard_map/ppermute | solution.py:520
  13.5 13.4 %collective-permute-start.3 = (bf16[6,80,128]{2,1,0:T(8,128)(2,1)S(1)}, bf16[6,80,128]{2,1,0:T(8,128)(2,1)S(1)}, u32[]{:S(2)}, u32[]{:S(2)}) collective-permute-start(bf16[6,80,128]{2,1,0:T(8,128)(2,1)S(1)} %get-tuple-element.62), channel_id=1, source_target_pairs={{0,24},{4,28},{8,16},{12,20},{16,8},{20,12},{24,0},{28,4},{1,25},{... | collective-permute-start | bytes 368648 | tf_op jit(solution)/shard_map/ppermute | solution.py:520
  14.1 15.8 %collective-permute-start.4 = (bf16[6,80,128]{2,1,0:T(8,128)(2,1)S(1)}, bf16[6,80,128]{2,1,0:T(8,128)(2,1)S(1)}, u32[]{:S(2)}, u32[]{:S(2)}) collective-permute-start(bf16[6,80,128]{2,1,0:T(8,128)(2,1)S(1)} %get-tuple-element.63), channel_id=1, source_target_pairs={{0,28},{4,24},{8,20},{12,16},{16,12},{20,8},{24,4},{28,0},{1,29},{... | collective-permute-start | bytes 368648 | tf_op jit(solution)/shard_map/ppermute | solution.py:520
  18.4 22.1 %collective-permute-start.7 = (bf16[6,80,128]{2,1,0:T(8,128)(2,1)S(1)}, bf16[6,80,128]{2,1,0:T(8,128)(2,1)S(1)}, u32[]{:S(2)}, u32[]{:S(2)}) collective-permute-start(bf16[6,80,128]{2,1,0:T(8,128)(2,1)S(1)} %get-tuple-element.65), channel_id=1, source_target_pairs={{0,4},{4,0},{8,12},{12,8},{16,20},{20,16},{24,28},{28,24},{1,5},{5... | collective-permute-start | bytes 368648 | tf_op jit(solution)/shard_map/ppermute | solution.py:520
  18.9 26.0 %collective-permute-start.15 = (bf16[6,80,128]{2,1,0:T(8,128)(2,1)S(1)}, bf16[6,80,128]{2,1,0:T(8,128)(2,1)S(1)}, u32[]{:S(2)}, u32[]{:S(2)}) collective-permute-start(bf16[6,80,128]{2,1,0:T(8,128)(2,1)S(1)} %get-tuple-element.73), channel_id=1, source_target_pairs={{0,8},{4,12},{8,0},{12,4},{16,24},{20,28},{24,16},{28,20},{1,9},{5... | collective-permute-start | bytes 368648 | tf_op jit(solution)/shard_map/ppermute | solution.py:520
  25.1 9.4 %collective-permute-start.19 = (bf16[6,80,128]{2,1,0:T(8,128)(2,1)S(1)}, bf16[6,80,128]{2,1,0:T(8,128)(2,1)S(1)}, u32[]{:S(2)}, u32[]{:S(2)}) collective-permute-start(bf16[6,80,128]{2,1,0:T(8,128)(2,1)S(1)} %get-tuple-element.76), channel_id=1, source_target_pairs={{0,16},{4,20},{8,24},{12,28},{16,0},{20,4},{24,8},{28,12},{1,17},{... | collective-permute-start | bytes 368648 | tf_op jit(solution)/shard_map/ppermute | solution.py:520
  27.0 10.5 %collective-permute-start.20 = (bf16[6,80,128]{2,1,0:T(8,128)(2,1)S(1)}, bf16[6,80,128]{2,1,0:T(8,128)(2,1)S(1)}, u32[]{:S(2)}, u32[]{:S(2)}) collective-permute-start(bf16[6,80,128]{2,1,0:T(8,128)(2,1)S(1)} %get-tuple-element.77), channel_id=1, source_target_pairs={{0,20},{4,16},{8,28},{12,24},{16,4},{20,0},{24,12},{28,8},{1,21},{... | collective-permute-start | bytes 368648 | tf_op jit(solution)/shard_map/ppermute | solution.py:520
  29.9 9.1 %collective-permute-start.5 = (bf16[2,6,80,128]{3,2,1,0:T(8,128)(2,1)S(1)}, bf16[2,6,80,128]{3,2,1,0:T(8,128)(2,1)S(1)}, u32[]{:S(2)}, u32[]{:S(2)}) collective-permute-start(bf16[2,6,80,128]{3,2,1,0:T(8,128)(2,1)S(1)} %pad_maximum_fusion.8), channel_id=1, source_target_pairs={{0,2},{1,3},{2,0},{3,1},{4,6},{5,7},{6,4},{7,5},{8,10},{9,11},{10,... | collective-permute-start | bytes 737288 | tf_op jit(solution)/shard_map/ppermute | solution.py:520
  34.5 10.4 %collective-permute-start.16 = (bf16[6,80,128]{2,1,0:T(8,128)(2,1)S(1)}, bf16[6,80,128]{2,1,0:T(8,128)(2,1)S(1)}, u32[]{:S(2)}, u32[]{:S(2)}) collective-permute-start(bf16[6,80,128]{2,1,0:T(8,128)(2,1)S(1)} %get-tuple-element.74), channel_id=1, source_target_pairs={{0,12},{4,8},{8,4},{12,0},{16,28},{20,24},{24,20},{28,16},{1,13},{... | collective-permute-start | bytes 368648 | tf_op jit(solution)/shard_map/ppermute | solution.py:520
  44.8 7.5 %collective-permute-start.22 = (bf16[2,12,80,128]{3,2,1,0:T(8,128)(2,1)S(1)}, bf16[2,12,80,128]{3,2,1,0:T(8,128)(2,1)S(1)}, u32[]{:S(2)}, u32[]{:S(2)}) collective-permute-start(bf16[2,12,80,128]{3,2,1,0:T(8,128)(2,1)S(1)} %pad_maximum_fusion.7), channel_id=1, source_target_pairs={{0,1},{1,0},{2,3},{3,2},{4,5},{5,4},{6,7},{7,6},{8,9},{9,8},{10,11... | collective-permute-start | bytes 1474568 | tf_op jit(solution)/shard_map/ppermute | solution.py:520
  48.7 18.9 %collective-permute-start.23 = (bf16[12,80,384]{2,1,0:T(8,128)(2,1)S(1)}, bf16[12,80,384]{2,1,0:T(8,128)(2,1)S(1)}, u32[]{:S(2)}, u32[]{:S(2)}) collective-permute-start(bf16[12,80,384]{2,1,0:T(8,128)(2,1)S(1)} %spread_blocks.4), channel_id=1, source_target_pairs={{0,4},{4,0},{8,12},{12,8},{16,20},{20,16},{24,28},{28,24},{1,5},{5... | collective-permute-start | bytes 2211848 | tf_op jit(solution)/shard_map/ppermute | solution.py:520
  50.3 8.8 %collective-permute-start.8 = (bf16[2,6,80,128]{3,2,1,0:T(8,128)(2,1)S(1)}, bf16[2,6,80,128]{3,2,1,0:T(8,128)(2,1)S(1)}, u32[]{:S(2)}, u32[]{:S(2)}) collective-permute-start(bf16[2,6,80,128]{3,2,1,0:T(8,128)(2,1)S(1)} %pad_maximum_fusion.9), channel_id=1, source_target_pairs={{0,2},{1,3},{2,0},{3,1},{4,6},{5,7},{6,4},{7,5},{8,10},{9,11},{10,... | collective-permute-start | bytes 737288 | tf_op jit(solution)/shard_map/ppermute | solution.py:520
  51.7 11.8 %collective-permute-start.17 = (bf16[2,6,80,128]{3,2,1,0:T(8,128)(2,1)S(1)}, bf16[2,6,80,128]{3,2,1,0:T(8,128)(2,1)S(1)}, u32[]{:S(2)}, u32[]{:S(2)}) collective-permute-start(bf16[2,6,80,128]{3,2,1,0:T(8,128)(2,1)S(1)} %pad_maximum_fusion.10), channel_id=1, source_target_pairs={{0,2},{1,3},{2,0},{3,1},{4,6},{5,7},{6,4},{7,5},{8,10},{9,11},{10,... | collective-permute-start | bytes 737288 | tf_op jit(solution)/shard_map/ppermute | solution.py:520
  67.6 18.1 %collective-permute-start.24 = (bf16[12,80,384]{2,1,0:T(8,128)(2,1)S(1)}, bf16[12,80,384]{2,1,0:T(8,128)(2,1)S(1)}, u32[]{:S(2)}, u32[]{:S(2)}) collective-permute-start(bf16[12,80,384]{2,1,0:T(8,128)(2,1)S(1)} %spread_blocks.7), channel_id=1, source_target_pairs={{0,4},{4,0},{8,12},{12,8},{16,20},{20,16},{24,28},{28,24},{1,5},{5... | collective-permute-start | bytes 2211848 | tf_op jit(solution)/shard_map/ppermute | solution.py:520
  73.8 23.7 %collective-permute-start.27 = (bf16[1376,384]{1,0:T(8,128)(2,1)S(1)}, bf16[1376,384]{1,0:T(8,128)(2,1)S(1)}, u32[]{:S(2)}, u32[]{:S(2)}) collective-permute-start(bf16[1376,384]{1,0:T(8,128)(2,1)S(1)} %render_blocks.7), channel_id=1, source_target_pairs={{0,8},{4,12},{24,16},{28,20},{1,9},{5,13},{25,17},{29,21},{2,10},{... | collective-permute-start | bytes 3170312 | tf_op jit(solution)/shard_map/ppermute | solution.py:520
  75.2 8.3 %collective-permute-start.10 = (bf16[192,768]{1,0:T(8,128)(2,1)S(1)}, bf16[192,768]{1,0:T(8,128)(2,1)S(1)}, u32[]{:S(2)}, u32[]{:S(2)}) collective-permute-start(bf16[192,768]{1,0:T(8,128)(2,1)S(1)} %copy-done.30), channel_id=1, source_target_pairs={{0,2},{1,3},{2,0},{3,1},{4,6},{5,7},{6,4},{7,5},{8,10},{9,11},{10,... | collective-permute-start | bytes 884744 | tf_op jit(solution)/shard_map/ppermute | solution.py:520
  83.6 21.6 %collective-permute-start.11 = (bf16[384,768]{1,0:T(8,128)(2,1)S(1)}, bf16[384,768]{1,0:T(8,128)(2,1)S(1)}, u32[]{:S(2)}, u32[]{:S(2)}) collective-permute-start(bf16[384,768]{1,0:T(8,128)(2,1)S(1)} %pad_maximum_fusion.3), channel_id=1, source_target_pairs={{0,1},{1,0},{2,3},{3,2},{4,5},{5,4},{6,7},{7,6},{8,9},{9,8},{10,11... | collective-permute-start | bytes 1769480 | tf_op jit(solution)/shard_map/ppermute | solution.py:520
  85.7 19.5 %collective-permute-start.25 = (bf16[12,80,384]{2,1,0:T(8,128)(2,1)S(1)}, bf16[12,80,384]{2,1,0:T(8,128)(2,1)S(1)}, u32[]{:S(2)}, u32[]{:S(2)}) collective-permute-start(bf16[12,80,384]{2,1,0:T(8,128)(2,1)S(1)} %spread_blocks.6), channel_id=1, source_target_pairs={{0,4},{4,0},{8,12},{12,8},{16,20},{20,16},{24,28},{28,24},{1,5},{5... | collective-permute-start | bytes 2211848 | tf_op jit(solution)/shard_map/ppermute | solution.py:520
  97.8 25.9 %collective-permute-start.30 = (bf16[1376,384]{1,0:T(8,128)(2,1)S(1)}, bf16[1376,384]{1,0:T(8,128)(2,1)S(1)}, u32[]{:S(2)}, u32[]{:S(2)}) collective-permute-start(bf16[1376,384]{1,0:T(8,128)(2,1)S(1)} %add_convert_fusion), channel_id=1, source_target_pairs={{0,8},{4,12},{24,16},{28,20},{1,9},{5,13},{25,17},{29,21},{2,10},{... | collective-permute-start | bytes 3170312 | tf_op jit(solution)/shard_map/ppermute | solution.py:520
  102.3 22.5 %collective-permute-start.28 = (bf16[1376,384]{1,0:T(8,128)(2,1)S(1)}, bf16[1376,384]{1,0:T(8,128)(2,1)S(1)}, u32[]{:S(2)}, u32[]{:S(2)}) collective-permute-start(bf16[1376,384]{1,0:T(8,128)(2,1)S(1)} %add_convert_fusion), channel_id=1, source_target_pairs={{8,16},{12,20},{16,8},{20,12},{9,17},{13,21},{17,9},{21,13},{10,18... | collective-permute-start | bytes 3170312 | tf_op jit(solution)/shard_map/ppermute | solution.py:520
  105.2 26.7 %collective-permute-start.26 = (bf16[12,80,384]{2,1,0:T(8,128)(2,1)S(1)}, bf16[12,80,384]{2,1,0:T(8,128)(2,1)S(1)}, u32[]{:S(2)}, u32[]{:S(2)}) collective-permute-start(bf16[12,80,384]{2,1,0:T(8,128)(2,1)S(1)} %spread_blocks.5), channel_id=1, source_target_pairs={{0,4},{4,0},{8,12},{12,8},{16,20},{20,16},{24,28},{28,24},{1,5},{5... | collective-permute-start | bytes 2211848 | tf_op jit(solution)/shard_map/ppermute | solution.py:520
  124.0 12.1 %collective-permute-start.31 = (bf16[688,384]{1,0:T(8,128)(2,1)S(1)}, bf16[688,384]{1,0:T(8,128)(2,1)S(1)}, u32[]{:S(2)}, u32[]{:S(2)}) collective-permute-start(bf16[688,384]{1,0:T(8,128)(2,1)S(1)} %get-tuple-element.131), channel_id=1, source_target_pairs={{8,16},{12,20},{16,8},{20,12},{9,17},{13,21},{17,9},{21,13},{10,18... | collective-permute-start | bytes 1585160 | tf_op jit(solution)/shard_map/ppermute | solution.py:520
  125.1 13.9 %collective-permute-start.29 = (bf16[688,384]{1,0:T(8,128)(2,1)S(1)}, bf16[688,384]{1,0:T(8,128)(2,1)S(1)}, u32[]{:S(2)}, u32[]{:S(2)}) collective-permute-start(bf16[688,384]{1,0:T(8,128)(2,1)S(1)} %get-tuple-element.133), channel_id=1, source_target_pairs={{0,8},{4,12},{8,0},{12,4},{16,24},{20,28},{24,16},{28,20},{1,9},{5... | collective-permute-start | bytes 1585160 | tf_op jit(solution)/shard_map/ppermute | solution.py:520
  130.4 12.3 %collective-permute-start.12 = (bf16[2,176,384]{2,1,0:T(8,128)(2,1)S(1)}, bf16[2,176,384]{2,1,0:T(8,128)(2,1)S(1)}, u32[]{:S(2)}, u32[]{:S(2)}) collective-permute-start(bf16[2,176,384]{2,1,0:T(8,128)(2,1)S(1)} %get-tuple-element.70), channel_id=1, source_target_pairs={{0,1},{1,0},{2,3},{3,2},{4,5},{5,4},{6,7},{7,6},{8,9},{9,8},{10,11... | collective-permute-start | bytes 811016 | tf_op jit(solution)/shard_map/ppermute | solution.py:520
  130.5 13.8 %collective-permute-start.13 = (bf16[2,176,384]{2,1,0:T(8,128)(2,1)S(1)}, bf16[2,176,384]{2,1,0:T(8,128)(2,1)S(1)}, u32[]{:S(2)}, u32[]{:S(2)}) collective-permute-start(bf16[2,176,384]{2,1,0:T(8,128)(2,1)S(1)} %get-tuple-element.71), channel_id=1, source_target_pairs={{0,2},{1,3},{2,0},{3,1},{4,6},{5,7},{6,4},{7,5},{8,10},{9,11},{10,... | collective-permute-start | bytes 811016 | tf_op jit(solution)/shard_map/ppermute | solution.py:520
  131.9 12.8 %collective-permute-start.14 = (bf16[2,176,384]{2,1,0:T(8,128)(2,1)S(1)}, bf16[2,176,384]{2,1,0:T(8,128)(2,1)S(1)}, u32[]{:S(2)}, u32[]{:S(2)}) collective-permute-start(bf16[2,176,384]{2,1,0:T(8,128)(2,1)S(1)} %get-tuple-element.72), channel_id=1, source_target_pairs={{0,3},{1,2},{2,1},{3,0},{4,7},{5,6},{6,5},{7,4},{8,11},{9,10},{10,... | collective-permute-start | bytes 811016 | tf_op jit(solution)/shard_map/ppermute | solution.py:520
  136.1 19.3 %collective-permute-start.40 = (bf16[688,384]{1,0:T(8,128)(2,1)S(1)}, bf16[688,384]{1,0:T(8,128)(2,1)S(1)}, u32[]{:S(2)}, u32[]{:S(2)}) collective-permute-start(bf16[688,384]{1,0:T(8,128)(2,1)S(1)} %get-tuple-element.130), channel_id=1, source_target_pairs={{8,16},{12,20},{16,8},{20,12},{9,17},{13,21},{17,9},{21,13},{10,18... | collective-permute-start | bytes 1585160 | tf_op jit(solution)/shard_map/ppermute | solution.py:520
  139.0 16.3 %collective-permute-start.39 = (bf16[688,384]{1,0:T(8,128)(2,1)S(1)}, bf16[688,384]{1,0:T(8,128)(2,1)S(1)}, u32[]{:S(2)}, u32[]{:S(2)}) collective-permute-start(bf16[688,384]{1,0:T(8,128)(2,1)S(1)} %get-tuple-element.132), channel_id=1, source_target_pairs={{0,8},{4,12},{8,0},{12,4},{16,24},{20,28},{24,16},{28,20},{1,9},{5... | collective-permute-start | bytes 1585160 | tf_op jit(solution)/shard_map/ppermute | solution.py:520
  155.6 10.5 %collective-permute-start.41 = (bf16[176,384]{1,0:T(8,128)(2,1)S(1)}, bf16[176,384]{1,0:T(8,128)(2,1)S(1)}, u32[]{:S(2)}, u32[]{:S(2)}) collective-permute-start(bf16[176,384]{1,0:T(8,128)(2,1)S(1)} %get-tuple-element.92), channel_id=1, source_target_pairs={{0,2},{1,3},{2,0},{3,1},{4,6},{5,7},{6,4},{7,5},{8,10},{9,11},{10,... | collective-permute-start | bytes 405512 | tf_op jit(solution)/shard_map/ppermute | solution.py:520
  157.1 9.1 %collective-permute-start.42 = (bf16[176,384]{1,0:T(8,128)(2,1)S(1)}, bf16[176,384]{1,0:T(8,128)(2,1)S(1)}, u32[]{:S(2)}, u32[]{:S(2)}) collective-permute-start(bf16[176,384]{1,0:T(8,128)(2,1)S(1)} %get-tuple-element.93), channel_id=1, source_target_pairs={{0,1},{1,0},{2,3},{3,2},{4,5},{5,4},{6,7},{7,6},{8,9},{9,8},{10,11... | collective-permute-start | bytes 405512 | tf_op jit(solution)/shard_map/ppermute | solution.py:520
  157.5 9.8 %collective-permute-start.43 = (bf16[176,384]{1,0:T(8,128)(2,1)S(1)}, bf16[176,384]{1,0:T(8,128)(2,1)S(1)}, u32[]{:S(2)}, u32[]{:S(2)}) collective-permute-start(bf16[176,384]{1,0:T(8,128)(2,1)S(1)} %get-tuple-element.94), channel_id=1, source_target_pairs={{0,3},{1,2},{2,1},{3,0},{4,7},{5,6},{6,5},{7,4},{8,11},{9,10},{10,... | collective-permute-start | bytes 405512 | tf_op jit(solution)/shard_map/ppermute | solution.py:520
  162.2 16.6 %collective-permute-start.47 = (bf16[688,384]{1,0:T(8,128)(2,1)S(1)}, bf16[688,384]{1,0:T(8,128)(2,1)S(1)}, u32[]{:S(2)}, u32[]{:S(2)}) collective-permute-start(bf16[688,384]{1,0:T(8,128)(2,1)S(1)} %gather_rows.2.rest_0_.refs_10_), channel_id=1, source_target_pairs={{0,8},{4,12},{8,0},{12,4},{16,24},{20,28},{24,16},{28,20},{1,9},{5... | collective-permute-start | bytes 1585160 | tf_op jit(solution)/shard_map/ppermute | solution.py:520
  162.3 16.5 %collective-permute-start.38 = (bf16[688,384]{1,0:T(8,128)(2,1)S(1)}, bf16[688,384]{1,0:T(8,128)(2,1)S(1)}, u32[]{:S(2)}, u32[]{:S(2)}) collective-permute-start(bf16[688,384]{1,0:T(8,128)(2,1)S(1)} %gather_rows.2.rest_0_.refs_10_), channel_id=1, source_target_pairs={{8,16},{12,20},{16,8},{20,12},{9,17},{13,21},{17,9},{21,13},{10,18... | collective-permute-start | bytes 1585160 | tf_op jit(solution)/shard_map/ppermute | solution.py:520
  179.0 20.3 %collective-permute-start.57 = (f32[2,192,768]{2,1,0:T(8,128)S(1)}, f32[2,192,768]{2,1,0:T(8,128)S(1)}, u32[]{:S(2)}, u32[]{:S(2)}) collective-permute-start(f32[2,192,768]{2,1,0:T(8,128)S(1)} %bitcast.115), channel_id=1, source_target_pairs={{0,1},{1,0},{2,3},{3,2},{4,5},{5,4},{6,7},{7,6},{8,9},{9,8},{10,11... | collective-permute-start | bytes 3538952 | tf_op jit(solution)/shard_map/ppermute | solution.py:520
  179.8 14.0 %collective-permute-start.49 = (bf16[688,384]{1,0:T(8,128)(2,1)S(1)}, bf16[688,384]{1,0:T(8,128)(2,1)S(1)}, u32[]{:S(2)}, u32[]{:S(2)}) collective-permute-start(bf16[688,384]{1,0:T(8,128)(2,1)S(1)} %gather_rows.3.rest_1_.refs_11_), channel_id=1, source_target_pairs={{0,8},{4,12},{8,0},{12,4},{16,24},{20,28},{24,16},{28,20},{1,9},{5... | collective-permute-start | bytes 1585160 | tf_op jit(solution)/shard_map/ppermute | solution.py:520
  181.1 16.0 %collective-permute-start.48 = (bf16[688,384]{1,0:T(8,128)(2,1)S(1)}, bf16[688,384]{1,0:T(8,128)(2,1)S(1)}, u32[]{:S(2)}, u32[]{:S(2)}) collective-permute-start(bf16[688,384]{1,0:T(8,128)(2,1)S(1)} %gather_rows.3.rest_1_.refs_11_), channel_id=1, source_target_pairs={{8,16},{12,20},{16,8},{20,12},{9,17},{13,21},{17,9},{21,13},{10,18... | collective-permute-start | bytes 1585160 | tf_op jit(solution)/shard_map/ppermute | solution.py:520
  185.0 22.2 %collective-permute-start.53 = (bf16[12,80,384]{2,1,0:T(8,128)(2,1)}, bf16[12,80,384]{2,1,0:T(8,128)(2,1)}, u32[]{:S(2)}, u32[]{:S(2)}) collective-permute-start(bf16[12,80,384]{2,1,0:T(8,128)(2,1)} %pick_bands.6), channel_id=1, source_target_pairs={{0,4},{4,0},{8,12},{12,8},{16,20},{20,16},{24,28},{28,24},{1,5},{5... | collective-permute-start | bytes 2211848 | tf_op jit(solution)/shard_map/ppermute | solution.py:520
  194.6 20.5 %collective-permute-start.50 = (bf16[1376,384]{1,0:T(8,128)(2,1)}, bf16[1376,384]{1,0:T(8,128)(2,1)}, u32[]{:S(2)}, u32[]{:S(2)}) collective-permute-start(bf16[1376,384]{1,0:T(8,128)(2,1)} %constant_dynamic-update-slice_fusion.11), channel_id=1, source_target_pairs={{8,16},{12,20},{16,8},{20,12},{9,17},{13,21},{17,9},{21,13},{10,18... | collective-permute-start | bytes 3170312 | tf_op jit(solution)/shard_map/ppermute | solution.py:520
  198.0 29.2 %collective-permute-start.52 = (bf16[1376,384]{1,0:T(8,128)(2,1)}, bf16[1376,384]{1,0:T(8,128)(2,1)}, u32[]{:S(2)}, u32[]{:S(2)}) collective-permute-start(bf16[1376,384]{1,0:T(8,128)(2,1)} %constant_dynamic-update-slice_fusion.9), channel_id=1, source_target_pairs={{8,0},{12,4},{16,24},{20,28},{9,1},{13,5},{17,25},{21,29},{10,2},{... | collective-permute-start | bytes 3170312 | tf_op jit(solution)/shard_map/ppermute | solution.py:520
  201.3 15.1 %collective-permute-start.58 = (f32[192,768]{1,0:T(8,128)}, f32[192,768]{1,0:T(8,128)}, u32[]{:S(2)}, u32[]{:S(2)}) collective-permute-start(f32[192,768]{1,0:T(8,128)} %slice_bitcast_fusion), channel_id=1, source_target_pairs={{0,2},{1,3},{2,0},{3,1},{4,6},{5,7},{6,4},{7,5},{8,10},{9,11},{10,... | collective-permute-start | bytes 1769480 | tf_op jit(solution)/shard_map/ppermute | solution.py:520
  207.2 23.8 %collective-permute-start.54 = (bf16[12,80,384]{2,1,0:T(8,128)(2,1)S(1)}, bf16[12,80,384]{2,1,0:T(8,128)(2,1)S(1)}, u32[]{:S(2)}, u32[]{:S(2)}) collective-permute-start(bf16[12,80,384]{2,1,0:T(8,128)(2,1)S(1)} %pick_bands.5), channel_id=1, source_target_pairs={{0,4},{4,0},{8,12},{12,8},{16,20},{20,16},{24,28},{28,24},{1,5},{5... | collective-permute-start | bytes 2211848 | tf_op jit(solution)/shard_map/ppermute | solution.py:520
  215.1 34.6 %collective-permute-start.51 = (bf16[1376,384]{1,0:T(8,128)(2,1)}, bf16[1376,384]{1,0:T(8,128)(2,1)S(1)}, u32[]{:S(2)}, u32[]{:S(2)}) collective-permute-start(bf16[1376,384]{1,0:T(8,128)(2,1)} %collective-permute-done.50), channel_id=1, source_target_pairs={{8,0},{12,4},{16,24},{20,28},{9,1},{13,5},{17,25},{21,29},{10,2},{... | collective-permute-start | bytes 3170312 | tf_op jit(solution)/shard_map/ppermute | solution.py:520
  217.6 17.9 %collective-permute-start.59 = (f32[96,768]{1,0:T(8,128)S(1)}, f32[96,768]{1,0:T(8,128)S(1)}, u32[]{:S(2)}, u32[]{:S(2)}) collective-permute-start(f32[96,768]{1,0:T(8,128)S(1)} %constant_dynamic-slice_fusion), channel_id=1, source_target_pairs={{0,4},{4,0},{8,12},{12,8},{16,20},{20,16},{24,28},{28,24},{1,5},{5... | collective-permute-start | bytes 884744 | tf_op jit(solution)/shard_map/ppermute | solution.py:520
  230.9 21.3 %collective-permute-start.55 = (bf16[12,80,384]{2,1,0:T(8,128)(2,1)S(1)}, bf16[12,80,384]{2,1,0:T(8,128)(2,1)S(1)}, u32[]{:S(2)}, u32[]{:S(2)}) collective-permute-start(bf16[12,80,384]{2,1,0:T(8,128)(2,1)S(1)} %pick_bands.4), channel_id=1, source_target_pairs={{0,4},{4,0},{8,12},{12,8},{16,20},{20,16},{24,28},{28,24},{1,5},{5... | collective-permute-start | bytes 2211848 | tf_op jit(solution)/shard_map/ppermute | solution.py:520
  235.6 16.7 %collective-permute-start.60 = (bf16[96,768]{1,0:T(8,128)(2,1)S(1)}, bf16[96,768]{1,0:T(8,128)(2,1)S(1)}, u32[]{:S(2)}, u32[]{:S(2)}) collective-permute-start(bf16[96,768]{1,0:T(8,128)(2,1)S(1)} %get-tuple-element.126), channel_id=1, source_target_pairs={{0,8},{4,12},{8,0},{12,4},{16,24},{20,28},{24,16},{28,20},{1,9},{5... | collective-permute-start | bytes 442376 | tf_op jit(solution)/shard_map/ppermute | solution.py:520
  252.3 16.7 %collective-permute-start.56 = (bf16[12,80,384]{2,1,0:T(8,128)(2,1)S(1)}, bf16[12,80,384]{2,1,0:T(8,128)(2,1)S(1)}, u32[]{:S(2)}, u32[]{:S(2)}) collective-permute-start(bf16[12,80,384]{2,1,0:T(8,128)(2,1)S(1)} %pick_bands.7), channel_id=1, source_target_pairs={{0,4},{4,0},{8,12},{12,8},{16,20},{20,16},{24,28},{28,24},{1,5},{5... | collective-permute-start | bytes 2211848 | tf_op jit(solution)/shard_map/ppermute | solution.py:520
  252.4 9.1 %collective-permute-start.61 = (bf16[96,768]{1,0:T(8,128)(2,1)S(1)}, bf16[96,768]{1,0:T(8,128)(2,1)S(1)}, u32[]{:S(2)}, u32[]{:S(2)}) collective-permute-start(bf16[96,768]{1,0:T(8,128)(2,1)S(1)} %fusion.1), channel_id=1, source_target_pairs={{0,16},{4,20},{8,24},{12,28},{16,0},{20,4},{24,8},{28,12},{1,17},{... | collective-permute-start | bytes 442376 | tf_op jit(solution)/shard_map/ppermute | solution.py:520
  (47 other events, 772.5 us)

commit v5 on v4

--- a/solution.py
+++ b/solution.py
@@ -443,7 +443,7 @@
             refs[len(terms) + d][...] = value.astype(jnp.bfloat16)
 
     out = jax.ShapeDtypeStruct((rows, terms[0].shape[1]), jnp.bfloat16)
-    return call(body, [out] * sides, (side,) + tuple(terms), 1, 1, "deal_rows")
+    return call(body, [out] * sides, (side,) + tuple(terms), 1, 3, "deal_rows")
 
 
 def gather(side, parts, half_rows):
@@ -456,7 +456,7 @@
             refs[-1][here, :] = refs[d][...]
 
     out = jax.ShapeDtypeStruct((half_rows, lanes), jnp.bfloat16)
-    return call(body, out, (side,) + tuple(parts), 1, 1, "gather_rows")
+    return call(body, out, (side,) + tuple(parts), 1, 3, "gather_rows")
 
 
 def turn_teacher(side, teacher, sides, padded):
@@ -658,7 +658,7 @@
     low = me % 2
     mine = lax.dynamic_slice_in_dim(grad, low * rows, rows, 0)
     other = lax.dynamic_slice_in_dim(grad, (1 - low) * rows, rows, 0)
-    grad = mine + after(swap(other, "view", 1), marks[2])
+    grad = mine + after(swap(other.astype(jnp.bfloat16), "view", 1), marks[2]).astype(jnp.float32)
     sent = grad.astype(jnp.bfloat16)
     grad = grad + after(swap(sent, "view", 2), marks[3]).astype(jnp.float32)
     sent = grad.astype(jnp.bfloat16)

time: 279 us -> 279 us (level)
  starting transfers between devices: 73.2 us -> 76.3 us
  waiting for transfers between devices: 108 us -> 105 us
    ppermute x63, waiting for transfers between devices: 108 us -> 105 us  [hop(): return lax.ppermute(value, axis, pairs)]
    ppermute x63, starting transfers between devices: 73.2 us -> 76.3 us  [hop(): return lax.ppermute(value, axis, pairs)]
  transfers between devices with their start and end apart: 63 -> 63, of which waited for: 25 -> 24; matrix products, arithmetic and copies ran while one was open for 6% -> 6% of each run, Pallas kernels for 22% -> 23%
where the time goes in v5:
time: 279 us; the launch traced here: 277 us
  waiting for transfers between devices  105 us (38%)
  starting transfers between devices  76.3 us (27%)
  Pallas kernels  62.8 us (23%)
  local copies, waits for them, and re-layouts  23.5 us (8%)
  other arithmetic  8.44 us (3%)
    ppermute x63, waiting for transfers between devices, hop(): return lax.ppermute(value, axis, pairs)  105 us
    ppermute x63, starting transfers between devices, hop(): return lax.ppermute(value, axis, pairs)  76.3 us
    pallas_call x24, Pallas kernels, call(): pl.pallas_call(body, out_shape=out_shape, in_specs=[smem] * n_scalars + [...  62.8 us
    unnamed x75, local copies, waits for them, and re-layouts  16.3 us
  transfers between devices with their start and end apart: 63, of which 24 were waited for; matrix products, arithmetic and copies ran while one was open for 6% of the time, Pallas kernels for 23%

profile of v5, /device:TPU:0, one launch (start us, length us, event | category | flops | bytes accessed | tf_op | source)
XLA Modules:
  0.0 277.1 jit_solution(16449642046260566945)
XLA Ops:
  3.3 4.1 %collective-permute-start = (s32[1,4,128]{2,1,0:T(4,128)S(1)}, s32[1,4,128]{2,1,0:T(4,128)S(1)}, u32[]{:S(2)}, u32[]{:S(2)}) collective-permute-start(s32[1,4,128]{2,1,0:T(4,128)S(1)} %add_bitcast_fusion), channel_id=1, source_target_pairs={{0,16},{4,20},{8,24},{12,28},{16,0},{20,4},{24,8},{28,12},{1,17},{... | collective-permute-start | bytes 6152 | tf_op jit(solution)/shard_map/ppermute | solution.py:520
  8.0 3.3 %copy.22 = bf16[2,64,74,128]{3,2,1,0:T(8,128)(2,1)S(1)} copy(bf16[2,64,74,128]{3,1,2,0:T(8,128)(2,1)} %param.10) | data formatting | bytes 4849664 | tf_op args[3]
  14.1 4.3 %collective-permute-start.4 = (bf16[6,80,128]{2,1,0:T(8,128)(2,1)S(1)}, bf16[6,80,128]{2,1,0:T(8,128)(2,1)S(1)}, u32[]{:S(2)}, u32[]{:S(2)}) collective-permute-start(bf16[6,80,128]{2,1,0:T(8,128)(2,1)S(1)} %get-tuple-element.63), channel_id=1, source_target_pairs={{0,28},{4,24},{8,20},{12,16},{16,12},{20,8},{24,4},{28,0},{1,29},{... | collective-permute-start | bytes 368648 | tf_op jit(solution)/shard_map/ppermute | solution.py:520
  20.5 4.6 %collective-permute-done.2 = s32[4,4,128]{2,1,0:T(4,128)S(1)} collective-permute-done((s32[4,4,128]{2,1,0:T(4,128)S(1)}, s32[4,4,128]{2,1,0:T(4,128)S(1)}, u32[]{:S(2)}, u32[]{:S(2)}) %collective-permute-start.2) | collective-permute-done | bytes 8224 | tf_op jit(solution)/shard_map/ppermute | solution.py:520
  27.0 2.9 %collective-permute-start.20 = (bf16[6,80,128]{2,1,0:T(8,128)(2,1)S(1)}, bf16[6,80,128]{2,1,0:T(8,128)(2,1)S(1)}, u32[]{:S(2)}, u32[]{:S(2)}) collective-permute-start(bf16[6,80,128]{2,1,0:T(8,128)(2,1)S(1)} %get-tuple-element.77), channel_id=1, source_target_pairs={{0,20},{4,16},{8,28},{12,24},{16,4},{20,0},{24,12},{28,8},{1,21},{... | collective-permute-start | bytes 368648 | tf_op jit(solution)/shard_map/ppermute | solution.py:520
  31.5 3.0 %collective-permute-done.19 = bf16[6,80,128]{2,1,0:T(8,128)(2,1)S(1)} collective-permute-done((bf16[6,80,128]{2,1,0:T(8,128)(2,1)S(1)}, bf16[6,80,128]{2,1,0:T(8,128)(2,1)S(1)}, u32[]{:S(2)}, u32[]{:S(2)}) %collective-permute-start.19) | collective-permute-done | bytes 122912 | tf_op jit(solution)/shard_map/ppermute | solution.py:520
  34.5 3.0 %collective-permute-done.20 = bf16[6,80,128]{2,1,0:T(8,128)(2,1)S(1)} collective-permute-done((bf16[6,80,128]{2,1,0:T(8,128)(2,1)S(1)}, bf16[6,80,128]{2,1,0:T(8,128)(2,1)S(1)}, u32[]{:S(2)}, u32[]{:S(2)}) %collective-permute-start.20) | collective-permute-done | bytes 122912 | tf_op jit(solution)/shard_map/ppermute | solution.py:520
  40.5 4.2 %collective-permute-done.21 = bf16[2,6,80,128]{3,2,1,0:T(8,128)(2,1)S(1)} collective-permute-done((bf16[2,6,80,128]{3,2,1,0:T(8,128)(2,1)S(1)}, bf16[2,6,80,128]{3,2,1,0:T(8,128)(2,1)S(1)}, u32[]{:S(2)}, u32[]{:S(2)}) %collective-permute-start.21) | collective-permute-done | bytes 245792 | tf_op jit(solution)/shard_map/ppermute | solution.py:520
  52.1 6.6 %collective-permute-done.8 = bf16[2,6,80,128]{3,2,1,0:T(8,128)(2,1)S(1)} collective-permute-done((bf16[2,6,80,128]{3,2,1,0:T(8,128)(2,1)S(1)}, bf16[2,6,80,128]{3,2,1,0:T(8,128)(2,1)S(1)}, u32[]{:S(2)}, u32[]{:S(2)}) %collective-permute-start.8) | collective-permute-done | bytes 245792 | tf_op jit(solution)/shard_map/ppermute | solution.py:520
  58.9 4.4 %collective-permute-done.17 = bf16[2,6,80,128]{3,2,1,0:T(8,128)(2,1)S(1)} collective-permute-done((bf16[2,6,80,128]{3,2,1,0:T(8,128)(2,1)S(1)}, bf16[2,6,80,128]{3,2,1,0:T(8,128)(2,1)S(1)}, u32[]{:S(2)}, u32[]{:S(2)}) %collective-permute-start.17) | collective-permute-done | bytes 245792 | tf_op jit(solution)/shard_map/ppermute | solution.py:520
  63.4 2.0 spread_blocks.7
  65.7 2.2 collective-permute-done.23.other_ref
  68.8 3.9 %render_blocks.7 = bf16[1376,384]{1,0:T(8,128)(2,1)S(1)} custom-call(s32[1]{0:T(128)} %get-tuple-element.177.count_ref.refs_3_, s32[24]{0:T(128)S(1)} %get-tuple-element.158.block_ref, s32[24]{0:T(128)S(1)} %get-tuple-element.188.place_ref.refs_5_, s32[24]{0:T(128)S(1)} %fusion.10.where_ref.refs_0_, s32[1]{0:T(128)} %get-tuple-element.175.other_count_ref.count_ref, ...), custom_call_target="tpu_custom_call" | custom-call | flops 5000000000 | bytes 10000000 | tf_op jit(solution)/shard_map/render_blocks/pallas_call | solution.py:120
  75.9 2.2 spread_blocks.6
  78.1 4.4 %collective-permute-done.10 = bf16[192,768]{1,0:T(8,128)(2,1)S(1)} collective-permute-done((bf16[192,768]{1,0:T(8,128)(2,1)S(1)}, bf16[192,768]{1,0:T(8,128)(2,1)S(1)}, u32[]{:S(2)}, u32[]{:S(2)}) %collective-permute-start.10) | collective-permute-done | bytes 294944 | tf_op jit(solution)/shard_map/ppermute | solution.py:520
  82.6 3.3 %collective-permute-done.24.other_ref = bf16[12,80,384]{2,1,0:T(8,128)(2,1)S(1)} collective-permute-done((bf16[12,80,384]{2,1,0:T(8,128)(2,1)S(1)}, bf16[12,80,384]{2,1,0:T(8,128)(2,1)S(1)}, u32[]{:S(2)}, u32[]{:S(2)}) %collective-permute-start.24) | collective-permute-done | bytes 737312 | tf_op jit(solution)/shard_map/ppermute | solution.py:520
  86.9 4.2 %render_blocks.6 = bf16[1376,384]{1,0:T(8,128)(2,1)S(1)} custom-call(s32[1]{0:T(128)} %get-tuple-element.178.count_ref.refs_3_, s32[24]{0:T(128)S(1)} %get-tuple-element.159.block_ref, s32[24]{0:T(128)S(1)} %get-tuple-element.187.place_ref.refs_5_, s32[24]{0:T(128)S(1)} %fusion.10.where_ref.refs_0_, s32[1]{0:T(128)} %get-tuple-element.173.other_count_ref.count_ref, ...), custom_call_target="tpu_custom_call" | custom-call | flops 5000000000 | bytes 10000000 | tf_op jit(solution)/shard_map/render_blocks/pallas_call | solution.py:120
  91.1 5.4 %collective-permute-done.27 = bf16[1376,384]{1,0:T(8,128)(2,1)S(1)} collective-permute-done((bf16[1376,384]{1,0:T(8,128)(2,1)S(1)}, bf16[1376,384]{1,0:T(8,128)(2,1)S(1)}, u32[]{:S(2)}, u32[]{:S(2)}) %collective-permute-start.27) | collective-permute-done | bytes 1056800 | tf_op jit(solution)/shard_map/ppermute | solution.py:520
  96.8 4.5 %collective-permute-start.30 = (bf16[1376,384]{1,0:T(8,128)(2,1)S(1)}, bf16[1376,384]{1,0:T(8,128)(2,1)S(1)}, u32[]{:S(2)}, u32[]{:S(2)}) collective-permute-start(bf16[1376,384]{1,0:T(8,128)(2,1)S(1)} %add_convert_fusion), channel_id=1, source_target_pairs={{0,8},{4,12},{24,16},{28,20},{1,9},{5,13},{25,17},{29,21},{2,10},{... | collective-permute-start | bytes 3170312 | tf_op jit(solution)/shard_map/ppermute | solution.py:520
  104.1 2.4 collective-permute-start.26
  106.5 4.2 %render_blocks.5 = bf16[1376,384]{1,0:T(8,128)(2,1)S(1)} custom-call(s32[1]{0:T(128)} %get-tuple-element.176.count_ref.refs_6_, s32[24]{0:T(128)S(1)} %get-tuple-element.157.block_ref, s32[24]{0:T(128)S(1)} %get-tuple-element.189.place_ref.refs_8_, s32[24]{0:T(128)S(1)} %fusion.10.where_ref.refs_0_, s32[1]{0:T(128)} %get-tuple-element.172.other_count_ref.count_ref, ...), custom_call_target="tpu_custom_call" | custom-call | flops 5000000000 | bytes 10000000 | tf_op jit(solution)/shard_map/render_blocks/pallas_call | solution.py:120
  110.7 12.0 %collective-permute-done.30 = bf16[1376,384]{1,0:T(8,128)(2,1)S(1)} collective-permute-done((bf16[1376,384]{1,0:T(8,128)(2,1)S(1)}, bf16[1376,384]{1,0:T(8,128)(2,1)S(1)}, u32[]{:S(2)}, u32[]{:S(2)}) %collective-permute-start.30) | collective-permute-done | bytes 1056800 | tf_op jit(solution)/shard_map/ppermute | solution.py:520
  124.2 4.0 %collective-permute-start.29 = (bf16[688,384]{1,0:T(8,128)(2,1)S(1)}, bf16[688,384]{1,0:T(8,128)(2,1)S(1)}, u32[]{:S(2)}, u32[]{:S(2)}) collective-permute-start(bf16[688,384]{1,0:T(8,128)(2,1)S(1)} %get-tuple-element.131), channel_id=1, source_target_pairs={{0,8},{4,12},{8,0},{12,4},{16,24},{20,28},{24,16},{28,20},{1,9},{5... | collective-permute-start | bytes 1585160 | tf_op jit(solution)/shard_map/ppermute | solution.py:520
  131.0 4.3 %render_blocks.4.refs_0_ = bf16[1376,384]{1,0:T(8,128)(2,1)S(1)} custom-call(s32[1]{0:T(128)} %get-tuple-element.182.count_ref.refs_1_, s32[24]{0:T(128)S(1)} %get-tuple-element.163.block_ref, s32[24]{0:T(128)S(1)} %get-tuple-element.186.place_ref.refs_3_, s32[24]{0:T(128)S(1)} %fusion.10.where_ref.refs_0_, s32[1]{0:T(128)} %get-tuple-element.174.other_count_ref.count_ref, ...), custom_call_target="tpu_custom_call" | custom-call | flops 5000000000 | bytes 10000000 | tf_op jit(solution)/shard_map/render_blocks/pallas_call | solution.py:120
  137.9 3.4 %collective-permute-start.39 = (bf16[688,384]{1,0:T(8,128)(2,1)S(1)}, bf16[688,384]{1,0:T(8,128)(2,1)S(1)}, u32[]{:S(2)}, u32[]{:S(2)}) collective-permute-start(bf16[688,384]{1,0:T(8,128)(2,1)S(1)} %get-tuple-element.130), channel_id=1, source_target_pairs={{0,8},{4,12},{8,0},{12,4},{16,24},{20,28},{24,16},{28,20},{1,9},{5... | collective-permute-start | bytes 1585160 | tf_op jit(solution)/shard_map/ppermute | solution.py:520
  143.4 2.0 collective-permute-start.34
  146.7 2.1 collective-permute-done.34.refs_6_
  148.8 2.8 %loss_rows.2 = (bf16[176,384]{1,0:T(8,128)(2,1)S(1)}, bf16[176,384]{1,0:T(8,128)(2,1)S(1)}, bf16[176,384]{1,0:T(8,128)(2,1)S(1)}, bf16[176,384]{1,0:T(8,128)(2,1)S(1)}, f32[768,768]{1,0:T(8,128)S(1)}) custom-call(s32[1]{0:T(128)} %bitcast.18.side_ref.refs_0_, bf16[768,768]{1,0:T(8,128)(2,1)S(1)} %constant_dynamic-update-slice_fusion.3.refs_1_, ...), custom_call_target="tpu_custom_call" | custom-call | flops 3000000000 | bytes 6000000 | tf_op jit(solution)/shard_map/loss_rows/pallas_call | solution.py:120
  156.8 2.2 collective-permute-done.36.refs_2_
  159.0 2.2 collective-permute-done.37.refs_3_
  162.0 2.8 collective-permute-done.41.refs_4_
  166.1 2.8 %loss_rows.3 = (bf16[176,384]{1,0:T(8,128)(2,1)S(1)}, bf16[176,384]{1,0:T(8,128)(2,1)S(1)}, bf16[176,384]{1,0:T(8,128)(2,1)S(1)}, bf16[176,384]{1,0:T(8,128)(2,1)S(1)}, f32[768,768]{1,0:T(8,128)S(1)}) custom-call(s32[1]{0:T(128)} %bitcast.18.side_ref.refs_0_, bf16[768,768]{1,0:T(8,128)(2,1)S(1)} %constant_dynamic-update-slice_fusion.3.refs_1_, ...), custom_call_target="tpu_custom_call" | custom-call | flops 3000000000 | bytes 6000000 | tf_op jit(solution)/shard_map/loss_rows/pallas_call | solution.py:120
  171.6 4.7 %collective-permute-done.45.refs_2_ = bf16[176,384]{1,0:T(8,128)(2,1)S(1)} collective-permute-done((bf16[176,384]{1,0:T(8,128)(2,1)S(1)}, bf16[176,384]{1,0:T(8,128)(2,1)S(1)}, u32[]{:S(2)}, u32[]{:S(2)}) %collective-permute-start.45) | collective-permute-done | bytes 135200 | tf_op jit(solution)/shard_map/ppermute | solution.py:520
  180.7 3.2 %pick_bands.6 = bf16[12,80,384]{2,1,0:T(8,128)(2,1)} custom-call(s32[1]{0:T(128)} %get-tuple-element.174.other_count_ref.count_ref, s32[24]{0:T(128)S(1)} %get-tuple-element.167.other_place_ref.place_ref, bf16[688,384]{1,0:T(8,128)(2,1)S(1)} %gather_rows.2.rest_0_.refs_10_, bf16[688,384]{1,0:T(8,128)(2,1)S(1)} %gather_rows.3.rest_1_.refs_11_), custom_call_target="tpu_custom_call" | custom-call | flops 100000000 | bytes 200000 | tf_op jit(solution)/shard_map/pick_bands/pallas_call | solution.py:120
  185.6 7.0 %collective-permute-done.49.rest_1_.refs_16_ = bf16[688,384]{1,0:T(8,128)(2,1)S(1)} collective-permute-done((bf16[688,384]{1,0:T(8,128)(2,1)S(1)}, bf16[688,384]{1,0:T(8,128)(2,1)S(1)}, u32[]{:S(2)}, u32[]{:S(2)}) %collective-permute-start.49) | collective-permute-done | bytes 528416 | tf_op jit(solution)/shard_map/ppermute | solution.py:520
  203.7 2.5 pick_bands.5
  208.4 7.1 %pull_blocks.4.refs_10_ = f32[65,192,128]{2,1,0:T(8,128)S(1)} custom-call(s32[24]{0:T(128)S(1)} %fusion.10.where_ref.refs_0_, s32[1]{0:T(128)} %get-tuple-element.182.count_ref.refs_1_, s32[24]{0:T(128)S(1)} %get-tuple-element.149.refs_2_, s32[24]{0:T(128)S(1)} %copy-done.22, s32[1]{0:T(128)} %get-tuple-element.181.count_ref.refs_4_, ...), custom_call_target="tpu_custom_call" | custom-call | flops 100000000 | bytes 200000 | tf_op jit(solution)/shard_map/pull_blocks/pallas_call | solution.py:120
  218.0 3.2 %collective-permute-start.59 = (bf16[96,768]{1,0:T(8,128)(2,1)S(1)}, bf16[96,768]{1,0:T(8,128)(2,1)S(1)}, u32[]{:S(2)}, u32[]{:S(2)}) collective-permute-start(bf16[96,768]{1,0:T(8,128)(2,1)S(1)} %dynamic-slice_convert_fusion), channel_id=1, source_target_pairs={{0,4},{4,0},{8,12},{12,8},{16,20},{20,16},{24,28},{28,24},{1,5},{5... | collective-permute-start | bytes 442376 | tf_op jit(solution)/shard_map/ppermute | solution.py:520
  221.2 5.1 %collective-permute-done.52 = bf16[1376,384]{1,0:T(8,128)(2,1)} collective-permute-done((bf16[1376,384]{1,0:T(8,128)(2,1)}, bf16[1376,384]{1,0:T(8,128)(2,1)}, u32[]{:S(2)}, u32[]{:S(2)}) %collective-permute-start.52) | collective-permute-done | bytes 1056800 | tf_op jit(solution)/shard_map/ppermute | solution.py:520
  227.8 2.2 pick_bands.4
  230.9 4.8 %pull_blocks.5.refs_10_ = f32[65,192,128]{2,1,0:T(8,128)S(1)} custom-call(s32[24]{0:T(128)S(1)} %fusion.10.where_ref.refs_0_, s32[1]{0:T(128)} %get-tuple-element.180.count_ref.refs_1_, s32[24]{0:T(128)S(1)} %get-tuple-element.151.refs_2_, s32[1]{0:T(128)} %get-tuple-element.178.count_ref.refs_3_, s32[24]{0:T(128)S(1)} %get-tuple-element.150.refs_4_, ...), custom_call_target="tpu_custom_call" | custom-call | flops 100000000 | bytes 200000 | tf_op jit(solution)/shard_map/pull_blocks/pallas_call | solution.py:120
  236.8 12.1 %collective-permute-done.51 = bf16[1376,384]{1,0:T(8,128)(2,1)S(1)} collective-permute-done((bf16[1376,384]{1,0:T(8,128)(2,1)}, bf16[1376,384]{1,0:T(8,128)(2,1)S(1)}, u32[]{:S(2)}, u32[]{:S(2)}) %collective-permute-start.51) | collective-permute-done | bytes 1056800 | tf_op jit(solution)/shard_map/ppermute | solution.py:520
  249.1 2.2 pick_bands.7
  253.5 4.3 %pull_blocks.6.refs_5_ = f32[65,192,128]{2,1,0:T(8,128)S(1)} custom-call(s32[24]{0:T(128)S(1)} %fusion.10.where_ref.refs_0_, s32[1]{0:T(128)} %get-tuple-element.179.count_ref.refs_1_, s32[24]{0:T(128)S(1)} %get-tuple-element.146.refs_2_, s32[1]{0:T(128)} %get-tuple-element.177.count_ref.refs_3_, s32[24]{0:T(128)S(1)} %get-tuple-element.145.refs_4_, ...), custom_call_target="tpu_custom_call" | custom-call | flops 100000000 | bytes 200000 | tf_op jit(solution)/shard_map/pull_blocks/pallas_call | solution.py:120
  257.8 2.6 copy-done.1
  260.5 7.6 %collective-permute-done.56.refs_4_ = bf16[12,80,384]{2,1,0:T(8,128)(2,1)S(1)} collective-permute-done((bf16[12,80,384]{2,1,0:T(8,128)(2,1)S(1)}, bf16[12,80,384]{2,1,0:T(8,128)(2,1)S(1)}, u32[]{:S(2)}, u32[]{:S(2)}) %collective-permute-start.56) | collective-permute-done | bytes 737312 | tf_op jit(solution)/shard_map/ppermute | solution.py:520
  269.0 2.8 %copy-done.2 = f32[65,192,128]{2,1,0:T(8,128)S(1)} copy-done((f32[65,192,128]{2,1,0:T(8,128)S(1)}, f32[65,192,128]{2,1,0:T(8,128)}, u32[]{:S(2)}) %copy-start.2) | copy-done | bytes 6389784
  271.8 4.4 %pull_blocks.7 = bf16[64,192,128]{2,1,0:T(8,128)(2,1)} custom-call(s32[24]{0:T(128)S(1)} %fusion.10.where_ref.refs_0_, s32[1]{0:T(128)} %get-tuple-element.183.count_ref.refs_1_, s32[24]{0:T(128)S(1)} %copy-done.27, bf16[24,80,128]{2,1,0:T(8,128)(2,1)S(1)} %get-tuple-element.137.weight_ref.refs_3_, bf16[12,80,384]{2,1,0:T(8,128)(2,1)S(1)} %collective-permute-done.56.refs_4_, ...), custom_call_target="tpu_custom_call" | custom-call | flops 100000000 | bytes 200000 | tf_op jit(solution)/shard_map/pull_blocks/pallas_call | solution.py:120
  (249 shorter events, 80.2 us)
Async XLA Ops:
  3.3 7.9 %collective-permute-start = (s32[1,4,128]{2,1,0:T(4,128)S(1)}, s32[1,4,128]{2,1,0:T(4,128)S(1)}, u32[]{:S(2)}, u32[]{:S(2)}) collective-permute-start(s32[1,4,128]{2,1,0:T(4,128)S(1)} %add_bitcast_fusion), channel_id=1, source_target_pairs={{0,16},{4,20},{8,24},{12,28},{16,0},{20,4},{24,8},{28,12},{1,17},{... | collective-permute-start | bytes 6152 | tf_op jit(solution)/shard_map/ppermute | solution.py:520
  11.3 7.7 %collective-permute-start.1 = (s32[2,4,128]{2,1,0:T(4,128)S(1)}, s32[2,4,128]{2,1,0:T(4,128)S(1)}, u32[]{:S(2)}, u32[]{:S(2)}) collective-permute-start(s32[2,4,128]{2,1,0:T(4,128)S(1)} %pad_add_fusion.2), channel_id=1, source_target_pairs={{0,8},{4,12},{8,0},{12,4},{16,24},{20,28},{24,16},{28,20},{1,9},{5... | collective-permute-start | bytes 12296 | tf_op jit(solution)/shard_map/ppermute | solution.py:520
  13.5 13.4 %collective-permute-start.3 = (bf16[6,80,128]{2,1,0:T(8,128)(2,1)S(1)}, bf16[6,80,128]{2,1,0:T(8,128)(2,1)S(1)}, u32[]{:S(2)}, u32[]{:S(2)}) collective-permute-start(bf16[6,80,128]{2,1,0:T(8,128)(2,1)S(1)} %get-tuple-element.62), channel_id=1, source_target_pairs={{0,24},{4,28},{8,16},{12,20},{16,8},{20,12},{24,0},{28,4},{1,25},{... | collective-permute-start | bytes 368648 | tf_op jit(solution)/shard_map/ppermute | solution.py:520
  14.1 15.8 %collective-permute-start.4 = (bf16[6,80,128]{2,1,0:T(8,128)(2,1)S(1)}, bf16[6,80,128]{2,1,0:T(8,128)(2,1)S(1)}, u32[]{:S(2)}, u32[]{:S(2)}) collective-permute-start(bf16[6,80,128]{2,1,0:T(8,128)(2,1)S(1)} %get-tuple-element.63), channel_id=1, source_target_pairs={{0,28},{4,24},{8,20},{12,16},{16,12},{20,8},{24,4},{28,0},{1,29},{... | collective-permute-start | bytes 368648 | tf_op jit(solution)/shard_map/ppermute | solution.py:520
  18.4 22.1 %collective-permute-start.7 = (bf16[6,80,128]{2,1,0:T(8,128)(2,1)S(1)}, bf16[6,80,128]{2,1,0:T(8,128)(2,1)S(1)}, u32[]{:S(2)}, u32[]{:S(2)}) collective-permute-start(bf16[6,80,128]{2,1,0:T(8,128)(2,1)S(1)} %get-tuple-element.65), channel_id=1, source_target_pairs={{0,4},{4,0},{8,12},{12,8},{16,20},{20,16},{24,28},{28,24},{1,5},{5... | collective-permute-start | bytes 368648 | tf_op jit(solution)/shard_map/ppermute | solution.py:520
  18.9 26.0 %collective-permute-start.15 = (bf16[6,80,128]{2,1,0:T(8,128)(2,1)S(1)}, bf16[6,80,128]{2,1,0:T(8,128)(2,1)S(1)}, u32[]{:S(2)}, u32[]{:S(2)}) collective-permute-start(bf16[6,80,128]{2,1,0:T(8,128)(2,1)S(1)} %get-tuple-element.73), channel_id=1, source_target_pairs={{0,8},{4,12},{8,0},{12,4},{16,24},{20,28},{24,16},{28,20},{1,9},{5... | collective-permute-start | bytes 368648 | tf_op jit(solution)/shard_map/ppermute | solution.py:520
  25.1 9.4 %collective-permute-start.19 = (bf16[6,80,128]{2,1,0:T(8,128)(2,1)S(1)}, bf16[6,80,128]{2,1,0:T(8,128)(2,1)S(1)}, u32[]{:S(2)}, u32[]{:S(2)}) collective-permute-start(bf16[6,80,128]{2,1,0:T(8,128)(2,1)S(1)} %get-tuple-element.76), channel_id=1, source_target_pairs={{0,16},{4,20},{8,24},{12,28},{16,0},{20,4},{24,8},{28,12},{1,17},{... | collective-permute-start | bytes 368648 | tf_op jit(solution)/shard_map/ppermute | solution.py:520
  27.0 10.5 %collective-permute-start.20 = (bf16[6,80,128]{2,1,0:T(8,128)(2,1)S(1)}, bf16[6,80,128]{2,1,0:T(8,128)(2,1)S(1)}, u32[]{:S(2)}, u32[]{:S(2)}) collective-permute-start(bf16[6,80,128]{2,1,0:T(8,128)(2,1)S(1)} %get-tuple-element.77), channel_id=1, source_target_pairs={{0,20},{4,16},{8,28},{12,24},{16,4},{20,0},{24,12},{28,8},{1,21},{... | collective-permute-start | bytes 368648 | tf_op jit(solution)/shard_map/ppermute | solution.py:520
  29.9 9.1 %collective-permute-start.5 = (bf16[2,6,80,128]{3,2,1,0:T(8,128)(2,1)S(1)}, bf16[2,6,80,128]{3,2,1,0:T(8,128)(2,1)S(1)}, u32[]{:S(2)}, u32[]{:S(2)}) collective-permute-start(bf16[2,6,80,128]{3,2,1,0:T(8,128)(2,1)S(1)} %pad_maximum_fusion.8), channel_id=1, source_target_pairs={{0,2},{1,3},{2,0},{3,1},{4,6},{5,7},{6,4},{7,5},{8,10},{9,11},{10,... | collective-permute-start | bytes 737288 | tf_op jit(solution)/shard_map/ppermute | solution.py:520
  34.5 10.4 %collective-permute-start.16 = (bf16[6,80,128]{2,1,0:T(8,128)(2,1)S(1)}, bf16[6,80,128]{2,1,0:T(8,128)(2,1)S(1)}, u32[]{:S(2)}, u32[]{:S(2)}) collective-permute-start(bf16[6,80,128]{2,1,0:T(8,128)(2,1)S(1)} %get-tuple-element.74), channel_id=1, source_target_pairs={{0,12},{4,8},{8,4},{12,0},{16,28},{20,24},{24,20},{28,16},{1,13},{... | collective-permute-start | bytes 368648 | tf_op jit(solution)/shard_map/ppermute | solution.py:520
  48.9 18.9 %collective-permute-start.23 = (bf16[12,80,384]{2,1,0:T(8,128)(2,1)S(1)}, bf16[12,80,384]{2,1,0:T(8,128)(2,1)S(1)}, u32[]{:S(2)}, u32[]{:S(2)}) collective-permute-start(bf16[12,80,384]{2,1,0:T(8,128)(2,1)S(1)} %spread_blocks.4), channel_id=1, source_target_pairs={{0,4},{4,0},{8,12},{12,8},{16,20},{20,16},{24,28},{28,24},{1,5},{5... | collective-permute-start | bytes 2211848 | tf_op jit(solution)/shard_map/ppermute | solution.py:520
  49.9 8.8 %collective-permute-start.8 = (bf16[2,6,80,128]{3,2,1,0:T(8,128)(2,1)S(1)}, bf16[2,6,80,128]{3,2,1,0:T(8,128)(2,1)S(1)}, u32[]{:S(2)}, u32[]{:S(2)}) collective-permute-start(bf16[2,6,80,128]{3,2,1,0:T(8,128)(2,1)S(1)} %pad_maximum_fusion.9), channel_id=1, source_target_pairs={{0,2},{1,3},{2,0},{3,1},{4,6},{5,7},{6,4},{7,5},{8,10},{9,11},{10,... | collective-permute-start | bytes 737288 | tf_op jit(solution)/shard_map/ppermute | solution.py:520
  51.4 11.8 %collective-permute-start.17 = (bf16[2,6,80,128]{3,2,1,0:T(8,128)(2,1)S(1)}, bf16[2,6,80,128]{3,2,1,0:T(8,128)(2,1)S(1)}, u32[]{:S(2)}, u32[]{:S(2)}) collective-permute-start(bf16[2,6,80,128]{3,2,1,0:T(8,128)(2,1)S(1)} %pad_maximum_fusion.10), channel_id=1, source_target_pairs={{0,2},{1,3},{2,0},{3,1},{4,6},{5,7},{6,4},{7,5},{8,10},{9,11},{10,... | collective-permute-start | bytes 737288 | tf_op jit(solution)/shard_map/ppermute | solution.py:520
  67.8 18.1 %collective-permute-start.24 = (bf16[12,80,384]{2,1,0:T(8,128)(2,1)S(1)}, bf16[12,80,384]{2,1,0:T(8,128)(2,1)S(1)}, u32[]{:S(2)}, u32[]{:S(2)}) collective-permute-start(bf16[12,80,384]{2,1,0:T(8,128)(2,1)S(1)} %spread_blocks.7), channel_id=1, source_target_pairs={{0,4},{4,0},{8,12},{12,8},{16,20},{20,16},{24,28},{28,24},{1,5},{5... | collective-permute-start | bytes 2211848 | tf_op jit(solution)/shard_map/ppermute | solution.py:520
  72.8 23.7 %collective-permute-start.27 = (bf16[1376,384]{1,0:T(8,128)(2,1)S(1)}, bf16[1376,384]{1,0:T(8,128)(2,1)S(1)}, u32[]{:S(2)}, u32[]{:S(2)}) collective-permute-start(bf16[1376,384]{1,0:T(8,128)(2,1)S(1)} %render_blocks.7), channel_id=1, source_target_pairs={{0,8},{4,12},{24,16},{28,20},{1,9},{5,13},{25,17},{29,21},{2,10},{... | collective-permute-start | bytes 3170312 | tf_op jit(solution)/shard_map/ppermute | solution.py:520
  74.2 8.3 %collective-permute-start.10 = (bf16[192,768]{1,0:T(8,128)(2,1)S(1)}, bf16[192,768]{1,0:T(8,128)(2,1)S(1)}, u32[]{:S(2)}, u32[]{:S(2)}) collective-permute-start(bf16[192,768]{1,0:T(8,128)(2,1)S(1)} %copy-done.30), channel_id=1, source_target_pairs={{0,2},{1,3},{2,0},{3,1},{4,6},{5,7},{6,4},{7,5},{8,10},{9,11},{10,... | collective-permute-start | bytes 884744 | tf_op jit(solution)/shard_map/ppermute | solution.py:520
  82.6 21.4 %collective-permute-start.11 = (bf16[384,768]{1,0:T(8,128)(2,1)S(1)}, bf16[384,768]{1,0:T(8,128)(2,1)S(1)}, u32[]{:S(2)}, u32[]{:S(2)}) collective-permute-start(bf16[384,768]{1,0:T(8,128)(2,1)S(1)} %pad_maximum_fusion.3), channel_id=1, source_target_pairs={{0,1},{1,0},{2,3},{3,2},{4,5},{5,4},{6,7},{7,6},{8,9},{9,8},{10,11... | collective-permute-start | bytes 1769480 | tf_op jit(solution)/shard_map/ppermute | solution.py:520
  85.9 18.1 %collective-permute-start.25 = (bf16[12,80,384]{2,1,0:T(8,128)(2,1)S(1)}, bf16[12,80,384]{2,1,0:T(8,128)(2,1)S(1)}, u32[]{:S(2)}, u32[]{:S(2)}) collective-permute-start(bf16[12,80,384]{2,1,0:T(8,128)(2,1)S(1)} %spread_blocks.6), channel_id=1, source_target_pairs={{0,4},{4,0},{8,12},{12,8},{16,20},{20,16},{24,28},{28,24},{1,5},{5... | collective-permute-start | bytes 2211848 | tf_op jit(solution)/shard_map/ppermute | solution.py:520
  96.8 25.9 %collective-permute-start.30 = (bf16[1376,384]{1,0:T(8,128)(2,1)S(1)}, bf16[1376,384]{1,0:T(8,128)(2,1)S(1)}, u32[]{:S(2)}, u32[]{:S(2)}) collective-permute-start(bf16[1376,384]{1,0:T(8,128)(2,1)S(1)} %add_convert_fusion), channel_id=1, source_target_pairs={{0,8},{4,12},{24,16},{28,20},{1,9},{5,13},{25,17},{29,21},{2,10},{... | collective-permute-start | bytes 3170312 | tf_op jit(solution)/shard_map/ppermute | solution.py:520
  101.3 22.5 %collective-permute-start.28 = (bf16[1376,384]{1,0:T(8,128)(2,1)S(1)}, bf16[1376,384]{1,0:T(8,128)(2,1)S(1)}, u32[]{:S(2)}, u32[]{:S(2)}) collective-permute-start(bf16[1376,384]{1,0:T(8,128)(2,1)S(1)} %add_convert_fusion), channel_id=1, source_target_pairs={{8,16},{12,20},{16,8},{20,12},{9,17},{13,21},{17,9},{21,13},{10,18... | collective-permute-start | bytes 3170312 | tf_op jit(solution)/shard_map/ppermute | solution.py:520
  104.1 26.5 %collective-permute-start.26 = (bf16[12,80,384]{2,1,0:T(8,128)(2,1)S(1)}, bf16[12,80,384]{2,1,0:T(8,128)(2,1)S(1)}, u32[]{:S(2)}, u32[]{:S(2)}) collective-permute-start(bf16[12,80,384]{2,1,0:T(8,128)(2,1)S(1)} %spread_blocks.5), channel_id=1, source_target_pairs={{0,4},{4,0},{8,12},{12,8},{16,20},{20,16},{24,28},{28,24},{1,5},{5... | collective-permute-start | bytes 2211848 | tf_op jit(solution)/shard_map/ppermute | solution.py:520
  123.0 12.3 %collective-permute-start.31 = (bf16[688,384]{1,0:T(8,128)(2,1)S(1)}, bf16[688,384]{1,0:T(8,128)(2,1)S(1)}, u32[]{:S(2)}, u32[]{:S(2)}) collective-permute-start(bf16[688,384]{1,0:T(8,128)(2,1)S(1)} %get-tuple-element.129), channel_id=1, source_target_pairs={{8,16},{12,20},{16,8},{20,12},{9,17},{13,21},{17,9},{21,13},{10,18... | collective-permute-start | bytes 1585160 | tf_op jit(solution)/shard_map/ppermute | solution.py:520
  124.2 13.8 %collective-permute-start.29 = (bf16[688,384]{1,0:T(8,128)(2,1)S(1)}, bf16[688,384]{1,0:T(8,128)(2,1)S(1)}, u32[]{:S(2)}, u32[]{:S(2)}) collective-permute-start(bf16[688,384]{1,0:T(8,128)(2,1)S(1)} %get-tuple-element.131), channel_id=1, source_target_pairs={{0,8},{4,12},{8,0},{12,4},{16,24},{20,28},{24,16},{28,20},{1,9},{5... | collective-permute-start | bytes 1585160 | tf_op jit(solution)/shard_map/ppermute | solution.py:520
  129.0 12.6 %collective-permute-start.12 = (bf16[2,176,384]{2,1,0:T(8,128)(2,1)S(1)}, bf16[2,176,384]{2,1,0:T(8,128)(2,1)S(1)}, u32[]{:S(2)}, u32[]{:S(2)}) collective-permute-start(bf16[2,176,384]{2,1,0:T(8,128)(2,1)S(1)} %get-tuple-element.70), channel_id=1, source_target_pairs={{0,1},{1,0},{2,3},{3,2},{4,5},{5,4},{6,7},{7,6},{8,9},{9,8},{10,11... | collective-permute-start | bytes 811016 | tf_op jit(solution)/shard_map/ppermute | solution.py:520
  129.1 14.3 %collective-permute-start.13 = (bf16[2,176,384]{2,1,0:T(8,128)(2,1)S(1)}, bf16[2,176,384]{2,1,0:T(8,128)(2,1)S(1)}, u32[]{:S(2)}, u32[]{:S(2)}) collective-permute-start(bf16[2,176,384]{2,1,0:T(8,128)(2,1)S(1)} %get-tuple-element.71), channel_id=1, source_target_pairs={{0,2},{1,3},{2,0},{3,1},{4,6},{5,7},{6,4},{7,5},{8,10},{9,11},{10,... | collective-permute-start | bytes 811016 | tf_op jit(solution)/shard_map/ppermute | solution.py:520
  130.6 12.8 %collective-permute-start.14 = (bf16[2,176,384]{2,1,0:T(8,128)(2,1)S(1)}, bf16[2,176,384]{2,1,0:T(8,128)(2,1)S(1)}, u32[]{:S(2)}, u32[]{:S(2)}) collective-permute-start(bf16[2,176,384]{2,1,0:T(8,128)(2,1)S(1)} %get-tuple-element.72), channel_id=1, source_target_pairs={{0,3},{1,2},{2,1},{3,0},{4,7},{5,6},{6,5},{7,4},{8,11},{9,10},{10,... | collective-permute-start | bytes 811016 | tf_op jit(solution)/shard_map/ppermute | solution.py:520
  135.3 19.0 %collective-permute-start.40 = (bf16[688,384]{1,0:T(8,128)(2,1)S(1)}, bf16[688,384]{1,0:T(8,128)(2,1)S(1)}, u32[]{:S(2)}, u32[]{:S(2)}) collective-permute-start(bf16[688,384]{1,0:T(8,128)(2,1)S(1)} %get-tuple-element.128), channel_id=1, source_target_pairs={{8,16},{12,20},{16,8},{20,12},{9,17},{13,21},{17,9},{21,13},{10,18... | collective-permute-start | bytes 1585160 | tf_op jit(solution)/shard_map/ppermute | solution.py:520
  137.9 16.4 %collective-permute-start.39 = (bf16[688,384]{1,0:T(8,128)(2,1)S(1)}, bf16[688,384]{1,0:T(8,128)(2,1)S(1)}, u32[]{:S(2)}, u32[]{:S(2)}) collective-permute-start(bf16[688,384]{1,0:T(8,128)(2,1)S(1)} %get-tuple-element.130), channel_id=1, source_target_pairs={{0,8},{4,12},{8,0},{12,4},{16,24},{20,28},{24,16},{28,20},{1,9},{5... | collective-permute-start | bytes 1585160 | tf_op jit(solution)/shard_map/ppermute | solution.py:520
  154.6 10.2 %collective-permute-start.41 = (bf16[176,384]{1,0:T(8,128)(2,1)S(1)}, bf16[176,384]{1,0:T(8,128)(2,1)S(1)}, u32[]{:S(2)}, u32[]{:S(2)}) collective-permute-start(bf16[176,384]{1,0:T(8,128)(2,1)S(1)} %get-tuple-element.92), channel_id=1, source_target_pairs={{0,2},{1,3},{2,0},{3,1},{4,6},{5,7},{6,4},{7,5},{8,10},{9,11},{10,... | collective-permute-start | bytes 405512 | tf_op jit(solution)/shard_map/ppermute | solution.py:520
  156.0 8.7 %collective-permute-start.42 = (bf16[176,384]{1,0:T(8,128)(2,1)S(1)}, bf16[176,384]{1,0:T(8,128)(2,1)S(1)}, u32[]{:S(2)}, u32[]{:S(2)}) collective-permute-start(bf16[176,384]{1,0:T(8,128)(2,1)S(1)} %get-tuple-element.93), channel_id=1, source_target_pairs={{0,1},{1,0},{2,3},{3,2},{4,5},{5,4},{6,7},{7,6},{8,9},{9,8},{10,11... | collective-permute-start | bytes 405512 | tf_op jit(solution)/shard_map/ppermute | solution.py:520
  156.5 9.6 %collective-permute-start.43 = (bf16[176,384]{1,0:T(8,128)(2,1)S(1)}, bf16[176,384]{1,0:T(8,128)(2,1)S(1)}, u32[]{:S(2)}, u32[]{:S(2)}) collective-permute-start(bf16[176,384]{1,0:T(8,128)(2,1)S(1)} %get-tuple-element.94), channel_id=1, source_target_pairs={{0,3},{1,2},{2,1},{3,0},{4,7},{5,6},{6,5},{7,4},{8,11},{9,10},{10,... | collective-permute-start | bytes 405512 | tf_op jit(solution)/shard_map/ppermute | solution.py:520
  161.2 16.3 %collective-permute-start.47 = (bf16[688,384]{1,0:T(8,128)(2,1)S(1)}, bf16[688,384]{1,0:T(8,128)(2,1)S(1)}, u32[]{:S(2)}, u32[]{:S(2)}) collective-permute-start(bf16[688,384]{1,0:T(8,128)(2,1)S(1)} %gather_rows.2.rest_0_.refs_10_), channel_id=1, source_target_pairs={{0,8},{4,12},{8,0},{12,4},{16,24},{20,28},{24,16},{28,20},{1,9},{5... | collective-permute-start | bytes 1585160 | tf_op jit(solution)/shard_map/ppermute | solution.py:520
  161.3 16.3 %collective-permute-start.38 = (bf16[688,384]{1,0:T(8,128)(2,1)S(1)}, bf16[688,384]{1,0:T(8,128)(2,1)S(1)}, u32[]{:S(2)}, u32[]{:S(2)}) collective-permute-start(bf16[688,384]{1,0:T(8,128)(2,1)S(1)} %gather_rows.2.rest_0_.refs_10_), channel_id=1, source_target_pairs={{8,16},{12,20},{16,8},{20,12},{9,17},{13,21},{17,9},{21,13},{10,18... | collective-permute-start | bytes 1585160 | tf_op jit(solution)/shard_map/ppermute | solution.py:520
  177.8 20.3 %collective-permute-start.57 = (f32[2,192,768]{2,1,0:T(8,128)S(1)}, f32[2,192,768]{2,1,0:T(8,128)S(1)}, u32[]{:S(2)}, u32[]{:S(2)}) collective-permute-start(f32[2,192,768]{2,1,0:T(8,128)S(1)} %bitcast.115), channel_id=1, source_target_pairs={{0,1},{1,0},{2,3},{3,2},{4,5},{5,4},{6,7},{7,6},{8,9},{9,8},{10,11... | collective-permute-start | bytes 3538952 | tf_op jit(solution)/shard_map/ppermute | solution.py:520
  178.4 14.2 %collective-permute-start.49 = (bf16[688,384]{1,0:T(8,128)(2,1)S(1)}, bf16[688,384]{1,0:T(8,128)(2,1)S(1)}, u32[]{:S(2)}, u32[]{:S(2)}) collective-permute-start(bf16[688,384]{1,0:T(8,128)(2,1)S(1)} %gather_rows.3.rest_1_.refs_11_), channel_id=1, source_target_pairs={{0,8},{4,12},{8,0},{12,4},{16,24},{20,28},{24,16},{28,20},{1,9},{5... | collective-permute-start | bytes 1585160 | tf_op jit(solution)/shard_map/ppermute | solution.py:520
  180.0 16.0 %collective-permute-start.48 = (bf16[688,384]{1,0:T(8,128)(2,1)S(1)}, bf16[688,384]{1,0:T(8,128)(2,1)S(1)}, u32[]{:S(2)}, u32[]{:S(2)}) collective-permute-start(bf16[688,384]{1,0:T(8,128)(2,1)S(1)} %gather_rows.3.rest_1_.refs_11_), channel_id=1, source_target_pairs={{8,16},{12,20},{16,8},{20,12},{9,17},{13,21},{17,9},{21,13},{10,18... | collective-permute-start | bytes 1585160 | tf_op jit(solution)/shard_map/ppermute | solution.py:520
  183.9 22.4 %collective-permute-start.53 = (bf16[12,80,384]{2,1,0:T(8,128)(2,1)}, bf16[12,80,384]{2,1,0:T(8,128)(2,1)}, u32[]{:S(2)}, u32[]{:S(2)}) collective-permute-start(bf16[12,80,384]{2,1,0:T(8,128)(2,1)} %pick_bands.6), channel_id=1, source_target_pairs={{0,4},{4,0},{8,12},{12,8},{16,20},{20,16},{24,28},{28,24},{1,5},{5... | collective-permute-start | bytes 2211848 | tf_op jit(solution)/shard_map/ppermute | solution.py:520
  193.5 22.0 %collective-permute-start.50 = (bf16[1376,384]{1,0:T(8,128)(2,1)}, bf16[1376,384]{1,0:T(8,128)(2,1)}, u32[]{:S(2)}, u32[]{:S(2)}) collective-permute-start(bf16[1376,384]{1,0:T(8,128)(2,1)} %constant_dynamic-update-slice_fusion.11), channel_id=1, source_target_pairs={{8,16},{12,20},{16,8},{20,12},{9,17},{13,21},{17,9},{21,13},{10,18... | collective-permute-start | bytes 3170312 | tf_op jit(solution)/shard_map/ppermute | solution.py:520
  196.8 29.6 %collective-permute-start.52 = (bf16[1376,384]{1,0:T(8,128)(2,1)}, bf16[1376,384]{1,0:T(8,128)(2,1)}, u32[]{:S(2)}, u32[]{:S(2)}) collective-permute-start(bf16[1376,384]{1,0:T(8,128)(2,1)} %constant_dynamic-update-slice_fusion.9), channel_id=1, source_target_pairs={{8,0},{12,4},{16,24},{20,28},{9,1},{13,5},{17,25},{21,29},{10,2},{... | collective-permute-start | bytes 3170312 | tf_op jit(solution)/shard_map/ppermute | solution.py:520
  200.1 16.6 %collective-permute-start.58 = (f32[192,768]{1,0:T(8,128)}, f32[192,768]{1,0:T(8,128)}, u32[]{:S(2)}, u32[]{:S(2)}) collective-permute-start(f32[192,768]{1,0:T(8,128)} %slice_bitcast_fusion), channel_id=1, source_target_pairs={{0,2},{1,3},{2,0},{3,1},{4,6},{5,7},{6,4},{7,5},{8,10},{9,11},{10,... | collective-permute-start | bytes 1769480 | tf_op jit(solution)/shard_map/ppermute | solution.py:520
  206.2 23.8 %collective-permute-start.54 = (bf16[12,80,384]{2,1,0:T(8,128)(2,1)S(1)}, bf16[12,80,384]{2,1,0:T(8,128)(2,1)S(1)}, u32[]{:S(2)}, u32[]{:S(2)}) collective-permute-start(bf16[12,80,384]{2,1,0:T(8,128)(2,1)S(1)} %pick_bands.5), channel_id=1, source_target_pairs={{0,4},{4,0},{8,12},{12,8},{16,20},{20,16},{24,28},{28,24},{1,5},{5... | collective-permute-start | bytes 2211848 | tf_op jit(solution)/shard_map/ppermute | solution.py:520
  215.5 33.5 %collective-permute-start.51 = (bf16[1376,384]{1,0:T(8,128)(2,1)}, bf16[1376,384]{1,0:T(8,128)(2,1)S(1)}, u32[]{:S(2)}, u32[]{:S(2)}) collective-permute-start(bf16[1376,384]{1,0:T(8,128)(2,1)} %collective-permute-done.50), channel_id=1, source_target_pairs={{8,0},{12,4},{16,24},{20,28},{9,1},{13,5},{17,25},{21,29},{10,2},{... | collective-permute-start | bytes 3170312 | tf_op jit(solution)/shard_map/ppermute | solution.py:520
  218.0 17.8 %collective-permute-start.59 = (bf16[96,768]{1,0:T(8,128)(2,1)S(1)}, bf16[96,768]{1,0:T(8,128)(2,1)S(1)}, u32[]{:S(2)}, u32[]{:S(2)}) collective-permute-start(bf16[96,768]{1,0:T(8,128)(2,1)S(1)} %dynamic-slice_convert_fusion), channel_id=1, source_target_pairs={{0,4},{4,0},{8,12},{12,8},{16,20},{20,16},{24,28},{28,24},{1,5},{5... | collective-permute-start | bytes 442376 | tf_op jit(solution)/shard_map/ppermute | solution.py:520
  230.0 21.3 %collective-permute-start.55 = (bf16[12,80,384]{2,1,0:T(8,128)(2,1)S(1)}, bf16[12,80,384]{2,1,0:T(8,128)(2,1)S(1)}, u32[]{:S(2)}, u32[]{:S(2)}) collective-permute-start(bf16[12,80,384]{2,1,0:T(8,128)(2,1)S(1)} %pick_bands.4), channel_id=1, source_target_pairs={{0,4},{4,0},{8,12},{12,8},{16,20},{20,16},{24,28},{28,24},{1,5},{5... | collective-permute-start | bytes 2211848 | tf_op jit(solution)/shard_map/ppermute | solution.py:520
  235.8 16.5 %collective-permute-start.60 = (bf16[96,768]{1,0:T(8,128)(2,1)S(1)}, bf16[96,768]{1,0:T(8,128)(2,1)S(1)}, u32[]{:S(2)}, u32[]{:S(2)}) collective-permute-start(bf16[96,768]{1,0:T(8,128)(2,1)S(1)} %fusion.4), channel_id=1, source_target_pairs={{0,8},{4,12},{8,0},{12,4},{16,24},{20,28},{24,16},{28,20},{1,9},{5... | collective-permute-start | bytes 442376 | tf_op jit(solution)/shard_map/ppermute | solution.py:520
  251.3 16.7 %collective-permute-start.56 = (bf16[12,80,384]{2,1,0:T(8,128)(2,1)S(1)}, bf16[12,80,384]{2,1,0:T(8,128)(2,1)S(1)}, u32[]{:S(2)}, u32[]{:S(2)}) collective-permute-start(bf16[12,80,384]{2,1,0:T(8,128)(2,1)S(1)} %pick_bands.7), channel_id=1, source_target_pairs={{0,4},{4,0},{8,12},{12,8},{16,20},{20,16},{24,28},{28,24},{1,5},{5... | collective-permute-start | bytes 2211848 | tf_op jit(solution)/shard_map/ppermute | solution.py:520
  252.4 8.0 %collective-permute-start.61 = (bf16[96,768]{1,0:T(8,128)(2,1)S(1)}, bf16[96,768]{1,0:T(8,128)(2,1)S(1)}, u32[]{:S(2)}, u32[]{:S(2)}) collective-permute-start(bf16[96,768]{1,0:T(8,128)(2,1)S(1)} %fusion.1), channel_id=1, source_target_pairs={{0,16},{4,20},{8,24},{12,28},{16,0},{20,4},{24,8},{28,12},{1,17},{... | collective-permute-start | bytes 442376 | tf_op jit(solution)/shard_map/ppermute | solution.py:520
  268.0 8.2 %collective-permute-start.62 = (bf16[96,768]{1,0:T(8,128)(2,1)S(1)}, bf16[96,768]{1,0:T(8,128)(2,1)S(1)}, u32[]{:S(2)}, u32[]{:S(2)}) collective-permute-start(bf16[96,768]{1,0:T(8,128)(2,1)S(1)} %get-tuple-element.121), channel_id=1, source_target_pairs={{0,4},{4,0},{8,12},{12,8},{16,20},{20,16},{24,28},{28,24},{1,5},{5... | collective-permute-start | bytes 442376 | tf_op jit(solution)/shard_map/ppermute | solution.py:520
  (47 other events, 764.9 us)
